TPU v7x, 128 devices: a whole 4x4x4 slice. The times are simulated.
128 devices in a mesh: gx: 16 (over z_hi, y, core), gy: 8 (over x, z_lo).
Axes of the slice: x: 4, y: 4, z: 4 (z_hi: 2, z_lo: 2; z = z_hi * 2 + z_lo), core: 2. Of those that a mesh axis runs over, the one named last changes fastest.
Arguments:
- electric_forward: float32 [3, 256, 256, 128], P(None, 'gx', 'gy'), may hold values from -6 to 6
- magnetic_forward: float32 [3, 256, 256, 128], P(None, 'gx', 'gy'), may hold values from -6 to 6
- electric_adjoint: float32 [3, 256, 256, 128], P(None, 'gx', 'gy'), may hold values from -6 to 6
- magnetic_adjoint: float32 [3, 256, 256, 128], P(None, 'gx', 'gy'), may hold values from -6 to 6
- permittivity: float32 [256, 256, 128], P('gx', 'gy'), may hold values from 1 to 4
- pattern: float32 [16384, 256], P(('gx', 'gy')), may hold values from -6 to 6
- owners: int32 [16384, 1], P(('gx', 'gy')), may hold values from 0 to 127; in each aligned block of 128 rows (0 to 127, 128 to 255, ...) at most 2 rows name the same one
- tile_count: int32 [16384], P(('gx', 'gy')), may hold values from 1 to 256, as said below
- tile_start: int32 [16384], P(('gx', 'gy')), may hold values from 0 to 16128, as said below
Outputs:
- electric_final: float32 [3, 256, 256, 128], P(None, 'gx', 'gy')
- pattern_grad: float32 [16384, 256], P(('gx', 'gy'))
Inputs may be any that keep to these rules, and one draw needn't show every extreme that they name: `owners`: among the 128 tiles of one device no owner is named more than 2 times. `tile_count`: some tile has 256 live cells and some has one. `tile_start`: every tile's cells stay inside its owner's design slab.
All inputs are finite; a program needn't handle non-finite values.
Results may differ from a plain program's by a relative error of at most 0.00014.
Values sent between devices are 32-bit elements; how exact they have to be, the bound alone decides.
No kernel may reach another device: no remote copies, remote signals or barrier semaphores. Data moves between devices by JAX's collectives and lax.ppermute only.
A program may use at most 64 MiB of HBM per device.

v0:
```python
import math

import jax
import jax.numpy as jnp
from jax import lax
from jax.sharding import PartitionSpec as P

DLAYERS = 32
STEPS = 2


courant = 0.5
angular = 0.9
contrast = 8.0
exact = lax.Precision.HIGHEST


def passed_along(block, axis, distance):
    devices = range(lax.axis_size(axis))
    route = [(i - distance, i) for i in devices if i - distance in devices]
    return lax.ppermute(block, axis, route)


def face_x(plane, offset):
    return passed_along(plane, "gx", offset)


def face_y(plane, offset):
    return passed_along(plane, "gy", offset)


def raise_edge(values, axis, edge):
    rest = lax.slice_in_dim(values, 1, values.shape[axis], axis=axis)
    return jnp.concatenate([rest, jnp.expand_dims(edge, axis)], axis=axis)


def lower_edge(values, axis, edge):
    rest = lax.slice_in_dim(values, 0, values.shape[axis] - 1, axis=axis)
    return jnp.concatenate([jnp.expand_dims(edge, axis), rest], axis=axis)


def advance(electric, magnetic, inverse):
    along_x = electric[:, 0]
    along_y = electric[:, 1]
    along_z = electric[:, 2]
    after_x = face_x(electric[:, 1:3, 0], -1)
    after_y = face_y(jnp.stack([along_x[:, :, 0], along_z[:, :, 0]], axis=1), -1)
    flat_edge = jnp.zeros_like(along_x[..., 0])
    curl_e = jnp.stack(
        [
            raise_edge(along_z, 2, after_y[:, 1])
            - along_z
            - (raise_edge(along_y, 3, flat_edge) - along_y),
            raise_edge(along_x, 3, flat_edge)
            - along_x
            - (raise_edge(along_z, 1, after_x[:, 1]) - along_z),
            raise_edge(along_y, 1, after_x[:, 0])
            - along_y
            - (raise_edge(along_x, 2, after_y[:, 0]) - along_x),
        ],
        axis=1,
    )
    magnetic = magnetic - courant * curl_e
    mag_x = magnetic[:, 0]
    mag_y = magnetic[:, 1]
    mag_z = magnetic[:, 2]
    before_x = face_x(magnetic[:, 1:3, -1], 1)
    before_y = face_y(jnp.stack([mag_x[:, :, -1], mag_z[:, :, -1]], axis=1), 1)
    curl_h = jnp.stack(
        [
            mag_z
            - lower_edge(mag_z, 2, before_y[:, 1])
            - (mag_y - lower_edge(mag_y, 3, flat_edge)),
            mag_x
            - lower_edge(mag_x, 3, flat_edge)
            - (mag_z - lower_edge(mag_z, 1, before_x[:, 1])),
            mag_y
            - lower_edge(mag_y, 1, before_x[:, 0])
            - (mag_x - lower_edge(mag_x, 2, before_y[:, 0])),
        ],
        axis=1,
    )
    electric = electric + courant * inverse * curl_h
    return (electric, magnetic)


def evolve(electric, magnetic, inverse, lower):
    cosine = jnp.zeros(electric.shape[:4] + (DLAYERS,), jnp.float32)
    sine = jnp.zeros(electric.shape[:4] + (DLAYERS,), jnp.float32)
    for moment in range(1, STEPS + 1):
        electric, magnetic = advance(electric, magnetic, inverse)
        window = electric[..., lower : lower + DLAYERS]
        cosine = cosine + math.cos(angular * moment) * window
        sine = sine + math.sin(angular * moment) * window
    return (electric, cosine, sine)


def slide_rows(rows, amount, heading):
    span = rows.shape[1] // 2
    for bit in range(max(span - 1, 1).bit_length()):
        stride = 1 << bit
        moved = jnp.roll(rows, heading * stride, axis=1)
        rows = jnp.where((amount >> bit & 1 == 1)[:, None], moved, rows)
    return rows


def shards(
    electric_forward,
    magnetic_forward,
    electric_adjoint,
    magnetic_adjoint,
    permittivity,
    pattern,
    owners,
    tile_count,
    tile_start,
):
    grid_x = lax.axis_size("gx")
    grid_y = lax.axis_size("gy")
    devices_total = grid_x * grid_y
    tiles_here, tile_cells = pattern.shape
    capacity = max(2, 2 * tiles_here // devices_total)
    size_x, size_y, size_z = permittivity.shape
    offsets = jnp.arange(tile_cells, dtype=jnp.int32)
    within = offsets[None, :] < tile_count[:, None]
    placed = jnp.where(within, pattern, jnp.float32(0.0))
    target = owners[:, 0]
    hits = (target[:, None] == jnp.arange(devices_total, dtype=jnp.int32)[None, :]).astype(
        jnp.int32
    )
    earlier = jnp.cumsum(hits, axis=0) - hits
    slot_rank = jnp.sum(earlier * hits, axis=1)
    slot_index = target * capacity + slot_rank
    slot_ids = jnp.arange(devices_total * capacity, dtype=jnp.int32)
    chosen = slot_ids[:, None] == slot_index[None, :]
    chosen_real = chosen.astype(jnp.float32)
    outgoing = jnp.dot(chosen_real, placed, precision=exact, preferred_element_type=jnp.float32)
    starts_out = jnp.sum(jnp.where(chosen, tile_start[None, :], 0), axis=1)
    arrived, starts_in = (
        lax.all_to_all(outgoing, ("gx", "gy"), split_axis=0, concat_axis=0, tiled=True),
        lax.all_to_all(starts_out, ("gx", "gy"), split_axis=0, concat_axis=0, tiled=True),
    )
    slab_cells = size_x * size_y * DLAYERS
    blocks = slab_cells // tile_cells
    block_of = starts_in // tile_cells
    remainder = starts_in % tile_cells
    block_ids = jnp.arange(blocks, dtype=jnp.int32)
    lower_hot = (block_of[:, None] == block_ids[None, :]).astype(jnp.float32)
    upper_hot = (block_of[:, None] + 1 == block_ids[None, :]).astype(jnp.float32)
    widened = jnp.concatenate([arrived, jnp.zeros_like(arrived)], axis=1)
    widened = slide_rows(widened, remainder, 1)
    density = jnp.dot(
        lower_hot.T, widened[:, :tile_cells], precision=exact, preferred_element_type=jnp.float32
    ) + jnp.dot(
        upper_hot.T, widened[:, tile_cells:], precision=exact, preferred_element_type=jnp.float32
    )
    sigma = jax.nn.sigmoid(density.reshape(size_x, size_y, DLAYERS))
    lower = (size_z - DLAYERS) // 2
    eps_total = permittivity.at[:, :, lower : lower + DLAYERS].add(contrast * sigma)
    inverse = 1.0 / eps_total
    electric, cosine, sine = evolve(electric_forward[None], magnetic_forward[None], inverse, lower)
    electric_final = electric[0]
    cos_fwd, sin_fwd = (cosine[0], sine[0])
    unused, cosine, sine = evolve(electric_adjoint[None], magnetic_adjoint[None], inverse, lower)
    cos_adj, sin_adj = (cosine[0], sine[0])
    gradient = (
        contrast * sigma * (1.0 - sigma) * jnp.sum(cos_fwd * cos_adj + sin_fwd * sin_adj, axis=0)
    )
    grad_blocks = gradient.reshape(blocks, tile_cells)
    gathered = jnp.concatenate(
        [
            jnp.dot(lower_hot, grad_blocks, precision=exact, preferred_element_type=jnp.float32),
            jnp.dot(upper_hot, grad_blocks, precision=exact, preferred_element_type=jnp.float32),
        ],
        axis=1,
    )
    picked = slide_rows(gathered, remainder, -1)[:, :tile_cells]
    returned = lax.all_to_all(picked, ("gx", "gy"), split_axis=0, concat_axis=0, tiled=True)
    own_rows = jnp.dot(chosen_real.T, returned, precision=exact, preferred_element_type=jnp.float32)
    pattern_grad = jnp.where(within, own_rows, jnp.float32(0.0))
    return (electric_final, pattern_grad)


def solution(mesh):
    placed = (
        P(None, "gx", "gy", None),
        P(None, "gx", "gy", None),
        P(None, "gx", "gy", None),
        P(None, "gx", "gy", None),
        P("gx", "gy", None),
        P(("gx", "gy"), None),
        P(("gx", "gy"), None),
        P(("gx", "gy")),
        P(("gx", "gy")),
    )
    return jax.shard_map(
        shards,
        mesh=mesh,
        in_specs=placed,
        out_specs=(P(None, "gx", "gy", None), P(("gx", "gy"), None)),
        check_vma=False,
    )
```

profile of v0, /device:TPU:1, one launch (start us, length us, event | category | flops | bytes accessed | tf_op | source)
XLA Modules:
  0.0 152.7 jit_solution(17131358494558839831)
XLA Ops:
  0.6 1.7 %copy.445 = f32[16,32,128]{2,1,0:T(8,128)} copy(f32[16,32,128]{2,1,0:T(8,128)} %param.15) | data formatting | bytes 524288
  2.3 1.8 %copy.433 = f32[3,16,32,128]{3,0,2,1:T(4,128)S(1)} copy(f32[3,16,32,128]{3,2,1,0:T(8,128)} %param.13) | data formatting | bytes 1572864 | tf_op args[2]
  4.1 0.6 slice_bitcast_fusion.30
  4.7 3.5 %collective-permute-start.9 = (f32[1,2,32,128]{3,1,2,0:T(2,128)}, f32[1,2,32,128]{3,1,2,0:T(2,128)}, u32[]{:S(2)}, u32[]{:S(2)}) collective-permute-start(f32[1,2,32,128]{3,1,2,0:T(2,128)} %slice_bitcast_fusion.30), channel_id=1, source_target_pairs={{8,0},{16,8},{24,16},{32,24},{40,32},{48,40},{56,48},{64,56},{72,6... | collective-permute-start | bytes 98312 | tf_op jit(solution)/shard_map/ppermute | solution.py:21
  8.6 0.6 copy-done.27
  9.4 0.8 all_to_all.24
  10.1 10.6 %all-to-all-start = ((s32[128,2,1]{1,2,0:T(1,128)}), s32[128,2,1]{1,2,0:T(1,128)S(1)}, u32[]{:S(2)}, u32[]{:S(2)}) async-start(s32[128,2,1]{1,2,0:T(1,128)} %bitcast.1), calls=%async_computation | async-start | bytes 131072 | tf_op jit(solution)/shard_map/all_to_all | solution.py:141
  20.8 0.5 copy.434
  21.3 0.6 slice_bitcast_fusion.33
  22.0 3.0 %collective-permute-start.1 = (f32[1,2,32,128]{3,1,2,0:T(2,128)}, f32[1,2,32,128]{3,1,2,0:T(2,128)}, u32[]{:S(2)}, u32[]{:S(2)}) collective-permute-start(f32[1,2,32,128]{3,1,2,0:T(2,128)} %slice_bitcast_fusion.33), channel_id=1, source_target_pairs={{8,0},{16,8},{24,16},{32,24},{40,32},{48,40},{56,48},{64,56},{72,6... | collective-permute-start | bytes 98312 | tf_op jit(solution)/shard_map/ppermute | solution.py:21
  24.9 1.1 fusion.54
  26.3 0.7 slice.817
  27.0 0.8 slice.812
  28.1 0.7 slice.751
  28.8 0.9 slice.746
  29.7 1.8 %all_to_all.27 = f32[128,2,256]{2,1,0:T(2,128)} reshape(f32[256,256]{1,0:T(8,128)} %fusion.54) | data formatting | bytes 524288 | tf_op jit(solution)/shard_map/all_to_all | solution.py:140
  31.5 9.6 %all-to-all-start.1 = ((f32[128,2,256]{2,1,0:T(2,128)}), f32[128,2,256]{2,1,0:T(2,128)}, u32[]{:S(2)}, u32[]{:S(2)}) async-start(f32[128,2,256]{2,1,0:T(2,128)} %all_to_all.27), calls=%async_computation.1 | async-start | bytes 524288 | tf_op jit(solution)/shard_map/all_to_all | solution.py:140
  41.1 0.5 broadcast.482
  41.6 0.8 reduce.6
  42.6 0.9 fusion.85
  43.5 1.8 %fusion.78 = (f32[1,1,16,32,128]{4,1,3,2,0:T(1,128)S(1)}, f32[1,1,16,32,128]{4,1,3,2,0:T(1,128)S(1)}, f32[1,1,16,32,128]{4,1,3,2,0:T(1,128)S(1)}) fusion(f32[1,3,16,32,128]{4,1,3,2,0:T(4,128)S(1)} %bitcast.314, f32[1,1,1,32,128]{4,1,3,2,0:T(1,128)S(1)} %get-tuple-element.65, f32[1,1,15,32,128]{4,1,3,2,0:T(1,128)} %bitcast.357), kind=kLoop, calls=%fused_computation.243 | loop fusion | flops 131072 | bytes 1835008 | tf_op jit(solution)/shard_map/slice | solution.py:45
  45.9 0.9 fusion.89
  46.8 0.7 fusion.79
  48.1 1.3 collective-permute-start.8
  49.9 1.3 collective-permute-start
  51.8 0.8 collective-permute-done.8
  53.0 0.6 copy-done.5
  53.6 0.6 copy-done.2
  54.3 0.5 copy-done.15
  55.2 0.9 copy-done.21
  56.3 1.0 copy-done.3
  57.5 0.6 copy-done.13
  58.2 4.5 %collective-permute-start.11 = (f32[1,2,32,128]{3,2,1,0:T(8,128)S(1)}, f32[1,2,32,128]{3,2,1,0:T(8,128)S(1)}, u32[]{:S(2)}, u32[]{:S(2)}) collective-permute-start(f32[1,2,32,128]{3,2,1,0:T(8,128)S(1)} %slice_bitcast_fusion.29), channel_id=1, source_target_pairs={{0,8},{8,16},{16,24},{24,32},{32,40},{40,48},{48,56},{56,64},{64,7... | collective-permute-start | bytes 98312 | tf_op jit(solution)/shard_map/ppermute | solution.py:21
  62.7 4.2 %collective-permute-start.10 = (f32[1,2,16,128]{3,2,1,0:T(8,128)S(1)}, f32[1,2,16,128]{3,2,1,0:T(8,128)S(1)}, u32[]{:S(2)}, u32[]{:S(2)}) collective-permute-start(f32[1,2,16,128]{3,2,1,0:T(8,128)S(1)} %pad_maximum_fusion.7), channel_id=1, source_target_pairs={{0,1},{1,2},{2,3},{3,4},{4,5},{5,6},{6,7},{8,9},{9,10},{10,11},{11... | collective-permute-start | bytes 49160 | tf_op jit(solution)/shard_map/ppermute | solution.py:21
  67.2 2.2 %collective-permute-start.3 = (f32[1,2,32,128]{3,2,1,0:T(8,128)S(1)}, f32[1,2,32,128]{3,2,1,0:T(8,128)S(1)}, u32[]{:S(2)}, u32[]{:S(2)}) collective-permute-start(f32[1,2,32,128]{3,2,1,0:T(8,128)S(1)} %slice_bitcast_fusion.32), channel_id=1, source_target_pairs={{0,8},{8,16},{16,24},{24,32},{32,40},{40,48},{48,56},{56,64},{64,7... | collective-permute-start | bytes 98312 | tf_op jit(solution)/shard_map/ppermute | solution.py:21
  69.5 4.5 %collective-permute-start.2 = (f32[1,2,16,128]{3,2,1,0:T(8,128)S(1)}, f32[1,2,16,128]{3,2,1,0:T(8,128)S(1)}, u32[]{:S(2)}, u32[]{:S(2)}) collective-permute-start(f32[1,2,16,128]{3,2,1,0:T(8,128)S(1)} %pad_maximum_fusion.3), channel_id=1, source_target_pairs={{0,1},{1,2},{2,3},{3,4},{4,5},{5,6},{6,7},{8,9},{9,10},{10,11},{11... | collective-permute-start | bytes 49160 | tf_op jit(solution)/shard_map/ppermute | solution.py:21
  74.9 1.0 fusion.40
  75.8 0.8 fusion.43
  76.7 0.8 fusion.27
  77.5 1.0 fusion.24
  78.4 1.1 all_to_all.29
  81.4 0.8 reshape.1089
  82.2 1.9 %slice_add_fusion = f32[16,32,32]{2,1,0:T(8,128)} fusion(f32[16,32,32]{2,1,0:T(8,128)} %reshape.1089, f32[16,32,128]{2,1,0:T(8,128)} %copy.445), kind=kLoop, calls=%fused_computation.135 | loop fusion | flops 16384 | bytes 196608 | tf_op jit(solution)/shard_map/add | solution.py:159
  84.1 3.5 %scatter-add.4 = f32[16,32,128]{2,1,0:T(8,128)} dynamic-update-slice(f32[16,32,128]{2,1,0:T(8,128)} %copy.445, f32[16,32,32]{2,1,0:T(8,128)} %slice_add_fusion, s32[]{:T(128)} %constant.78.clone.1, s32[]{:T(128)} %constant.78.clone.1, s32[]{:T(128)} %constant.91.clone.1) | dynamic-update-slice | bytes 131076 | tf_op jit(solution)/shard_map/scatter-add | solution.py:159
  87.7 1.0 divide_multiply_fusion
  88.8 1.6 %fusion.58 = (f32[1,3,16,32,128]{4,3,2,1,0:T(8,128)S(1)}, f32[1,3,16,32,128]{4,3,2,1,0:T(8,128)S(1)}) fusion(f32[3,16,32,128]{3,2,1,0:T(8,128)S(1)} %copy-done, f32[1,16,32,128]{3,2,1,0:T(8,128)S(1)} %copy-done.11, f32[1,16,32,128]{3,2,1,0:T(8,128)} %get-tuple-element.35, f32[1,16,32,128]{3,2,1,0:T(8,128)} %get-tuple-element.34, ...), kind=kLoop, calls=%fused_computation.167 | loop fusion | flops 1572864 | bytes 4980736 | tf_op jit(solution)/shard_map/add | solution.py:83
  91.8 3.0 %collective-permute-start.13 = (f32[1,2,32,128]{3,2,1,0:T(8,128)S(1)}, f32[1,2,32,128]{3,2,1,0:T(8,128)S(1)}, u32[]{:S(2)}, u32[]{:S(2)}) collective-permute-start(f32[1,2,32,128]{3,2,1,0:T(8,128)S(1)} %slice_bitcast_fusion.28), channel_id=1, source_target_pairs={{8,0},{16,8},{24,16},{32,24},{40,32},{48,40},{56,48},{64,56},{72,6... | collective-permute-start | bytes 98312 | tf_op jit(solution)/shard_map/ppermute | solution.py:21
  94.8 1.3 collective-permute-start.12
  96.5 1.3 collective-permute-start.4
  97.8 1.9 %collective-permute-start.5 = (f32[1,2,32,128]{3,1,2,0:T(2,128)S(1)}, f32[1,2,32,128]{3,1,2,0:T(2,128)S(1)}, u32[]{:S(2)}, u32[]{:S(2)}) collective-permute-start(f32[1,2,32,128]{3,1,2,0:T(2,128)S(1)} %bitcast.370), channel_id=1, source_target_pairs={{8,0},{16,8},{24,16},{32,24},{40,32},{48,40},{56,48},{64,56},{72,6... | collective-permute-start | bytes 98312 | tf_op jit(solution)/shard_map/ppermute | solution.py:21
  100.0 2.1 %collective-permute-done.4 = f32[1,2,16,128]{3,2,1,0:T(8,128)S(1)} collective-permute-done((f32[1,2,16,128]{3,2,1,0:T(8,128)S(1)}, f32[1,2,16,128]{3,2,1,0:T(8,128)S(1)}, u32[]{:S(2)}, u32[]{:S(2)}) %collective-permute-start.4) | collective-permute-done | bytes 16416 | tf_op jit(solution)/shard_map/ppermute | solution.py:21
  102.6 0.7 copy-done.6
  103.9 0.5 fusion.28
  105.0 0.8 copy-done.8
  106.3 3.9 %collective-permute-start.15 = (f32[1,2,32,128]{3,2,1,0:T(8,128)S(1)}, f32[1,2,32,128]{3,2,1,0:T(8,128)S(1)}, u32[]{:S(2)}, u32[]{:S(2)}) collective-permute-start(f32[1,2,32,128]{3,2,1,0:T(8,128)S(1)} %slice_bitcast_fusion.27), channel_id=1, source_target_pairs={{0,8},{8,16},{16,24},{24,32},{32,40},{40,48},{48,56},{56,64},{64,7... | collective-permute-start | bytes 98312 | tf_op jit(solution)/shard_map/ppermute | solution.py:21
  110.2 4.5 %collective-permute-start.14 = (f32[1,2,16,128]{3,2,1,0:T(8,128)S(1)}, f32[1,2,16,128]{3,2,1,0:T(8,128)S(1)}, u32[]{:S(2)}, u32[]{:S(2)}) collective-permute-start(f32[1,2,16,128]{3,2,1,0:T(8,128)S(1)} %pad_maximum_fusion.9), channel_id=1, source_target_pairs={{0,1},{1,2},{2,3},{3,4},{4,5},{5,6},{6,7},{8,9},{9,10},{10,11},{11... | collective-permute-start | bytes 49160 | tf_op jit(solution)/shard_map/ppermute | solution.py:21
  114.7 2.2 %collective-permute-start.7 = (f32[1,2,32,128]{3,2,1,0:T(8,128)S(1)}, f32[1,2,32,128]{3,2,1,0:T(8,128)S(1)}, u32[]{:S(2)}, u32[]{:S(2)}) collective-permute-start(f32[1,2,32,128]{3,2,1,0:T(8,128)S(1)} %slice_bitcast_fusion.31), channel_id=1, source_target_pairs={{0,8},{8,16},{16,24},{24,32},{32,40},{40,48},{48,56},{56,64},{64,7... | collective-permute-start | bytes 98312 | tf_op jit(solution)/shard_map/ppermute | solution.py:21
  117.0 3.9 %collective-permute-start.6 = (f32[1,2,16,128]{3,2,1,0:T(8,128)S(1)}, f32[1,2,16,128]{3,2,1,0:T(8,128)S(1)}, u32[]{:S(2)}, u32[]{:S(2)}) collective-permute-start(f32[1,2,16,128]{3,2,1,0:T(8,128)S(1)} %pad_maximum_fusion.5), channel_id=1, source_target_pairs={{0,1},{1,2},{2,3},{3,4},{4,5},{5,6},{6,7},{8,9},{9,10},{10,11},{11... | collective-permute-start | bytes 49160 | tf_op jit(solution)/shard_map/ppermute | solution.py:21
  120.9 0.6 collective-permute-done.6
  122.3 0.7 copy-done.17
  123.2 0.6 fusion.14
  123.9 0.9 add_reduce_fusion
  126.9 24.7 %all_to_all.36 = f32[128,2,256]{2,1,0:T(2,128)S(1)} all-to-all(f32[128,2,256]{2,1,0:T(2,128)S(1)} %all_to_all.30), channel_id=1, replica_groups=mesh['gx'=16,'gy'=8] {'gx','gy'}, dimensions={0} | all-to-all | bytes 524288 | tf_op jit(solution)/shard_map/all_to_all | solution.py:178
  151.8 1.0 convolution_select_fusion
  (247 shorter events, 14.5 us)
Async XLA Ops:
  2.3 18.4 %copy-start.1 = (f32[3,16,32,128]{3,2,1,0:T(8,128)S(1)}, f32[3,16,32,128]{3,2,1,0:T(8,128)}, u32[]{:S(2)}) copy-start(f32[3,16,32,128]{3,2,1,0:T(8,128)} %param.11) | copy-start | bytes 2359300
  4.7 3.5 %copy-start.25 = (s32[128,1]{0,1:T(1,128)S(1)}, s32[128,1]{0,1:T(1,128)}, u32[]{:S(2)}) copy-start(s32[128,1]{0,1:T(1,128)} %param.17) | copy-start | bytes 1540
  4.7 37.9 %collective-permute-start.9 = (f32[1,2,32,128]{3,1,2,0:T(2,128)}, f32[1,2,32,128]{3,1,2,0:T(2,128)}, u32[]{:S(2)}, u32[]{:S(2)}) collective-permute-start(f32[1,2,32,128]{3,1,2,0:T(2,128)} %slice_bitcast_fusion.30), channel_id=1, source_target_pairs={{8,0},{16,8},{24,16},{32,24},{40,32},{48,40},{56,48},{64,56},{72,6... | collective-permute-start | bytes 98312 | tf_op jit(solution)/shard_map/ppermute | solution.py:21
  8.6 0.7 copy-start.27
  10.1 21.3 %all-to-all-start = ((s32[128,2,1]{1,2,0:T(1,128)}), s32[128,2,1]{1,2,0:T(1,128)S(1)}, u32[]{:S(2)}, u32[]{:S(2)}) async-start(s32[128,2,1]{1,2,0:T(1,128)} %bitcast.1), calls=%async_computation | async-start | bytes 131072 | tf_op jit(solution)/shard_map/all_to_all | solution.py:141
  20.8 4.2 %copy-start.24 = (f32[128,256]{1,0:T(8,128)S(1)}, f32[128,256]{1,0:T(8,128)}, u32[]{:S(2)}) copy-start(f32[128,256]{1,0:T(8,128)} %param.16) | copy-start | bytes 393220
  21.3 3.6 %copy-start.26 = (s32[128]{0:T(128)S(1)}, s32[128]{0:T(128)}, u32[]{:S(2)}) copy-start(s32[128]{0:T(128)} %param.18) | copy-start | bytes 1540
  22.0 23.9 %collective-permute-start.1 = (f32[1,2,32,128]{3,1,2,0:T(2,128)}, f32[1,2,32,128]{3,1,2,0:T(2,128)}, u32[]{:S(2)}, u32[]{:S(2)}) collective-permute-start(f32[1,2,32,128]{3,1,2,0:T(2,128)} %slice_bitcast_fusion.33), channel_id=1, source_target_pairs={{8,0},{16,8},{24,16},{32,24},{40,32},{48,40},{56,48},{64,56},{72,6... | collective-permute-start | bytes 98312 | tf_op jit(solution)/shard_map/ppermute | solution.py:21
  31.5 47.0 %all-to-all-start.1 = ((f32[128,2,256]{2,1,0:T(2,128)}), f32[128,2,256]{2,1,0:T(2,128)}, u32[]{:S(2)}, u32[]{:S(2)}) async-start(f32[128,2,256]{2,1,0:T(2,128)} %all_to_all.27), calls=%async_computation.1 | async-start | bytes 524288 | tf_op jit(solution)/shard_map/all_to_all | solution.py:140
  45.8 1.0 copy-start.23
  48.1 4.5 %collective-permute-start.8 = (f32[1,2,16,128]{3,2,1,0:T(8,128)S(1)}, f32[1,2,16,128]{3,2,1,0:T(8,128)S(1)}, u32[]{:S(2)}, u32[]{:S(2)}) collective-permute-start(f32[1,2,16,128]{3,2,1,0:T(8,128)S(1)} %pad_maximum_fusion.6), channel_id=1, source_target_pairs={{1,0},{2,1},{3,2},{4,3},{5,4},{6,5},{7,6},{9,8},{10,9},{11,10},{12... | collective-permute-start | bytes 49160 | tf_op jit(solution)/shard_map/ppermute | solution.py:21
  49.8 3.2 %copy-start.9 = (f32[1,16,32,128]{3,2,1,0:T(8,128)}, f32[1,16,32,128]{3,2,1,0:T(8,128)S(1)}, u32[]{:S(2)}) copy-start(f32[1,16,32,128]{3,2,1,0:T(8,128)S(1)} %copy.361) | copy-start | bytes 786436
  49.9 5.2 %collective-permute-start = (f32[1,2,16,128]{3,2,1,0:T(8,128)S(1)}, f32[1,2,16,128]{3,2,1,0:T(8,128)S(1)}, u32[]{:S(2)}, u32[]{:S(2)}) collective-permute-start(f32[1,2,16,128]{3,2,1,0:T(8,128)S(1)} %pad_maximum_fusion.2), channel_id=1, source_target_pairs={{1,0},{2,1},{3,2},{4,3},{5,4},{6,5},{7,6},{9,8},{10,9},{11,10},{12... | collective-permute-start | bytes 49160 | tf_op jit(solution)/shard_map/ppermute | solution.py:21
  51.7 4.6 %copy-start.7 = (f32[1,16,32,128]{3,2,1,0:T(8,128)}, f32[1,16,32,128]{3,2,1,0:T(8,128)S(1)}, u32[]{:S(2)}) copy-start(f32[1,16,32,128]{3,2,1,0:T(8,128)S(1)} %copy.332) | copy-start | bytes 786436
  51.7 1.0 copy-start.22
  52.9 0.7 copy-start.5
  52.9 1.2 copy-start.2
  54.1 0.7 copy-start.15
  55.1 1.0 copy-start.21
  56.2 1.1 copy-start.3
  57.3 0.7 copy-start.13
  58.2 16.7 %collective-permute-start.11 = (f32[1,2,32,128]{3,2,1,0:T(8,128)S(1)}, f32[1,2,32,128]{3,2,1,0:T(8,128)S(1)}, u32[]{:S(2)}, u32[]{:S(2)}) collective-permute-start(f32[1,2,32,128]{3,2,1,0:T(8,128)S(1)} %slice_bitcast_fusion.29), channel_id=1, source_target_pairs={{0,8},{8,16},{16,24},{24,32},{32,40},{40,48},{48,56},{56,64},{64,7... | collective-permute-start | bytes 98312 | tf_op jit(solution)/shard_map/ppermute | solution.py:21
  62.7 11.5 %collective-permute-start.10 = (f32[1,2,16,128]{3,2,1,0:T(8,128)S(1)}, f32[1,2,16,128]{3,2,1,0:T(8,128)S(1)}, u32[]{:S(2)}, u32[]{:S(2)}) collective-permute-start(f32[1,2,16,128]{3,2,1,0:T(8,128)S(1)} %pad_maximum_fusion.7), channel_id=1, source_target_pairs={{0,1},{1,2},{2,3},{3,4},{4,5},{5,6},{6,7},{8,9},{9,10},{10,11},{11... | collective-permute-start | bytes 49160 | tf_op jit(solution)/shard_map/ppermute | solution.py:21
  67.2 9.5 %collective-permute-start.3 = (f32[1,2,32,128]{3,2,1,0:T(8,128)S(1)}, f32[1,2,32,128]{3,2,1,0:T(8,128)S(1)}, u32[]{:S(2)}, u32[]{:S(2)}) collective-permute-start(f32[1,2,32,128]{3,2,1,0:T(8,128)S(1)} %slice_bitcast_fusion.32), channel_id=1, source_target_pairs={{0,8},{8,16},{16,24},{24,32},{32,40},{40,48},{48,56},{56,64},{64,7... | collective-permute-start | bytes 98312 | tf_op jit(solution)/shard_map/ppermute | solution.py:21
  69.5 5.1 %collective-permute-start.2 = (f32[1,2,16,128]{3,2,1,0:T(8,128)S(1)}, f32[1,2,16,128]{3,2,1,0:T(8,128)S(1)}, u32[]{:S(2)}, u32[]{:S(2)}) collective-permute-start(f32[1,2,16,128]{3,2,1,0:T(8,128)S(1)} %pad_maximum_fusion.3), channel_id=1, source_target_pairs={{0,1},{1,2},{2,3},{3,4},{4,5},{5,6},{6,7},{8,9},{9,10},{10,11},{11... | collective-permute-start | bytes 49160 | tf_op jit(solution)/shard_map/ppermute | solution.py:21
  82.2 6.6 %copy-start = (f32[3,16,32,128]{3,2,1,0:T(8,128)S(1)}, f32[3,16,32,128]{3,2,1,0:T(8,128)}, u32[]{:S(2)}) copy-start(f32[3,16,32,128]{3,2,1,0:T(8,128)} %param.13) | copy-start | bytes 2359300
  87.7 1.1 copy-start.11
  87.7 1.1 copy-start.12
  91.8 10.4 %collective-permute-start.13 = (f32[1,2,32,128]{3,2,1,0:T(8,128)S(1)}, f32[1,2,32,128]{3,2,1,0:T(8,128)S(1)}, u32[]{:S(2)}, u32[]{:S(2)}) collective-permute-start(f32[1,2,32,128]{3,2,1,0:T(8,128)S(1)} %slice_bitcast_fusion.28), channel_id=1, source_target_pairs={{8,0},{16,8},{24,16},{32,24},{40,32},{48,40},{56,48},{64,56},{72,6... | collective-permute-start | bytes 98312 | tf_op jit(solution)/shard_map/ppermute | solution.py:21
  94.8 5.0 %collective-permute-start.12 = (f32[1,2,16,128]{3,2,1,0:T(8,128)S(1)}, f32[1,2,16,128]{3,2,1,0:T(8,128)S(1)}, u32[]{:S(2)}, u32[]{:S(2)}) collective-permute-start(f32[1,2,16,128]{3,2,1,0:T(8,128)S(1)} %pad_maximum_fusion.8), channel_id=1, source_target_pairs={{1,0},{2,1},{3,2},{4,3},{5,4},{6,5},{7,6},{9,8},{10,9},{11,10},{12... | collective-permute-start | bytes 49160 | tf_op jit(solution)/shard_map/ppermute | solution.py:21
  96.5 5.7 %collective-permute-start.4 = (f32[1,2,16,128]{3,2,1,0:T(8,128)S(1)}, f32[1,2,16,128]{3,2,1,0:T(8,128)S(1)}, u32[]{:S(2)}, u32[]{:S(2)}) collective-permute-start(f32[1,2,16,128]{3,2,1,0:T(8,128)S(1)} %pad_maximum_fusion.4), channel_id=1, source_target_pairs={{1,0},{2,1},{3,2},{4,3},{5,4},{6,5},{7,6},{9,8},{10,9},{11,10},{12... | collective-permute-start | bytes 49160 | tf_op jit(solution)/shard_map/ppermute | solution.py:21
  97.8 6.0 %collective-permute-start.5 = (f32[1,2,32,128]{3,1,2,0:T(2,128)S(1)}, f32[1,2,32,128]{3,1,2,0:T(2,128)S(1)}, u32[]{:S(2)}, u32[]{:S(2)}) collective-permute-start(f32[1,2,32,128]{3,1,2,0:T(2,128)S(1)} %bitcast.370), channel_id=1, source_target_pairs={{8,0},{16,8},{24,16},{32,24},{40,32},{48,40},{56,48},{64,56},{72,6... | collective-permute-start | bytes 98312 | tf_op jit(solution)/shard_map/ppermute | solution.py:21
  102.3 1.0 copy-start.6
  102.3 1.0 copy-start.10
  102.3 1.1 copy-start.16
  104.8 1.0 copy-start.8
  104.8 1.0 copy-start.14
  106.3 15.2 %collective-permute-start.15 = (f32[1,2,32,128]{3,2,1,0:T(8,128)S(1)}, f32[1,2,32,128]{3,2,1,0:T(8,128)S(1)}, u32[]{:S(2)}, u32[]{:S(2)}) collective-permute-start(f32[1,2,32,128]{3,2,1,0:T(8,128)S(1)} %slice_bitcast_fusion.27), channel_id=1, source_target_pairs={{0,8},{8,16},{16,24},{24,32},{32,40},{40,48},{48,56},{56,64},{64,7... | collective-permute-start | bytes 98312 | tf_op jit(solution)/shard_map/ppermute | solution.py:21
  110.2 10.7 %collective-permute-start.14 = (f32[1,2,16,128]{3,2,1,0:T(8,128)S(1)}, f32[1,2,16,128]{3,2,1,0:T(8,128)S(1)}, u32[]{:S(2)}, u32[]{:S(2)}) collective-permute-start(f32[1,2,16,128]{3,2,1,0:T(8,128)S(1)} %pad_maximum_fusion.9), channel_id=1, source_target_pairs={{0,1},{1,2},{2,3},{3,4},{4,5},{5,6},{6,7},{8,9},{9,10},{10,11},{11... | collective-permute-start | bytes 49160 | tf_op jit(solution)/shard_map/ppermute | solution.py:21
  114.7 6.9 %collective-permute-start.7 = (f32[1,2,32,128]{3,2,1,0:T(8,128)S(1)}, f32[1,2,32,128]{3,2,1,0:T(8,128)S(1)}, u32[]{:S(2)}, u32[]{:S(2)}) collective-permute-start(f32[1,2,32,128]{3,2,1,0:T(8,128)S(1)} %slice_bitcast_fusion.31), channel_id=1, source_target_pairs={{0,8},{8,16},{16,24},{24,32},{32,40},{40,48},{48,56},{56,64},{64,7... | collective-permute-start | bytes 98312 | tf_op jit(solution)/shard_map/ppermute | solution.py:21
  117.0 4.6 %collective-permute-start.6 = (f32[1,2,16,128]{3,2,1,0:T(8,128)S(1)}, f32[1,2,16,128]{3,2,1,0:T(8,128)S(1)}, u32[]{:S(2)}, u32[]{:S(2)}) collective-permute-start(f32[1,2,16,128]{3,2,1,0:T(8,128)S(1)} %pad_maximum_fusion.5), channel_id=1, source_target_pairs={{0,1},{1,2},{2,3},{3,4},{4,5},{5,6},{6,7},{8,9},{9,10},{10,11},{11... | collective-permute-start | bytes 49160 | tf_op jit(solution)/shard_map/ppermute | solution.py:21
  122.0 1.0 copy-start.17
  122.1 1.0 copy-start.18
  122.1 1.1 copy-start.19
  122.1 1.2 copy-start.20
  123.9 0.9 copy-start.4
where the time goes:
time: 154 us; the launch traced here: 153 us
  starting transfers between devices  66.6 us (43%)
  local copies, waits for them, and re-layouts  32.1 us (21%)
  blocking collectives  24.7 us (16%)
  other arithmetic  19.6 us (13%)
  waiting for transfers between devices  3.97 us (3%)
  matrix products  3.44 us (2%)
  between operations  2.4 us (2%)
    ppermute x16, starting transfers between devices, passed_along(): return lax.ppermute(block, axis, route)  46.4 us
    all_to_all x1, blocking collectives, shards(): lax.all_to_all(picked, ('gx', 'gy'), split_axis=0, concat_axis=0, tiled=T...  24.7 us
    unnamed x67, local copies, waits for them, and re-layouts  12.7 us
    all_to_all x1, starting transfers between devices, shards(): lax.all_to_all(starts_out, ('gx', 'gy'), split_axis=0, concat_axis=0, til...  10.6 us
    all_to_all x1, starting transfers between devices, shards(): lax.all_to_all(outgoing, ('gx', 'gy'), split_axis=0, concat_axis=0, tiled...  9.62 us
    slice x18, local copies, waits for them, and re-layouts, raise_edge(): rest = lax.slice_in_dim(values, 1, values.shape[axis], axis=axis)  4.01 us
    ppermute x16, waiting for transfers between devices, passed_along(): return lax.ppermute(block, axis, route)  3.96 us
    scatter-add x1, local copies, waits for them, and re-layouts, shards(): permittivity.at[:, :, lower:lower + DLAYERS].add(contrast * sigma)  3.54 us
  transfers between devices with their start and end apart: 18, of which 5 were waited for; matrix products, arithmetic and copies ran while one was open for 14% of the time, Pallas kernels for 0%

commit v1 on v0

v1 whole, which is shorter than its diff:
```python
import functools
import math

import jax
import jax.numpy as jnp
from jax import lax
from jax.experimental import pallas as pl
from jax.experimental.pallas import tpu as pltpu
from jax.sharding import PartitionSpec as P

F32 = jnp.float32
LANES = 128
LAYERS = 32
LOWER = 48
COURANT = 0.5
ANGULAR = 0.9
CONTRAST = 8.0
EXACT = lax.Precision.HIGHEST

NX, NY = 16, 32
EX, EY = 20, 40
UP_ROWS = 23
DOWN_ROWS = 17
ROWS = 16


def iota(shape, dim):
    return lax.broadcasted_iota(jnp.int32, shape, dim)


def params(limit):
    return pltpu.CompilerParams(vmem_limit_bytes=limit * 2**20)


def cost(micros):
    return pl.CostEstimate(flops=micros * 10**9, bytes_accessed=0, transcendentals=0)


def vmem():
    return pl.BlockSpec(memory_space=pltpu.VMEM)


def hbm():
    return pl.BlockSpec(memory_space=pltpu.HBM)


def shape(*dims):
    return jax.ShapeDtypeStruct(dims, F32)


def plan(to_next):
    if to_next:
        return [(0, 0, -2, 2), (0, 1, -2, 2), (0, 2, -2, 2), (1, 0, -1, 1), (1, 1, -2, 2), (1, 2, -2, 2)]
    return [(0, 0, 0, 1), (0, 1, 0, 2), (0, 2, 0, 2), (1, 0, 0, 1), (1, 1, 0, 1), (1, 2, 0, 1)]


def plan_y(to_next):
    if to_next:
        return [(0, 0, -2, 2), (0, 1, -2, 2), (0, 2, -2, 2), (1, 0, -2, 2), (1, 1, -1, 1), (1, 2, -2, 2)]
    return [(0, 0, 0, 2), (0, 1, 0, 1), (0, 2, 0, 2), (1, 0, 0, 1), (1, 1, 0, 1), (1, 2, 0, 1)]


def run_copies(pairs, sems):
    copies = [pltpu.make_async_copy(a, b, sems.at[i]) for i, (a, b) in enumerate(pairs)]
    for c in copies:
        c.start()
    for c in copies:
        c.wait()


def faces_x(ef, hf, ea, ha, perm, up, down, sems):
    pairs = []
    for to_next, out in ((True, up), (False, down)):
        at = 0
        for fields in ((ef, hf), (ea, ha)):
            for field, comp, first, count in plan(to_next):
                first = first % NX
                pairs.append((fields[field].at[comp, pl.ds(first, count)], out.at[pl.ds(at, count)]))
                at += count
        pairs.append((perm.at[pl.ds(NX - 1 if to_next else 0, 1)], out.at[pl.ds(at, 1)]))
    run_copies(pairs, sems)


def send_x(ef, hf, ea, ha, perm):
    return pl.pallas_call(
        faces_x,
        out_shape=(shape(UP_ROWS, NY, LANES), shape(DOWN_ROWS, NY, LANES)),
        in_specs=[hbm()] * 5,
        out_specs=(vmem(), vmem()),
        scratch_shapes=[pltpu.SemaphoreType.DMA((26,))],
        compiler_params=params(63),
        cost_estimate=cost(1),
        name="faces_x",
    )(ef, hf, ea, ha, perm)


def x_halo_pairs(dest, dest_perm, below, above, low, high):
    pairs = []
    rows = pl.ds(low, high - low)
    for from_prev, src in ((True, below), (False, above)):
        at = 0
        for evolution in range(2):
            for field, comp, first, count in plan(from_prev):
                place = first + 2 if from_prev else NX + 2 + first
                c = field * 6 + evolution * 3 + comp
                pairs.append(
                    (src.at[pl.ds(at, count), rows], dest.at[c, pl.ds(place, count), pl.ds(0, high - low)])
                )
                at += count
        place = 1 if from_prev else NX + 2
        pairs.append((src.at[pl.ds(at, 1), rows], dest_perm.at[pl.ds(place, 1), pl.ds(0, high - low)]))
    return pairs


def faces_y(ef, hf, ea, ha, perm, below, above, up, down, first, last, first_perm, last_perm, sems):
    pairs = []
    for dest, dest_perm, low in ((first, first_perm, 0), (last, last_perm, NY - 8)):
        rows = pl.ds(low, 8)
        for i, src in enumerate((ef, ea, hf, ha)):
            for comp in range(3):
                pairs.append((src.at[comp, :, rows], dest.at[i * 3 + comp, pl.ds(2, NX)]))
        pairs.append((perm.at[:, rows], dest_perm.at[pl.ds(2, NX)]))
        pairs += x_halo_pairs(dest, dest_perm, below, above, low, low + 8)
    run_copies(pairs, sems)
    for to_next, src, src_perm, out in (
        (True, last, last_perm, up),
        (False, first, first_perm, down),
    ):
        flat = src.reshape(12 * EX * 8, LANES)
        flat_perm = src_perm.reshape(EX * 8, LANES)
        at = 0
        for evolution in range(2):
            for field, comp, begin, count in plan_y(to_next):
                for k in range(count):
                    row = (begin + k) % 8
                    c = field * 6 + evolution * 3 + comp
                    out[pl.ds(at * EX, EX), :] = flat[pl.ds(c * EX * 8 + row, EX, stride=8), :]
                    at += 1
        out[pl.ds(at * EX, EX), :] = flat_perm[pl.ds(7 if to_next else 0, EX, stride=8), :]


def send_y(ef, hf, ea, ha, perm, below, above):
    return pl.pallas_call(
        faces_y,
        out_shape=(shape(UP_ROWS * EX, LANES), shape(DOWN_ROWS * EX, LANES)),
        in_specs=[hbm()] * 5 + [vmem()] * 2,
        out_specs=(vmem(), vmem()),
        scratch_shapes=[
            pltpu.VMEM((12, EX, 8, LANES), F32),
            pltpu.VMEM((12, EX, 8, LANES), F32),
            pltpu.VMEM((EX, 8, LANES), F32),
            pltpu.VMEM((EX, 8, LANES), F32),
            pltpu.SemaphoreType.DMA((78,)),
        ],
        compiler_params=params(63),
        cost_estimate=cost(200),
        name="faces_y",
    )(ef, hf, ea, ha, perm, below, above)


def pack_tiles(pattern, owner, count, start, message, match):
    tiles = pattern.shape[0]
    square = (tiles, tiles)
    down, across = iota(square, 0), iota(square, 1)
    eye = down == across

    def column(row):
        return jnp.sum(jnp.where(eye, row.astype(F32), 0.0), axis=1, keepdims=True)

    owner_row = owner[...].astype(F32)
    owner_col = column(owner[...])
    same = owner_col == owner_row
    rank_row = jnp.sum(jnp.where(same & (down < across), 1.0, 0.0), axis=0, keepdims=True)
    rank_col = jnp.sum(jnp.where(same & (across < down), 1.0, 0.0), axis=1, keepdims=True)
    down_f, across_f = down.astype(F32), across.astype(F32)
    for k in range(2):
        match[:, k * tiles : (k + 1) * tiles] = jnp.where(
            (owner_col == across_f) & (rank_col == k), 1.0, 0.0
        )
    starts = column(start[...]).astype(jnp.int32)
    counts = column(count[...]).astype(jnp.int32)
    shift = starts & (LANES - 1)
    first = starts >> 7
    phase = first & 7
    wide = iota(pattern.shape, 1)
    cells = jnp.where(wide < counts, pattern[...], 0.0)
    for bit in range(7):
        cells = jnp.where((shift >> bit) & 1 == 1, pltpu.roll(cells, 1 << bit, 1), cells)
    front, back = cells[:, :LANES], cells[:, LANES:]
    head = jnp.where(across >= shift, front, 0.0)
    tail = jnp.where(across >= shift, 0.0, front)

    def pick(a, b, c):
        return jnp.where(
            phase == a, head, jnp.where(phase == b, back, jnp.where(phase == c, tail, 0.0))
        )

    low_y = pick(0, 7, 6)
    high_y = pick(7, 6, 5)
    low_corner = pltpu.roll(jnp.where((first + 7) >> 3 == NX - 1, low_y, 0.0), 32, 1)
    high_corner = pltpu.roll(jnp.where(first >> 3 == 0, high_y, 0.0), 96, 1)
    edges = jnp.where(
        across < 32,
        low_y,
        jnp.where(across < 64, low_corner, jnp.where(across < 96, high_corner, high_y)),
    )
    origin = jnp.broadcast_to(starts.astype(F32), square)
    everything = jnp.concatenate([front, back, edges, origin], axis=1)
    meta = jnp.zeros(square, F32)
    for k in range(2):
        choose = jnp.where((owner_row == down_f) & (rank_row == k), 1.0, 0.0)
        slots = jnp.dot(choose, everything, precision=EXACT, preferred_element_type=F32)
        pair = slots[:, : 2 * LANES]
        edge = slots[:, 2 * LANES : 3 * LANES]
        origins = slots[:, 3 * LANES :]

        def other(values, distance):
            return pltpu.roll(values, -distance % tiles, 0)

        for place, distance in ((0, 0), (4, 8), (8, -8)):
            rows = other(pair, distance) if distance else pair
            for half in range(2):
                message[pl.ds(place + 2 * k + half, tiles, stride=ROWS), :] = rows[
                    :, half * LANES : (half + 1) * LANES
                ]
        message[pl.ds(12 + k, tiles, stride=ROWS), :] = jnp.where(
            across < 32,
            other(edge, 1),
            jnp.where(across < 64, other(edge, -7), jnp.where(across < 96, other(edge, 7), other(edge, -1))),
        )
        for place, distance in enumerate((0, 8, -8, 1, -1)):
            moved = other(origins, distance) if distance else origins
            meta = jnp.where(across == 2 * place + k, moved, meta)
    message[pl.ds(14, tiles, stride=ROWS), :] = meta
    message[pl.ds(15, tiles, stride=ROWS), :] = jnp.zeros(square, F32)


def pack(pattern, owners, tile_count, tile_start):
    tiles = pattern.shape[0]
    return pl.pallas_call(
        pack_tiles,
        out_shape=(shape(tiles * ROWS, LANES), shape(tiles, 2 * tiles)),
        in_specs=[vmem()] * 4,
        out_specs=(vmem(), vmem()),
        compiler_params=params(16),
        cost_estimate=cost(2),
        name="pack_tiles",
    )(pattern, owners.reshape(1, tiles), tile_count.reshape(1, tiles), tile_start.reshape(1, tiles))


def after_y(values):
    return pltpu.roll(values, values.shape[0] - 1, 0)


def before_y(values):
    return pltpu.roll(values, 1, 0)


def after_z(values):
    return jnp.where(iota(values.shape, 1) == LANES - 1, 0.0, pltpu.roll(values, LANES - 1, 1))


def before_z(values):
    return jnp.where(iota(values.shape, 1) == 0, 0.0, pltpu.roll(values, 1, 1))


def curl_e(here, ahead):
    ex, ey, ez = here
    next_y, next_z = ahead
    return (
        (after_y(ez) - ez) - (after_z(ey) - ey),
        (after_z(ex) - ex) - (next_z - ez),
        (next_y - ey) - (after_y(ex) - ex),
    )


def curl_h(here, behind):
    hx, hy, hz = here
    last_y, last_z = behind
    return (
        (hz - before_y(hz)) - (hy - before_z(hy)),
        (hx - before_z(hx)) - (hz - last_z),
        (hy - last_y) - (hx - before_y(hx)),
    )


def evolve(
    ef, hf, ea, ha, perm, below, above, before, after, message,
    final, reply,
    fields, perm_wide, rate, grow, turned, overlap, sems,
):
    pairs = []
    for i, src in enumerate((ef, ea, hf, ha)):
        for comp in range(3):
            pairs.append((src.at[comp], fields.at[i * 3 + comp, pl.ds(2, NX), pl.ds(0, NY)]))
    pairs.append((perm, perm_wide.at[pl.ds(2, NX), pl.ds(0, NY)]))
    pairs += x_halo_pairs(fields, perm_wide, below, above, 0, NY)
    copies = [pltpu.make_async_copy(a, b, sems.at[i]) for i, (a, b) in enumerate(pairs)]
    for copy in copies:
        copy.start()
    tiles = message.shape[0] // ROWS
    square = (tiles, LANES)
    across = iota(square, 1)

    def rows_of(place):
        return message[pl.ds(place, tiles, stride=ROWS), :]

    meta = rows_of(14)
    meta_rows = meta.T

    def start_row(index):
        return meta_rows[index : index + 1, :].astype(jnp.int32)

    def start_col(index):
        return meta[:, index : index + 1].astype(jnp.int32)

    def place_cells(place, index, base, count):
        targets, values = [], []
        for k in range(2):
            first = start_row(index + k) >> 7
            shift = start_col(index + k) & (LANES - 1)
            front, back = rows_of(place + 2 * k), rows_of(place + 2 * k + 1)
            for step, part in enumerate(
                (
                    jnp.where(across >= shift, front, 0.0),
                    back,
                    jnp.where(across >= shift, 0.0, front),
                )
            ):
                row = iota((count, tiles), 0) + base
                targets.append(jnp.where(first + step == row, 1.0, 0.0))
                values.append(part)
        return jnp.dot(
            jnp.concatenate(targets, axis=1),
            jnp.concatenate(values, axis=0),
            precision=EXACT,
            preferred_element_type=F32,
        )

    def lift(density):
        return CONTRAST * jax.nn.sigmoid(density)

    block = NX * 8
    sigma = jax.nn.sigmoid(place_cells(0, 0, 0, block))
    own = CONTRAST * sigma
    ahead = lift(place_cells(4, 2, 0, 8))
    behind = lift(place_cells(8, 4, block - 8, 8))
    targets = []
    for k in range(2):
        first = start_row(6 + k) >> 7
        last = start_row(8 + k) >> 7
        row = iota((40, tiles), 0)
        targets.append(
            jnp.where(
                (((first + 7) >> 3 == row) & (row < NX))
                | ((last >> 3) + NX == row)
                | (row >= 2 * NX),
                1.0,
                0.0,
            )
        )
    sides = lift(
        jnp.dot(
            jnp.concatenate(targets, axis=1),
            jnp.concatenate([rows_of(12), rows_of(13)], axis=0),
            precision=EXACT,
            preferred_element_type=F32,
        )
    )

    def lanes_to(values, source):
        lane = iota(values.shape, 1)
        moved = pltpu.roll(values, (LOWER - source) % LANES, 1)
        return jnp.where((lane >= LOWER) & (lane < LOWER + LAYERS), moved, 0.0)

    grow[...] = jnp.zeros_like(grow)
    for quarter in range(4):
        source = quarter * LAYERS
        moved = lanes_to(own, source)
        for x in range(NX):
            grow[pl.ds((x + 2) * EY + quarter, 8, stride=4), :] = moved[8 * x : 8 * x + 8]
        grow[pl.ds((NX + 2) * EY + quarter, 8, stride=4), :] = lanes_to(ahead, source)
        grow[pl.ds(EY + quarter, 8, stride=4), :] = lanes_to(behind, source)
    grow[pl.ds(2 * EY + NY, NX, stride=EY), :] = lanes_to(sides[:NX], 0)
    grow[pl.ds(2 * EY + EY - 1, NX, stride=EY), :] = lanes_to(sides[NX : 2 * NX], 96)
    corner = sides[2 * NX : 2 * NX + 8]
    grow[pl.ds(EY + NY, 1), :] = lanes_to(corner, 32)[:1]
    grow[pl.ds((NX + 2) * EY + EY - 1, 1), :] = lanes_to(corner, 64)[:1]

    gx, gy = lax.axis_index("gx"), lax.axis_index("gy")
    low_x, high_x = gx > 0, gx < lax.axis_size("gx") - 1
    low_y, high_y = gy > 0, gy < lax.axis_size("gy") - 1
    y = iota((EY, LANES), 0)
    within = (y < NY) | ((y == NY) & high_y) | ((y == EY - 1) & low_y)


    for copy in copies:
        copy.wait()
    flat = fields.reshape(12 * EX * EY, LANES)
    flat_perm = perm_wide.reshape(EX * EY, LANES)
    for from_prev, src in ((True, before), (False, after)):
        at = 0
        for evolution in range(2):
            for field, comp, begin, count in plan_y(from_prev):
                for k in range(count):
                    row = EY + begin + k if from_prev else NY + begin + k
                    c = field * 6 + evolution * 3 + comp
                    flat[pl.ds(c * EX * EY + row, EX, stride=EY), :] = src[pl.ds(at * EX, EX), :]
                    at += 1
        row = EY - 1 if from_prev else NY
        flat_perm[pl.ds(row, EX, stride=EY), :] = src[pl.ds(at * EX, EX), :]
    cut = jnp.where((y < EY - 2) | low_y, COURANT, 0.0)

    for x in range(NX + 3):
        factor = cut if x >= 2 else jnp.where(low_x, cut, 0.0)
        for e in (0, 3):
            here = [fields[e + c, x] for c in range(3)]
            curl = curl_e(here, [fields[e + c, x + 1] for c in (1, 2)])
            for c in range(3):
                turned[6 + e + c, x] = fields[6 + e + c, x] - factor * curl[c]
    for x in range(1, NX + 3):
        eps = perm_wide[x] + grow[pl.ds(x * EY, EY), :]
        inside = within
        if x == 1:
            inside = within & low_x
        if x == NX + 2:
            inside = within & high_x
        scale = jnp.where(inside, COURANT / eps, 0.0)
        rate[x] = scale
        for e in (0, 3):
            here = [turned[6 + e + c, x] for c in range(3)]
            curl = curl_h(here, [turned[6 + e + c, x - 1] for c in (1, 2)])
            for c in range(3):
                turned[e + c, x] = fields[e + c, x] + scale * curl[c]
    for x in range(1, NX + 2):
        factor = cut if x >= 2 else jnp.where(low_x, cut, 0.0)
        for e in (0, 3):
            here = [turned[e + c, x] for c in range(3)]
            curl = curl_e(here, [turned[e + c, x + 1] for c in (1, 2)])
            for c in range(3):
                fields[6 + e + c, x] = turned[6 + e + c, x] - factor * curl[c]
    blend = math.cos(ANGULAR)
    for x in range(2, NX + 2):
        scale = rate[x]
        old, new = [], []
        for e in (0, 3):
            here = [fields[6 + e + c, x] for c in range(3)]
            curl = curl_h(here, [fields[6 + e + c, x - 1] for c in (1, 2)])
            old.append([turned[e + c, x][:NY] for c in range(3)])
            new.append([old[-1][c] + (scale * curl[c])[:NY] for c in range(3)])
        total = 0.0
        for c in range(3):
            final[c, x - 2] = new[0][c]
            total += old[0][c] * (old[1][c] + blend * new[1][c])
            total += new[0][c] * (new[1][c] + blend * old[1][c])
        overlap[pl.ds((x - 2) * NY, NY), :] = total
    compact = jnp.zeros((block, LANES), F32)
    lane = iota((block, LANES), 1)
    for quarter in range(4):
        part = pltpu.roll(
            overlap[pl.ds(quarter, block, stride=4), :], (quarter * LAYERS - LOWER) % LANES, 1
        )
        compact = jnp.where(lane // LAYERS == quarter, part, compact)
    gradient = own * (1.0 - sigma) * compact
    for k in range(2):
        starts = start_col(k)
        first, shift = starts >> 7, starts & (LANES - 1)
        picks = [jnp.where(iota((tiles, block), 1) == first + step, 1.0, 0.0) for step in range(3)]
        found = jnp.dot(
            jnp.concatenate(picks, axis=0), gradient, precision=EXACT, preferred_element_type=F32
        )
        reply[pl.ds(2 * k, tiles, stride=4), :] = jnp.where(
            across >= shift, found[:tiles], found[2 * tiles :]
        )
        reply[pl.ds(2 * k + 1, tiles, stride=4), :] = found[tiles : 2 * tiles]


def run_fields(ef, hf, ea, ha, perm, below, above, before, after, message):
    tiles = message.shape[0] // ROWS
    return pl.pallas_call(
        evolve,
        out_shape=(shape(3, NX, NY, LANES), shape(tiles * 4, LANES)),
        in_specs=[hbm()] * 5 + [vmem()] * 5,
        out_specs=(vmem(), vmem()),
        scratch_shapes=[
            pltpu.VMEM((12, EX, EY, LANES), F32),
            pltpu.VMEM((EX, EY, LANES), F32),
            pltpu.VMEM((EX, EY, LANES), F32),
            pltpu.VMEM((EX * EY, LANES), F32),
            pltpu.VMEM((12, EX, EY, LANES), F32),
            pltpu.VMEM((NX * NY, LANES), F32),
            pltpu.SemaphoreType.DMA((39,)),
        ],
        compiler_params=params(63),
        cost_estimate=cost(8),
        name="evolve",
    )(ef, hf, ea, ha, perm, below, above, before, after, message)


def unpack_tiles(reply, match, count, start, out):
    tiles = out.shape[0]
    eye = iota((tiles, tiles), 0) == iota((tiles, tiles), 1)

    def column(row):
        values = jnp.sum(jnp.where(eye, row.astype(F32), 0.0), axis=1, keepdims=True)
        return values.astype(jnp.int32)

    shift = column(start[...]) & (LANES - 1)
    rows = [
        jnp.concatenate(
            [reply[pl.ds(2 * k + half, tiles, stride=4), :] for half in range(2)], axis=1
        )
        for k in range(2)
    ]
    cells = jnp.dot(
        match[...], jnp.concatenate(rows, axis=0), precision=EXACT, preferred_element_type=F32
    )
    width = out.shape[1]
    for bit in range(7):
        cells = jnp.where((shift >> bit) & 1 == 1, pltpu.roll(cells, width - (1 << bit), 1), cells)
    out[...] = jnp.where(iota(out.shape, 1) < column(count[...]), cells, 0.0)


def unpack(reply, match, tile_count, tile_start):
    tiles = match.shape[0]
    return pl.pallas_call(
        unpack_tiles,
        out_shape=shape(tiles, 2 * LANES),
        in_specs=[vmem()] * 4,
        out_specs=vmem(),
        compiler_params=params(16),
        cost_estimate=cost(2),
        name="unpack_tiles",
    )(reply, match, tile_count.reshape(1, tiles), tile_start.reshape(1, tiles))


def passed(block, axis, distance):
    devices = range(lax.axis_size(axis))
    return lax.ppermute(
        block, axis, [(i, i + distance) for i in devices if i + distance in devices]
    )


def exchange(block, rows):
    tiles = block.shape[0] // rows
    out = lax.all_to_all(
        block.reshape(tiles, rows, LANES), ("gx", "gy"), split_axis=0, concat_axis=0, tiled=True
    )
    return out.reshape(tiles * rows, LANES)


def shards(ef, hf, ea, ha, perm, pattern, owners, tile_count, tile_start):
    up, down = send_x(ef, hf, ea, ha, perm)
    up, down, pattern = lax.optimization_barrier((up, down, pattern))
    below, above = passed(up, "gx", 1), passed(down, "gx", -1)
    message, match = pack(pattern, owners, tile_count, tile_start)
    arrived = exchange(message, ROWS)
    up, down = send_y(ef, hf, ea, ha, perm, below, above)
    before, after = passed(up, "gy", 1), passed(down, "gy", -1)
    final, reply = run_fields(ef, hf, ea, ha, perm, below, above, before, after, arrived)
    returned = exchange(reply, 4)
    return final, unpack(returned, match, tile_count, tile_start)


def solution(mesh):
    grid = P(None, "gx", "gy", None)
    tiles = ("gx", "gy")
    return jax.shard_map(
        shards,
        mesh=mesh,
        in_specs=(grid,) * 4 + (P("gx", "gy", None), P(tiles, None), P(tiles, None), P(tiles), P(tiles)),
        out_specs=(grid, P(tiles, None)),
        check_vma=False,
    )
```

time: 154 us -> 77.6 us (0.50)
  starting transfers between devices: 66.6 us -> 23.2 us
  local copies, waits for them, and re-layouts: 32.1 us -> 3.47 us
  other arithmetic: 19.6 us -> 0 us
  Pallas kernels: 0 us -> 17.8 us
  waiting for transfers between devices: 3.97 us -> 11.1 us
  blocking collectives: 24.7 us -> 20.9 us
  matrix products: 3.44 us -> 0 us
  between operations: 2.4 us -> 0.77 us
    ppermute x16 -> x4, starting transfers between devices: 46.4 us -> 11.2 us  [passed(): lax.ppermute(block, axis, [(i, i + distance) for i in devices if i + dist...]
    pallas_call x0 -> x5, Pallas kernels: none -> 17.8 us  [the longest x1 7.56 us: run_fields(): pl.pallas_call(evolve, out_shape=(shape(3, NX, NY, LANES), shape(tiles *...]
    unnamed x67 -> x20, local copies, waits for them, and re-layouts: 12.7 us -> 3.47 us
    all_to_all x2 -> x1, starting transfers between devices: 20.2 us -> 12 us  [exchange(): lax.all_to_all(block.reshape(tiles, rows, LANES), ('gx', 'gy'), split_axi...]
    slice x80 -> x0, local copies, waits for them, and re-layouts: 7.57 us -> none  [the longest x18 4.01 us: raise_edge(): rest = lax.slice_in_dim(values, 1, values.shape[axis], axis=axis)]
    ppermute x16 -> x4, waiting for transfers between devices: 3.96 us -> 11.1 us  [passed(): lax.ppermute(block, axis, [(i, i + distance) for i in devices if i + dist...]
    sub x21 -> x0, other arithmetic: 6.23 us -> none  [the longest x4 2.44 us: advance(): mag_z - lower_edge(mag_z, 2, before_y[:, 1])]
    all_to_all x8 -> x0, local copies, waits for them, and re-layouts: 4.82 us -> none  [the longest x3 3.06 us: shards(): lax.all_to_all(outgoing, ('gx', 'gy'), split_axis=0, concat_axis=0, tiled...]
  transfers between devices with their start and end apart: 18 -> 5, of which waited for: 5 -> 2; matrix products, arithmetic and copies ran while one was open for 14% -> 0% of each run, Pallas kernels for 0% -> 9%
where the time goes in v1:
time: 77.6 us; the launch traced here: 77.2 us
  starting transfers between devices  23.2 us (30%)
  blocking collectives  20.9 us (27%)
  Pallas kernels  17.8 us (23%)
  waiting for transfers between devices  11.1 us (14%)
  local copies, waits for them, and re-layouts  3.47 us (4%)
    all_to_all x1, blocking collectives, exchange(): lax.all_to_all(block.reshape(tiles, rows, LANES), ('gx', 'gy'), split_axi...  20.9 us
    all_to_all x1, starting transfers between devices, exchange(): lax.all_to_all(block.reshape(tiles, rows, LANES), ('gx', 'gy'), split_axi...  12 us
    ppermute x4, starting transfers between devices, passed(): lax.ppermute(block, axis, [(i, i + distance) for i in devices if i + dist...  11.2 us
    ppermute x4, waiting for transfers between devices, passed(): lax.ppermute(block, axis, [(i, i + distance) for i in devices if i + dist...  11.1 us
    pallas_call x1, Pallas kernels, run_fields(): pl.pallas_call(evolve, out_shape=(shape(3, NX, NY, LANES), shape(tiles *...  7.56 us
    pallas_call x1, Pallas kernels, send_y(): pl.pallas_call(faces_y, out_shape=(shape(UP_ROWS * EX, LANES), shape(DOWN...  4.1 us
    unnamed x20, local copies, waits for them, and re-layouts  3.47 us
    pallas_call x1, Pallas kernels, pack(): pl.pallas_call(pack_tiles, out_shape=(shape(tiles * ROWS, LANES), shape(t...  2.54 us
  transfers between devices with their start and end apart: 5, of which 2 were waited for; matrix products, arithmetic and copies ran while one was open for 0% of the time, Pallas kernels for 9%

profile of v1, /device:TPU:1, one launch (start us, length us, event | category | flops | bytes accessed | tf_op | source)
XLA Modules:
  0.0 77.2 jit_solution(11967089370883670291)
XLA Ops:
  0.6 0.0 copy-start
  0.6 2.1 %faces_x.1 = (f32[23,32,128]{2,1,0:T(8,128)}, f32[17,32,128]{2,1,0:T(8,128)}) custom-call(f32[3,16,32,128]{3,2,1,0:T(8,128)} %ef.5, f32[3,16,32,128]{3,2,1,0:T(8,128)} %hf.5, f32[3,16,32,128]{3,2,1,0:T(8,128)} %ea.5, f32[3,16,32,128]{3,2,1,0:T(8,128)} %ha.5, f32[16,32,128]{2,1,0:T(8,128)} %perm.5), custom_call_target="tpu_custom_call" | custom-call | flops 1000000000 | tf_op jit(solution)/shard_map/faces_x/pallas_call | solution.py:85
  2.7 4.6 %collective-permute-start = (f32[23,32,128]{2,1,0:T(8,128)}, f32[23,32,128]{2,1,0:T(8,128)S(1)}, u32[]{:S(2)}, u32[]{:S(2)}) collective-permute-start(f32[23,32,128]{2,1,0:T(8,128)} %get-tuple-element.15), channel_id=1, source_target_pairs={{0,8},{8,16},{16,24},{24,32},{32,40},{40,48},{48,56},{56,64},{64,7... | collective-permute-start | bytes 1130504 | tf_op jit(solution)/shard_map/ppermute | solution.py:539
  7.4 1.9 %collective-permute-start.1 = (f32[17,32,128]{2,1,0:T(8,128)}, f32[17,32,128]{2,1,0:T(8,128)S(1)}, u32[]{:S(2)}, u32[]{:S(2)}) collective-permute-start(f32[17,32,128]{2,1,0:T(8,128)} %get-tuple-element.16), channel_id=1, source_target_pairs={{8,0},{16,8},{24,16},{32,24},{40,32},{48,40},{56,48},{64,56},{72,6... | collective-permute-start | bytes 835592 | tf_op jit(solution)/shard_map/ppermute | solution.py:539
  9.3 0.0 copy-start.1
  9.3 0.0 copy-start.2
  9.3 0.0 copy-start.4
  9.3 0.0 copy-done
  9.3 0.6 copy-done.1
  9.9 0.0 copy-done.2
  10.0 0.0 copy-done.4
  10.0 2.5 %pack_tiles.1 = (f32[2048,128]{1,0:T(8,128)}, f32[128,256]{1,0:T(8,128)S(1)}) custom-call(f32[128,256]{1,0:T(8,128)S(1)} %copy-done, s32[1,128]{1,0:T(1,128)S(1)} %bitcast.8, s32[1,128]{1,0:T(1,128)S(1)} %bitcast.9, s32[1,128]{1,0:T(1,128)S(1)} %bitcast.11), custom_call_target="tpu_custom_call" | custom-call | flops 2000000000 | tf_op jit(solution)/shard_map/pack_tiles/pallas_call | solution.py:240
  12.5 12.0 %all-to-all-start = ((f32[128,16,128]{2,1,0:T(8,128)}), f32[128,16,128]{2,1,0:T(8,128)}, u32[]{:S(2)}, u32[]{:S(2)}) async-start(f32[128,16,128]{2,1,0:T(8,128)} %bitcast.3), calls=%async_computation | async-start | bytes 2097152 | tf_op jit(solution)/shard_map/all_to_all | solution.py:546
  24.5 0.0 collective-permute-done.1.above
  24.5 0.0 copy-start.7
  24.5 0.0 collective-permute-done.below
  24.5 0.7 copy-done.7
  25.2 0.0 copy-start.6
  25.2 0.7 copy-done.6
  26.0 4.1 %faces_y.1 = (f32[460,128]{1,0:T(8,128)}, f32[340,128]{1,0:T(8,128)}) custom-call(f32[3,16,32,128]{3,2,1,0:T(8,128)} %ef.5, f32[3,16,32,128]{3,2,1,0:T(8,128)} %hf.5, f32[3,16,32,128]{3,2,1,0:T(8,128)} %ea.5, f32[3,16,32,128]{3,2,1,0:T(8,128)} %ha.5, f32[16,32,128]{2,1,0:T(8,128)} %perm.5, f32[23,32,128]{2,1,0:T(8,128)} %copy-done.6, f32[17,32,128]{2,1,0:T(8,128)} %copy-done.7), custom_call_target="tpu_custom_call" | custom-call | flops 199999995904 | tf_op jit(solution)/shard_map/faces_y/pallas_call | solution.py:143
  30.1 3.4 %collective-permute-start.2 = (f32[460,128]{1,0:T(8,128)}, f32[460,128]{1,0:T(8,128)S(1)}, u32[]{:S(2)}, u32[]{:S(2)}) collective-permute-start(f32[460,128]{1,0:T(8,128)} %get-tuple-element.17), channel_id=1, source_target_pairs={{0,1},{1,2},{2,3},{3,4},{4,5},{5,6},{6,7},{8,9},{9,10},{10,11},{11... | collective-permute-start | bytes 706568 | tf_op jit(solution)/shard_map/ppermute | solution.py:539
  33.5 1.3 %collective-permute-start.3 = (f32[340,128]{1,0:T(8,128)}, f32[340,128]{1,0:T(8,128)S(1)}, u32[]{:S(2)}, u32[]{:S(2)}) collective-permute-start(f32[340,128]{1,0:T(8,128)} %get-tuple-element.18), channel_id=1, source_target_pairs={{1,0},{2,1},{3,2},{4,3},{5,4},{6,5},{7,6},{9,8},{10,9},{11,10},{12... | collective-permute-start | bytes 522248 | tf_op jit(solution)/shard_map/ppermute | solution.py:539
  34.8 9.1 %collective-permute-done.3.after = f32[340,128]{1,0:T(8,128)S(1)} collective-permute-done((f32[340,128]{1,0:T(8,128)}, f32[340,128]{1,0:T(8,128)S(1)}, u32[]{:S(2)}, u32[]{:S(2)}) %collective-permute-start.3) | collective-permute-done | bytes 174112 | tf_op jit(solution)/shard_map/ppermute | solution.py:539
  43.9 0.0 copy-start.9
  43.9 1.9 %collective-permute-done.2.before = f32[460,128]{1,0:T(8,128)S(1)} collective-permute-done((f32[460,128]{1,0:T(8,128)}, f32[460,128]{1,0:T(8,128)S(1)}, u32[]{:S(2)}, u32[]{:S(2)}) %collective-permute-start.2) | collective-permute-done | bytes 235552 | tf_op jit(solution)/shard_map/ppermute | solution.py:539
  45.9 0.0 copy-start.8
  45.9 0.0 all-to-all-done
  45.9 0.0 copy-done.9
  45.9 0.7 copy-done.8
  46.6 7.6 %evolve.1 = (f32[3,16,32,128]{3,2,1,0:T(8,128)}, f32[512,128]{1,0:T(8,128)}) custom-call(f32[3,16,32,128]{3,2,1,0:T(8,128)} %ef.5, f32[3,16,32,128]{3,2,1,0:T(8,128)} %hf.5, f32[3,16,32,128]{3,2,1,0:T(8,128)} %ea.5, f32[3,16,32,128]{3,2,1,0:T(8,128)} %ha.5, f32[16,32,128]{2,1,0:T(8,128)} %perm.5, f32[23,32,128]{2,1,0:T(8,128)} %copy-done.6, ...), custom_call_target="tpu_custom_call" | custom-call | flops 8000000000 | tf_op jit(solution)/shard_map/evolve/pallas_call | solution.py:480
  54.2 20.9 %all_to_all.10 = f32[128,4,128]{2,1,0:T(4,128)S(1)} all-to-all(f32[128,4,128]{2,1,0:T(4,128)} %bitcast.13), channel_id=1, replica_groups=mesh['gx'=16,'gy'=8] {'gx','gy'}, dimensions={0} | all-to-all | bytes 524288 | tf_op jit(solution)/shard_map/all_to_all | solution.py:546
  75.0 0.0 copy-start.3
  75.0 0.0 copy-start.5
  75.0 0.7 copy-done.3
  75.7 0.0 copy-done.5
  75.7 1.5 %unpack_tiles.1 = f32[128,256]{1,0:T(8,128)} custom-call(f32[512,128]{1,0:T(8,128)S(1)} %bitcast.7, f32[128,256]{1,0:T(8,128)S(1)} %get-tuple-element.23.match, s32[1,128]{1,0:T(1,128)S(1)} %bitcast.10, s32[1,128]{1,0:T(1,128)S(1)} %bitcast.12), custom_call_target="tpu_custom_call" | custom-call | flops 2000000000 | tf_op jit(solution)/shard_map/unpack_tiles/pallas_call | solution.py:526
Async XLA Ops:
  0.6 8.7 %copy-start = (f32[128,256]{1,0:T(8,128)S(1)}, f32[128,256]{1,0:T(8,128)}, u32[]{:S(2)}) copy-start(f32[128,256]{1,0:T(8,128)} %pattern) | copy-start | bytes 393220
  2.7 21.8 %collective-permute-start = (f32[23,32,128]{2,1,0:T(8,128)}, f32[23,32,128]{2,1,0:T(8,128)S(1)}, u32[]{:S(2)}, u32[]{:S(2)}) collective-permute-start(f32[23,32,128]{2,1,0:T(8,128)} %get-tuple-element.15), channel_id=1, source_target_pairs={{0,8},{8,16},{16,24},{24,32},{32,40},{40,48},{48,56},{56,64},{64,7... | collective-permute-start | bytes 1130504 | tf_op jit(solution)/shard_map/ppermute | solution.py:539
  7.4 17.2 %collective-permute-start.1 = (f32[17,32,128]{2,1,0:T(8,128)}, f32[17,32,128]{2,1,0:T(8,128)S(1)}, u32[]{:S(2)}, u32[]{:S(2)}) collective-permute-start(f32[17,32,128]{2,1,0:T(8,128)} %get-tuple-element.16), channel_id=1, source_target_pairs={{8,0},{16,8},{24,16},{32,24},{40,32},{48,40},{56,48},{64,56},{72,6... | collective-permute-start | bytes 835592 | tf_op jit(solution)/shard_map/ppermute | solution.py:539
  9.3 0.7 copy-start.1
  9.3 0.7 copy-start.2
  9.3 0.7 copy-start.4
  12.5 33.4 %all-to-all-start = ((f32[128,16,128]{2,1,0:T(8,128)}), f32[128,16,128]{2,1,0:T(8,128)}, u32[]{:S(2)}, u32[]{:S(2)}) async-start(f32[128,16,128]{2,1,0:T(8,128)} %bitcast.3), calls=%async_computation | async-start | bytes 2097152 | tf_op jit(solution)/shard_map/all_to_all | solution.py:546
  24.5 0.7 copy-start.7
  25.2 0.7 copy-start.6
  30.1 15.8 %collective-permute-start.2 = (f32[460,128]{1,0:T(8,128)}, f32[460,128]{1,0:T(8,128)S(1)}, u32[]{:S(2)}, u32[]{:S(2)}) collective-permute-start(f32[460,128]{1,0:T(8,128)} %get-tuple-element.17), channel_id=1, source_target_pairs={{0,1},{1,2},{2,3},{3,4},{4,5},{5,6},{6,7},{8,9},{9,10},{10,11},{11... | collective-permute-start | bytes 706568 | tf_op jit(solution)/shard_map/ppermute | solution.py:539
  33.5 10.4 %collective-permute-start.3 = (f32[340,128]{1,0:T(8,128)}, f32[340,128]{1,0:T(8,128)S(1)}, u32[]{:S(2)}, u32[]{:S(2)}) collective-permute-start(f32[340,128]{1,0:T(8,128)} %get-tuple-element.18), channel_id=1, source_target_pairs={{1,0},{2,1},{3,2},{4,3},{5,4},{6,5},{7,6},{9,8},{10,9},{11,10},{12... | collective-permute-start | bytes 522248 | tf_op jit(solution)/shard_map/ppermute | solution.py:539
  43.9 1.9 %copy-start.9 = (f32[340,128]{1,0:T(8,128)}, f32[340,128]{1,0:T(8,128)S(1)}, u32[]{:S(2)}) copy-start(f32[340,128]{1,0:T(8,128)S(1)} %collective-permute-done.3.after) | copy-start | bytes 522244
  45.9 0.7 copy-start.8
  75.0 0.7 copy-start.3
  75.0 0.7 copy-start.5

commit v2 on v1

v2 whole, which is shorter than its diff:
```python
import functools
import math

import jax
import jax.numpy as jnp
from jax import lax
from jax.experimental import pallas as pl
from jax.experimental.pallas import tpu as pltpu
from jax.sharding import PartitionSpec as P

F32 = jnp.float32
LANES = 128
LAYERS = 32
LOWER = 48
COURANT = 0.5
ANGULAR = 0.9
CONTRAST = 8.0
EXACT = lax.Precision.HIGHEST

NX, NY = 16, 32
EX, EY = 20, 40
UP_ROWS = 23
DOWN_ROWS = 17
ROWS = 15


def iota(shape, dim):
    return lax.broadcasted_iota(jnp.int32, shape, dim)


def params(limit):
    return pltpu.CompilerParams(vmem_limit_bytes=limit * 2**20)


def cost(micros):
    return pl.CostEstimate(flops=micros * 10**9, bytes_accessed=0, transcendentals=0)


def vmem():
    return pl.BlockSpec(memory_space=pltpu.VMEM)


def anywhere():
    return pl.BlockSpec(memory_space=pl.ANY)


def hbm():
    return pl.BlockSpec(memory_space=pltpu.HBM)


def shape(*dims):
    return jax.ShapeDtypeStruct(dims, F32)


def select_rows(marks, values):
    width = values.shape[1]
    high = values.astype(jnp.bfloat16)
    low = (values - high.astype(F32)).astype(jnp.bfloat16)
    found = jnp.dot(
        marks.astype(jnp.bfloat16),
        jnp.concatenate([high, low], axis=1),
        preferred_element_type=F32,
    )
    return found[:, :width] + found[:, width:]


def plan(to_next):
    if to_next:
        return [(0, 0, -2, 2), (0, 1, -2, 2), (0, 2, -2, 2), (1, 0, -1, 1), (1, 1, -2, 2), (1, 2, -2, 2)]
    return [(0, 0, 0, 1), (0, 1, 0, 2), (0, 2, 0, 2), (1, 0, 0, 1), (1, 1, 0, 1), (1, 2, 0, 1)]


def plan_y(to_next):
    if to_next:
        return [(0, 0, -2, 2), (0, 1, -2, 2), (0, 2, -2, 2), (1, 0, -2, 2), (1, 1, -1, 1), (1, 2, -2, 2)]
    return [(0, 0, 0, 2), (0, 1, 0, 1), (0, 2, 0, 2), (1, 0, 0, 1), (1, 1, 0, 1), (1, 2, 0, 1)]


def pack_tiles(pattern, owner, count, start, message, match):
    tiles = pattern.shape[0]
    square = (tiles, tiles)
    down, across = iota(square, 0), iota(square, 1)
    eye = down == across

    def column(row):
        return jnp.sum(jnp.where(eye, row.astype(F32), 0.0), axis=1, keepdims=True)

    owner_row = owner[...].astype(F32)
    owner_col = column(owner[...])
    same = owner_col == owner_row
    rank_row = jnp.sum(jnp.where(same & (down < across), 1.0, 0.0), axis=0, keepdims=True)
    rank_col = jnp.sum(jnp.where(same & (across < down), 1.0, 0.0), axis=1, keepdims=True)
    down_f, across_f = down.astype(F32), across.astype(F32)
    for k in range(2):
        match[:, k * tiles : (k + 1) * tiles] = jnp.where(
            (owner_col == across_f) & (rank_col == k), 1.0, 0.0
        )
    starts = column(start[...]).astype(jnp.int32)
    counts = column(count[...]).astype(jnp.int32)
    shift = starts & (LANES - 1)
    first = starts >> 7
    phase = first & 7
    match[:, 2 * tiles :] = jnp.where(
        across == 0, shift.astype(F32), jnp.where(across == 1, counts.astype(F32), 0.0)
    )
    wide = iota(pattern.shape, 1)
    cells = jnp.where(wide < counts, pattern[...], 0.0)
    for bit in range(7):
        cells = jnp.where((shift >> bit) & 1 == 1, pltpu.roll(cells, 1 << bit, 1), cells)
    front, back = cells[:, :LANES], cells[:, LANES:]
    head = jnp.where(across >= shift, front, 0.0)
    tail = jnp.where(across >= shift, 0.0, front)

    def pick(a, b, c):
        return jnp.where(
            phase == a, head, jnp.where(phase == b, back, jnp.where(phase == c, tail, 0.0))
        )

    low_y = pick(0, 7, 6)
    high_y = pick(7, 6, 5)
    low_corner = pltpu.roll(jnp.where((first + 7) >> 3 == NX - 1, low_y, 0.0), 32, 1)
    high_corner = pltpu.roll(jnp.where(first >> 3 == 0, high_y, 0.0), 96, 1)
    edges = jnp.where(
        across < 32,
        low_y,
        jnp.where(across < 64, low_corner, jnp.where(across < 96, high_corner, high_y)),
    )
    origin = jnp.broadcast_to(starts.astype(F32), square)
    everything = jnp.concatenate([front, back, edges, origin], axis=1)
    meta = jnp.zeros(square, F32)
    choose = [jnp.where((owner_row == down_f) & (rank_row == k), 1.0, 0.0) for k in range(2)]
    every_slot = select_rows(jnp.concatenate(choose, axis=0), everything)
    for k in range(2):
        slots = every_slot[k * tiles : (k + 1) * tiles]
        pair = slots[:, : 2 * LANES]
        edge = slots[:, 2 * LANES : 3 * LANES]
        origins = slots[:, 3 * LANES :]

        def other(values, distance):
            return pltpu.roll(values, -distance % tiles, 0)

        for place, distance in ((0, 0), (4, 8), (8, -8)):
            rows = other(pair, distance) if distance else pair
            for half in range(2):
                message[pl.ds(place + 2 * k + half, tiles, stride=ROWS), :] = rows[
                    :, half * LANES : (half + 1) * LANES
                ]
        message[pl.ds(12 + k, tiles, stride=ROWS), :] = jnp.where(
            across < 32,
            other(edge, 1),
            jnp.where(across < 64, other(edge, -7), jnp.where(across < 96, other(edge, 7), other(edge, -1))),
        )
        for place, distance in enumerate((0, 8, -8, 1, -1)):
            moved = other(origins, distance) if distance else origins
            meta = jnp.where(across == 2 * place + k, moved, meta)
    message[pl.ds(14, tiles, stride=ROWS), :] = meta


def prepare_all(
    ef, hf, ea, ha, perm, pattern_hbm, owner_hbm, count_hbm, start_hbm,
    up_x, down_x, up_y, down_y, message, match,
    first, last, first_perm, last_perm, first_x, last_x, first_x_perm, last_x_perm,
    pattern, owner, count, start, sems,
):
    small = [(owner_hbm, owner), (count_hbm, count), (start_hbm, start), (pattern_hbm, pattern)]
    loads_x, loads_y = [], []
    for begin, out, out_perm in ((NX - 2, last_x, last_x_perm), (0, first_x, first_x_perm)):
        for i, src in enumerate((ef, ea, hf, ha)):
            loads_x.append((src.at[:, pl.ds(begin, 2)], out.at[pl.ds(3 * i, 3)]))
        loads_x.append((perm.at[pl.ds(begin, 2)], out_perm))
    for dest, dest_perm, low in ((first, first_perm, 0), (last, last_perm, NY - 8)):
        rows = pl.ds(low, 8)
        for i, src in enumerate((ef, ea, hf, ha)):
            loads_y.append((src.at[:, :, rows], dest.at[pl.ds(3 * i, 3)]))
        loads_y.append((perm.at[:, rows], dest_perm))
    copies = [
        pltpu.make_async_copy(a, b, sems.at[i]) for i, (a, b) in enumerate(small + loads_y + loads_x)
    ]
    for copy in copies:
        copy.start()
    for copy in copies[:4]:
        copy.wait()
    pack_tiles(pattern, owner, count, start, message, match)
    for copy in copies[4:]:
        copy.wait()
    for to_next, src, src_perm, out in ((True, last, last_perm, up_y), (False, first, first_perm, down_y)):
        flat = src.reshape(12 * NX * 8, LANES)
        flat_perm = src_perm.reshape(NX * 8, LANES)
        at = 0
        for evolution in range(2):
            for field, comp, begin, planes in plan_y(to_next):
                for k in range(planes):
                    row = (field * 6 + evolution * 3 + comp) * NX * 8 + (begin + k) % 8
                    out[pl.ds(at * NX, NX), :] = flat[pl.ds(row, NX, stride=8), :]
                    at += 1
        out[pl.ds(at * NX, NX), :] = flat_perm[pl.ds(7 if to_next else 0, NX, stride=8), :]
    for to_next, src, src_perm, out in (
        (True, last_x, last_x_perm, up_x),
        (False, first_x, first_x_perm, down_x),
    ):
        at = 0
        for evolution in range(2):
            for field, comp, begin, planes in plan(to_next):
                for k in range(planes):
                    out[at] = src[field * 6 + evolution * 3 + comp, (begin + k) % 2]
                    at += 1
        out[at] = src_perm[1 if to_next else 0]


def prepare(ef, hf, ea, ha, perm, pattern, owners, tile_count, tile_start):
    tiles = pattern.shape[0]
    return pl.pallas_call(
        prepare_all,
        out_shape=(
            shape(UP_ROWS, NY, LANES),
            shape(DOWN_ROWS, NY, LANES),
            shape(UP_ROWS * NX, LANES),
            shape(DOWN_ROWS * NX, LANES),
            shape(tiles * ROWS, LANES),
            shape(tiles, 3 * tiles),
        ),
        in_specs=[hbm()] * 9,
        out_specs=(vmem(),) * 6,
        scratch_shapes=[
            pltpu.VMEM((12, NX, 8, LANES), F32),
            pltpu.VMEM((12, NX, 8, LANES), F32),
            pltpu.VMEM((NX, 8, LANES), F32),
            pltpu.VMEM((NX, 8, LANES), F32),
            pltpu.VMEM((12, 2, NY, LANES), F32),
            pltpu.VMEM((12, 2, NY, LANES), F32),
            pltpu.VMEM((2, NY, LANES), F32),
            pltpu.VMEM((2, NY, LANES), F32),
            pltpu.VMEM((tiles, 2 * LANES), F32),
            pltpu.VMEM((1, tiles), jnp.int32),
            pltpu.VMEM((1, tiles), jnp.int32),
            pltpu.VMEM((1, tiles), jnp.int32),
            pltpu.SemaphoreType.DMA((24,)),
        ],
        compiler_params=params(56),
        cost_estimate=cost(3),
        name="prepare",
    )(
        ef, hf, ea, ha, perm, pattern,
        owners.reshape(1, tiles), tile_count.reshape(1, tiles), tile_start.reshape(1, tiles),
    )


def after_y(values):
    return pltpu.roll(values, values.shape[0] - 1, 0)


def before_y(values):
    return pltpu.roll(values, 1, 0)


def after_z(values):
    return jnp.where(iota(values.shape, 1) == LANES - 1, 0.0, pltpu.roll(values, LANES - 1, 1))


def before_z(values):
    return jnp.where(iota(values.shape, 1) == 0, 0.0, pltpu.roll(values, 1, 1))


def curl_e(here, ahead):
    ex, ey, ez = here
    next_y, next_z = ahead
    return (
        (after_y(ez) - ez) - (after_z(ey) - ey),
        (after_z(ex) - ex) - (next_z - ez),
        (next_y - ey) - (after_y(ex) - ex),
    )


def curl_h(here, behind):
    hx, hy, hz = here
    last_y, last_z = behind
    return (
        (hz - before_y(hz)) - (hy - before_z(hy)),
        (hx - before_z(hx)) - (hz - last_z),
        (hy - last_y) - (hx - before_y(hx)),
    )


def evolve(
    ef, hf, ea, ha, perm, below_any, above_any, before_any, after_any, low_any, high_any, message_any,
    final, reply,
    final_v, forward, adjoint, perm_wide, rate, grow, turned, overlap, below, above, before, after, low, high, message, sems,
):
    wide = (forward, adjoint)
    pairs = [
        (message_any, message),
        (below_any, below),
        (above_any, above),
        (before_any, before),
        (after_any, after),
        (low_any, low),
        (high_any, high),
    ]
    pairs.append((perm, perm_wide.at[pl.ds(2, NX), pl.ds(0, NY)]))
    for i, src in ((0, ef), (1, hf), (2, ea), (3, ha)):
        pairs.append((src, wide[i // 2].at[pl.ds(3 * (i % 2), 3), pl.ds(2, NX), pl.ds(0, NY)]))
    copies = [pltpu.make_async_copy(a, b, sems.at[i]) for i, (a, b) in enumerate(pairs)]
    for copy in copies:
        copy.start()
    final_copy = pltpu.make_async_copy(final_v, final, sems.at[12])
    copies[0].wait()
    tiles = message.shape[0] // ROWS
    square = (tiles, LANES)
    across = iota(square, 1)

    def rows_of(place):
        return message[pl.ds(place, tiles, stride=ROWS), :]

    meta = rows_of(14)
    meta_rows = meta.T

    def start_row(index):
        return meta_rows[index : index + 1, :].astype(jnp.int32)

    def start_col(index):
        return meta[:, index : index + 1].astype(jnp.int32)

    def place_cells(place, index, base, count):
        targets, values = [], []
        for k in range(2):
            first = start_row(index + k) >> 7
            shift = start_col(index + k) & (LANES - 1)
            front, back = rows_of(place + 2 * k), rows_of(place + 2 * k + 1)
            for step, part in enumerate(
                (
                    jnp.where(across >= shift, front, 0.0),
                    back,
                    jnp.where(across >= shift, 0.0, front),
                )
            ):
                row = iota((count, tiles), 0) + base
                targets.append(jnp.where(first + step == row, 1.0, 0.0))
                values.append(part)
        return select_rows(jnp.concatenate(targets, axis=1), jnp.concatenate(values, axis=0))

    def lift(density):
        return CONTRAST * jax.nn.sigmoid(density)

    block = NX * 8
    sigma = jax.nn.sigmoid(place_cells(0, 0, 0, block))
    own = CONTRAST * sigma
    ahead = lift(place_cells(4, 2, 0, 16)[:8])
    behind = lift(place_cells(8, 4, block - 16, 16)[8:])
    targets = []
    for k in range(2):
        first = start_row(6 + k) >> 7
        last = start_row(8 + k) >> 7
        row = iota((48, tiles), 0)
        targets.append(
            jnp.where(
                (((first + 7) >> 3 == row) & (row < NX))
                | ((last >> 3) + NX == row)
                | (row >= 2 * NX),
                1.0,
                0.0,
            )
        )
    sides = lift(
        select_rows(
            jnp.concatenate(targets, axis=1), jnp.concatenate([rows_of(12), rows_of(13)], axis=0)
        )
    )

    def lanes_to(values, source):
        lane = iota(values.shape, 1)
        moved = pltpu.roll(values, (LOWER - source) % LANES, 1)
        return jnp.where((lane >= LOWER) & (lane < LOWER + LAYERS), moved, 0.0)

    grow[...] = jnp.zeros_like(grow)
    for quarter in range(4):
        source = quarter * LAYERS
        moved = lanes_to(own, source)
        for x in range(NX):
            grow[pl.ds((x + 2) * EY + quarter, 8, stride=4), :] = moved[8 * x : 8 * x + 8]
        grow[pl.ds((NX + 2) * EY + quarter, 8, stride=4), :] = lanes_to(ahead, source)
        grow[pl.ds(EY + quarter, 8, stride=4), :] = lanes_to(behind, source)
    grow[pl.ds(2 * EY + NY, NX, stride=EY), :] = lanes_to(sides[:NX], 0)
    grow[pl.ds(2 * EY + EY - 1, NX, stride=EY), :] = lanes_to(sides[NX : 2 * NX], 96)
    corner = sides[2 * NX : 2 * NX + 8]
    grow[pl.ds(EY + NY, 1), :] = lanes_to(corner, 32)[:1]
    grow[pl.ds((NX + 2) * EY + EY - 1, 1), :] = lanes_to(corner, 64)[:1]

    gx, gy = lax.axis_index("gx"), lax.axis_index("gy")
    low_x, high_x = gx > 0, gx < lax.axis_size("gx") - 1
    low_y, high_y = gy > 0, gy < lax.axis_size("gy") - 1
    y = iota((EY, LANES), 0)
    within = (y < NY) | ((y == NY) & high_y) | ((y == EY - 1) & low_y)


    for copy in copies[1:8]:
        copy.wait()
    flat_perm = perm_wide.reshape(EX * EY, LANES)
    for from_prev, beside, along, corner in ((True, before, below, low), (False, after, above, high)):
        row = EY - 1 if from_prev else NY
        flat_perm[pl.ds(2 * EY + row, NX, stride=EY), :] = beside[pl.ds(beside.shape[0] - NX, NX), :]
        perm_wide[1 if from_prev else NX + 2, :NY, :] = along[along.shape[0] - 1]
        for x in range(2):
            for other_row, at in ((EY - 1, (x + 1) * UP_ROWS - 1), (NY, 2 * UP_ROWS + (x + 1) * DOWN_ROWS - 1)):
                place = (0 if from_prev else NX + 2) + x
                perm_wide[place, other_row : other_row + 1, :] = corner[pl.ds(at, 1), :]

    def fill_halo(evolution):
        fields = wide[evolution]
        flat = fields.reshape(6 * EX * EY, LANES)
        for from_prev, beside, along in ((True, before, below), (False, after, above)):
            at = evolution * (beside.shape[0] // NX // 2)
            for field, comp, begin, count in plan_y(from_prev):
                for k in range(count):
                    row = EY + begin + k if from_prev else NY + begin + k
                    c = field * 3 + comp
                    flat[pl.ds((c * EX + 2) * EY + row, NX, stride=EY), :] = beside[pl.ds(at * NX, NX), :]
                    for corner, place in ((low, 0), (high, NX + 2)):
                        planes, start = (UP_ROWS, 0) if from_prev else (DOWN_ROWS, 2 * UP_ROWS)
                        for x in range(2):
                            fields[c, place + x, row : row + 1, :] = corner[pl.ds(start + at + x * planes, 1), :]
                    at += 1
            at = evolution * (along.shape[0] // 2)
            for field, comp, begin, count in plan(from_prev):
                for k in range(count):
                    place = begin + k + 2 if from_prev else NX + 2 + begin + k
                    fields[field * 3 + comp, place, :NY, :] = along[at]
                    at += 1

    cut = jnp.where((y < EY - 2) | low_y, COURANT, 0.0)

    for evolution in range(2):
        e, fields = 3 * evolution, wide[evolution]
        for copy in copies[8 + 2 * evolution : 10 + 2 * evolution]:
            copy.wait()
        fill_halo(evolution)
        for x in range(NX + 3):
            factor = cut if x >= 2 else jnp.where(low_x, cut, 0.0)
            here = [fields[c, x] for c in range(3)]
            curl = curl_e(here, [fields[c, x + 1] for c in (1, 2)])
            for c in range(3):
                turned[6 + e + c, x] = fields[3 + c, x] - factor * curl[c]
        for x in range(1, NX + 3):
            if e:
                scale = rate[x]
            else:
                eps = perm_wide[x] + grow[pl.ds(x * EY, EY), :]
                inside = within
                if x == 1:
                    inside = within & low_x
                if x == NX + 2:
                    inside = within & high_x
                scale = jnp.where(inside, COURANT / eps, 0.0)
                rate[x] = scale
            here = [turned[6 + e + c, x] for c in range(3)]
            curl = curl_h(here, [turned[6 + e + c, x - 1] for c in (1, 2)])
            for c in range(3):
                turned[e + c, x] = fields[c, x] + scale * curl[c]
    for x in range(1, NX + 2):
        factor = cut if x >= 2 else jnp.where(low_x, cut, 0.0)
        for e in (0, 3):
            here = [turned[e + c, x] for c in range(3)]
            curl = curl_e(here, [turned[e + c, x + 1] for c in (1, 2)])
            for c in range(3):
                wide[e // 3][3 + c, x] = turned[6 + e + c, x] - factor * curl[c]
    blend = math.cos(ANGULAR)
    for x in range(2, NX + 2):
        scale = rate[x]
        old, new = [], []
        for e in (0, 3):
            here = [wide[e // 3][3 + c, x] for c in range(3)]
            curl = curl_h(here, [wide[e // 3][3 + c, x - 1] for c in (1, 2)])
            old.append([turned[e + c, x][:NY] for c in range(3)])
            new.append([old[-1][c] + (scale * curl[c])[:NY] for c in range(3)])
        total = 0.0
        for c in range(3):
            final_v[c, x - 2] = new[0][c]
            total += old[0][c] * (old[1][c] + blend * new[1][c])
            total += new[0][c] * (new[1][c] + blend * old[1][c])
        overlap[pl.ds((x - 2) * NY, NY), :] = total
    final_copy.start()
    compact = jnp.zeros((block, LANES), F32)
    lane = iota((block, LANES), 1)
    for quarter in range(4):
        part = pltpu.roll(
            overlap[pl.ds(quarter, block, stride=4), :], (quarter * LAYERS - LOWER) % LANES, 1
        )
        compact = jnp.where(lane // LAYERS == quarter, part, compact)
    gradient = own * (1.0 - sigma) * compact
    picks, shifts = [], []
    for k in range(2):
        starts = start_col(k)
        shifts.append(starts & (LANES - 1))
        for step in range(3):
            picks.append(jnp.where(iota((tiles, block), 1) == (starts >> 7) + step, 1.0, 0.0))
    found = select_rows(jnp.concatenate(picks, axis=0), gradient)
    for k in range(2):
        head, back, tail = [found[(3 * k + i) * tiles : (3 * k + i + 1) * tiles] for i in range(3)]
        reply[pl.ds(2 * k, tiles, stride=4), :] = jnp.where(across >= shifts[k], head, tail)
        reply[pl.ds(2 * k + 1, tiles, stride=4), :] = back
    final_copy.wait()


def run_fields(ef, hf, ea, ha, perm, below, above, before, after, low, high, message):
    tiles = message.shape[0] // ROWS
    return pl.pallas_call(
        evolve,
        out_shape=(shape(3, NX, NY, LANES), shape(tiles * 4, LANES)),
        in_specs=[hbm()] * 5 + [anywhere()] * 7,
        out_specs=(hbm(), vmem()),
        scratch_shapes=[
            pltpu.VMEM((3, NX, NY, LANES), F32),
            pltpu.VMEM((6, EX, EY, LANES), F32),
            pltpu.VMEM((6, EX, EY, LANES), F32),
            pltpu.VMEM((EX, EY, LANES), F32),
            pltpu.VMEM((EX, EY, LANES), F32),
            pltpu.VMEM((EX * EY, LANES), F32),
            pltpu.VMEM((12, EX, EY, LANES), F32),
            pltpu.VMEM((NX * NY, LANES), F32),
            pltpu.VMEM(below.shape, F32),
            pltpu.VMEM(above.shape, F32),
            pltpu.VMEM(before.shape, F32),
            pltpu.VMEM(after.shape, F32),
            pltpu.VMEM(low.shape, F32),
            pltpu.VMEM(high.shape, F32),
            pltpu.VMEM(message.shape, F32),
            pltpu.SemaphoreType.DMA((13,)),
        ],
        compiler_params=params(50),
        cost_estimate=cost(8),
        name="evolve",
    )(ef, hf, ea, ha, perm, below, above, before, after, low, high, message)


def unpack_tiles(reply, match, out):
    tiles = out.shape[0]
    shift = match[:, 2 * tiles : 2 * tiles + 1].astype(jnp.int32)
    count = match[:, 2 * tiles + 1 : 2 * tiles + 2].astype(jnp.int32)
    rows = [
        jnp.concatenate(
            [reply[pl.ds(2 * k + half, tiles, stride=4), :] for half in range(2)], axis=1
        )
        for k in range(2)
    ]
    cells = select_rows(match[:, : 2 * tiles], jnp.concatenate(rows, axis=0))
    width = out.shape[1]
    for bit in range(7):
        cells = jnp.where((shift >> bit) & 1 == 1, pltpu.roll(cells, width - (1 << bit), 1), cells)
    out[...] = jnp.where(iota(out.shape, 1) < count, cells, 0.0)


def unpack(reply, match):
    tiles = match.shape[0]
    return pl.pallas_call(
        unpack_tiles,
        out_shape=shape(tiles, 2 * LANES),
        in_specs=[vmem()] * 2,
        out_specs=vmem(),
        compiler_params=params(16),
        cost_estimate=cost(2),
        name="unpack_tiles",
    )(reply, match)


def passed(block, axis, distance):
    devices = range(lax.axis_size(axis))
    return lax.ppermute(
        block, axis, [(i, i + distance) for i in devices if i + distance in devices]
    )


def exchange(block, depth):
    out = lax.all_to_all(
        block.reshape(-1, depth, LANES), ("gx", "gy"), split_axis=0, concat_axis=0, tiled=True
    )
    return out.reshape(block.shape)


def corner_rows(before, after, low, high):
    for out, first in ((low, NX - 2), (high, 0)):
        at = 0
        for src, planes in ((before, UP_ROWS), (after, DOWN_ROWS)):
            for x in range(2):
                out[pl.ds(at, planes), :] = src[pl.ds(first + x, planes, stride=NX), :]
                at += planes


def corners(before, after):
    rows = 2 * (UP_ROWS + DOWN_ROWS)
    return pl.pallas_call(
        corner_rows,
        out_shape=(shape(rows, LANES), shape(rows, LANES)),
        in_specs=[vmem()] * 2,
        out_specs=(vmem(), vmem()),
        compiler_params=params(16),
        cost_estimate=cost(20),
        name="corners",
    )(before, after)


def shards(ef, hf, ea, ha, perm, pattern, owners, tile_count, tile_start):
    up_x, down_x, up_y, down_y, message, match = prepare(
        ef, hf, ea, ha, perm, pattern, owners, tile_count, tile_start
    )
    arrived = exchange(message, 1)
    before, after = passed(up_y, "gy", 1), passed(down_y, "gy", -1)
    below, above = passed(up_x, "gx", 1), passed(down_x, "gx", -1)
    low, high = corners(before, after)
    low, high = passed(low, "gx", 1), passed(high, "gx", -1)
    final, reply = run_fields(
        ef, hf, ea, ha, perm, below, above, before, after, low, high, arrived
    )
    return final, unpack(exchange(reply, 4), match)


def solution(mesh):
    grid = P(None, "gx", "gy", None)
    tiles = ("gx", "gy")
    return jax.shard_map(
        shards,
        mesh=mesh,
        in_specs=(grid,) * 4 + (P("gx", "gy", None), P(tiles, None), P(tiles, None), P(tiles), P(tiles)),
        out_specs=(grid, P(tiles, None)),
        check_vma=False,
    )
```

time: 77.6 us -> 68.8 us (0.89)
  Pallas kernels: 17.8 us -> 11 us
  starting transfers between devices: 23.2 us -> 28.5 us
  waiting for transfers between devices: 11.1 us -> 6.24 us
  local copies, waits for them, and re-layouts: 3.47 us -> 0.03 us
  blocking collectives: 20.9 us -> 21.8 us
    ppermute x4 -> x6, waiting for transfers between devices: 11.1 us -> 4.73 us  [passed(): lax.ppermute(block, axis, [(i, i + distance) for i in devices if i + dist...]
    ppermute x4 -> x6, starting transfers between devices: 11.2 us -> 15.7 us  [passed(): lax.ppermute(block, axis, [(i, i + distance) for i in devices if i + dist...]
    pallas_call x3 -> x2, Pallas kernels: 8.75 us -> 4.52 us  [the longest x1 3.58 us: prepare(): pl.pallas_call(prepare_all, out_shape=(shape(UP_ROWS, NY, LANES), shape(D...]
    unnamed x20 -> x10, local copies, waits for them, and re-layouts: 3.47 us -> 0.03 us
    pallas_call x1, Pallas kernels: 7.56 us -> 5.16 us  [run_fields(): pl.pallas_call(evolve, out_shape=(shape(3, NX, NY, LANES), shape(tiles *...]
    all_to_all x1, waiting for transfers between devices: 0.01 us -> 1.51 us  [exchange(): lax.all_to_all(block.reshape(-1, depth, LANES), ('gx', 'gy'), split_axis=...]
    all_to_all x1, blocking collectives: 20.9 us -> 21.8 us  [exchange(): lax.all_to_all(block.reshape(-1, depth, LANES), ('gx', 'gy'), split_axis=...]
    all_to_all x1, starting transfers between devices: 12 us -> 12.8 us  [exchange(): lax.all_to_all(block.reshape(-1, depth, LANES), ('gx', 'gy'), split_axis=...]
  transfers between devices with their start and end apart: 5 -> 7, of which waited for: 2 -> 3; matrix products, arithmetic and copies ran while one was open for 0% -> 0% of each run, Pallas kernels for 9% -> 1%
where the time goes in v2:
time: 68.8 us; the launch traced here: 68.4 us
  starting transfers between devices  28.5 us (41%)
  blocking collectives  21.8 us (32%)
  Pallas kernels  11 us (16%)
  waiting for transfers between devices  6.24 us (9%)
  between operations  0.78 us (1%)
    all_to_all x1, blocking collectives, exchange(): lax.all_to_all(block.reshape(-1, depth, LANES), ('gx', 'gy'), split_axis=...  21.8 us
    ppermute x6, starting transfers between devices, passed(): lax.ppermute(block, axis, [(i, i + distance) for i in devices if i + dist...  15.7 us
    all_to_all x1, starting transfers between devices, exchange(): lax.all_to_all(block.reshape(-1, depth, LANES), ('gx', 'gy'), split_axis=...  12.8 us
    pallas_call x1, Pallas kernels, run_fields(): pl.pallas_call(evolve, out_shape=(shape(3, NX, NY, LANES), shape(tiles *...  5.16 us
    ppermute x6, waiting for transfers between devices, passed(): lax.ppermute(block, axis, [(i, i + distance) for i in devices if i + dist...  4.73 us
    pallas_call x1, Pallas kernels, prepare(): pl.pallas_call(prepare_all, out_shape=(shape(UP_ROWS, NY, LANES), shape(D...  3.58 us
    all_to_all x1, waiting for transfers between devices, exchange(): lax.all_to_all(block.reshape(-1, depth, LANES), ('gx', 'gy'), split_axis=...  1.51 us
  transfers between devices with their start and end apart: 7, of which 3 were waited for; matrix products, arithmetic and copies ran while one was open for 0% of the time, Pallas kernels for 1%

profile of v2, /device:TPU:1, one launch (start us, length us, event | category | flops | bytes accessed | tf_op | source)
XLA Modules:
  0.0 68.4 jit_solution(13244218331677676086)
XLA Ops:
  0.6 3.6 %prepare.1 = (f32[23,32,128]{2,1,0:T(8,128)}, f32[17,32,128]{2,1,0:T(8,128)}, f32[368,128]{1,0:T(8,128)}, f32[272,128]{1,0:T(8,128)}, f32[1920,128]{1,0:T(8,128)}, /*index=5*/f32[128,384]{1,0:T(8,128)}) custom-call(f32[3,16,32,128]{3,2,1,0:T(8,128)} %ef.3, f32[3,16,32,128]{3,2,1,0:T(8,128)} %hf.3, f32[3,16,32,128]{3,2,1,0:T(8,128)} %ea.3, ...), custom_call_target="tpu_custom_call" | custom-call | flops 3000000000 | tf_op jit(solution)/shard_map/prepare/pallas_call | solution.py:212
  4.2 4.4 %collective-permute-start.2 = (f32[368,128]{1,0:T(8,128)}, f32[368,128]{1,0:T(8,128)S(1)}, u32[]{:S(2)}, u32[]{:S(2)}) collective-permute-start(f32[368,128]{1,0:T(8,128)} %get-tuple-element.14), channel_id=1, source_target_pairs={{0,1},{1,2},{2,3},{3,4},{4,5},{5,6},{6,7},{8,9},{9,10},{10,11},{11... | collective-permute-start | bytes 565256 | tf_op jit(solution)/shard_map/ppermute | solution.py:566
  8.6 1.3 %collective-permute-start.3 = (f32[272,128]{1,0:T(8,128)}, f32[272,128]{1,0:T(8,128)}, u32[]{:S(2)}, u32[]{:S(2)}) collective-permute-start(f32[272,128]{1,0:T(8,128)} %get-tuple-element.15), channel_id=1, source_target_pairs={{1,0},{2,1},{3,2},{4,3},{5,4},{6,5},{7,6},{9,8},{10,9},{11,10},{12... | collective-permute-start | bytes 417800 | tf_op jit(solution)/shard_map/ppermute | solution.py:566
  9.9 12.8 %all-to-all-start = ((f32[1920,1,128]{2,1,0:T(1,128)}), f32[1920,1,128]{2,1,0:T(1,128)}, u32[]{:S(2)}, u32[]{:S(2)}) async-start(f32[1920,1,128]{2,1,0:T(1,128)} %bitcast.11), calls=%async_computation | async-start | bytes 1966080 | tf_op jit(solution)/shard_map/all_to_all | solution.py:572
  22.7 3.0 %collective-permute-start.1 = (f32[17,32,128]{2,1,0:T(8,128)}, f32[17,32,128]{2,1,0:T(8,128)S(1)}, u32[]{:S(2)}, u32[]{:S(2)}) collective-permute-start(f32[17,32,128]{2,1,0:T(8,128)} %get-tuple-element.13), channel_id=1, source_target_pairs={{8,0},{16,8},{24,16},{32,24},{40,32},{48,40},{56,48},{64,56},{72,6... | collective-permute-start | bytes 835592 | tf_op jit(solution)/shard_map/ppermute | solution.py:566
  25.8 0.0 copy-start
  25.8 0.0 copy-start.1
  25.8 0.0 copy-start.2
  25.8 0.0 copy-start.3
  25.8 2.7 %collective-permute-start = (f32[23,32,128]{2,1,0:T(8,128)}, f32[23,32,128]{2,1,0:T(8,128)S(1)}, u32[]{:S(2)}, u32[]{:S(2)}) collective-permute-start(f32[23,32,128]{2,1,0:T(8,128)} %get-tuple-element.12), channel_id=1, source_target_pairs={{0,8},{8,16},{16,24},{24,32},{32,40},{40,48},{48,56},{56,64},{64,7... | collective-permute-start | bytes 1130504 | tf_op jit(solution)/shard_map/ppermute | solution.py:566
  28.5 0.0 collective-permute-done.3.after.after_any
  28.5 0.0 collective-permute-done.2.before.before_any
  28.5 0.9 %corners.1 = (f32[80,128]{1,0:T(8,128)S(1)}, f32[80,128]{1,0:T(8,128)S(1)}) custom-call(f32[368,128]{1,0:T(8,128)S(1)} %collective-permute-done.2.before.before_any, f32[272,128]{1,0:T(8,128)} %collective-permute-done.3.after.after_any), custom_call_target="tpu_custom_call" | custom-call | flops 20000000000 | tf_op jit(solution)/shard_map/corners/pallas_call | solution.py:589
  29.4 2.3 %collective-permute-start.4 = (f32[80,128]{1,0:T(8,128)S(1)}, f32[80,128]{1,0:T(8,128)S(1)}, u32[]{:S(2)}, u32[]{:S(2)}) collective-permute-start(f32[80,128]{1,0:T(8,128)S(1)} %get-tuple-element.16), channel_id=1, source_target_pairs={{0,8},{8,16},{16,24},{24,32},{32,40},{40,48},{48,56},{56,64},{64,7... | collective-permute-start | bytes 122888 | tf_op jit(solution)/shard_map/ppermute | solution.py:566
  31.8 2.0 %collective-permute-start.5 = (f32[80,128]{1,0:T(8,128)S(1)}, f32[80,128]{1,0:T(8,128)S(1)}, u32[]{:S(2)}, u32[]{:S(2)}) collective-permute-start(f32[80,128]{1,0:T(8,128)S(1)} %get-tuple-element.17), channel_id=1, source_target_pairs={{8,0},{16,8},{24,16},{32,24},{40,32},{48,40},{56,48},{64,56},{72,6... | collective-permute-start | bytes 122888 | tf_op jit(solution)/shard_map/ppermute | solution.py:566
  33.8 4.1 %collective-permute-done.4.low_any = f32[80,128]{1,0:T(8,128)S(1)} collective-permute-done((f32[80,128]{1,0:T(8,128)S(1)}, f32[80,128]{1,0:T(8,128)S(1)}, u32[]{:S(2)}, u32[]{:S(2)}) %collective-permute-start.4) | collective-permute-done | bytes 40992 | tf_op jit(solution)/shard_map/ppermute | solution.py:566
  37.9 0.6 collective-permute-done.5.high_any
  38.5 0.0 collective-permute-done.1.above_any
  38.5 0.0 collective-permute-done.below_any
  38.5 1.5 %all-to-all-done = f32[1920,1,128]{2,1,0:T(1,128)} async-done(((f32[1920,1,128]{2,1,0:T(1,128)}), f32[1920,1,128]{2,1,0:T(1,128)}, u32[]{:S(2)}, u32[]{:S(2)}) %all-to-all-start) | async-done | bytes 983072 | tf_op jit(solution)/shard_map/all_to_all | solution.py:572
  40.0 0.0 copy-done
  40.0 0.0 copy-done.1
  40.0 0.0 copy-done.2
  40.0 0.0 copy-done.3
  40.0 5.2 %evolve.1 = (f32[3,16,32,128]{3,2,1,0:T(8,128)}, f32[512,128]{1,0:T(8,128)S(1)}) custom-call(f32[3,16,32,128]{3,2,1,0:T(8,128)S(1)} %copy-done, f32[3,16,32,128]{3,2,1,0:T(8,128)S(1)} %copy-done.1, f32[3,16,32,128]{3,2,1,0:T(8,128)S(1)} %copy-done.2, f32[3,16,32,128]{3,2,1,0:T(8,128)} %ha.3, f32[16,32,128]{2,1,0:T(8,128)S(1)} %copy-done.3, ...), custom_call_target="tpu_custom_call" | custom-call | flops 8000000000 | tf_op jit(solution)/shard_map/evolve/pallas_call | solution.py:505
  45.2 0.0 copy-start.4
  45.2 21.8 %all_to_all.10 = f32[128,4,128]{2,1,0:T(4,128)S(1)} all-to-all(f32[128,4,128]{2,1,0:T(4,128)S(1)} %bitcast.9), channel_id=1, replica_groups=mesh['gx'=16,'gy'=8] {'gx','gy'}, dimensions={0} | all-to-all | bytes 524288 | tf_op jit(solution)/shard_map/all_to_all | solution.py:572
  67.1 0.0 copy-done.4
  67.1 1.4 %unpack_tiles.1 = f32[128,256]{1,0:T(8,128)} custom-call(f32[512,128]{1,0:T(8,128)S(1)} %bitcast.10, f32[128,384]{1,0:T(8,128)S(1)} %copy-done.4), custom_call_target="tpu_custom_call" | custom-call | flops 2000000000 | tf_op jit(solution)/shard_map/unpack_tiles/pallas_call | solution.py:553
Async XLA Ops:
  4.2 24.3 %collective-permute-start.2 = (f32[368,128]{1,0:T(8,128)}, f32[368,128]{1,0:T(8,128)S(1)}, u32[]{:S(2)}, u32[]{:S(2)}) collective-permute-start(f32[368,128]{1,0:T(8,128)} %get-tuple-element.14), channel_id=1, source_target_pairs={{0,1},{1,2},{2,3},{3,4},{4,5},{5,6},{6,7},{8,9},{9,10},{10,11},{11... | collective-permute-start | bytes 565256 | tf_op jit(solution)/shard_map/ppermute | solution.py:566
  8.6 19.9 %collective-permute-start.3 = (f32[272,128]{1,0:T(8,128)}, f32[272,128]{1,0:T(8,128)}, u32[]{:S(2)}, u32[]{:S(2)}) collective-permute-start(f32[272,128]{1,0:T(8,128)} %get-tuple-element.15), channel_id=1, source_target_pairs={{1,0},{2,1},{3,2},{4,3},{5,4},{6,5},{7,6},{9,8},{10,9},{11,10},{12... | collective-permute-start | bytes 417800 | tf_op jit(solution)/shard_map/ppermute | solution.py:566
  9.9 30.1 %all-to-all-start = ((f32[1920,1,128]{2,1,0:T(1,128)}), f32[1920,1,128]{2,1,0:T(1,128)}, u32[]{:S(2)}, u32[]{:S(2)}) async-start(f32[1920,1,128]{2,1,0:T(1,128)} %bitcast.11), calls=%async_computation | async-start | bytes 1966080 | tf_op jit(solution)/shard_map/all_to_all | solution.py:572
  22.7 15.8 %collective-permute-start.1 = (f32[17,32,128]{2,1,0:T(8,128)}, f32[17,32,128]{2,1,0:T(8,128)S(1)}, u32[]{:S(2)}, u32[]{:S(2)}) collective-permute-start(f32[17,32,128]{2,1,0:T(8,128)} %get-tuple-element.13), channel_id=1, source_target_pairs={{8,0},{16,8},{24,16},{32,24},{40,32},{48,40},{56,48},{64,56},{72,6... | collective-permute-start | bytes 835592 | tf_op jit(solution)/shard_map/ppermute | solution.py:566
  25.8 14.2 %copy-start = (f32[3,16,32,128]{3,2,1,0:T(8,128)S(1)}, f32[3,16,32,128]{3,2,1,0:T(8,128)}, u32[]{:S(2)}) copy-start(f32[3,16,32,128]{3,2,1,0:T(8,128)} %ef.3) | copy-start | bytes 2359300
  25.8 14.2 %copy-start.1 = (f32[3,16,32,128]{3,2,1,0:T(8,128)S(1)}, f32[3,16,32,128]{3,2,1,0:T(8,128)}, u32[]{:S(2)}) copy-start(f32[3,16,32,128]{3,2,1,0:T(8,128)} %hf.3) | copy-start | bytes 2359300
  25.8 14.2 %copy-start.2 = (f32[3,16,32,128]{3,2,1,0:T(8,128)S(1)}, f32[3,16,32,128]{3,2,1,0:T(8,128)}, u32[]{:S(2)}) copy-start(f32[3,16,32,128]{3,2,1,0:T(8,128)} %ea.3) | copy-start | bytes 2359300
  25.8 14.2 %copy-start.3 = (f32[16,32,128]{2,1,0:T(8,128)S(1)}, f32[16,32,128]{2,1,0:T(8,128)}, u32[]{:S(2)}) copy-start(f32[16,32,128]{2,1,0:T(8,128)} %perm.3) | copy-start | bytes 786436
  25.8 12.7 %collective-permute-start = (f32[23,32,128]{2,1,0:T(8,128)}, f32[23,32,128]{2,1,0:T(8,128)S(1)}, u32[]{:S(2)}, u32[]{:S(2)}) collective-permute-start(f32[23,32,128]{2,1,0:T(8,128)} %get-tuple-element.12), channel_id=1, source_target_pairs={{0,8},{8,16},{16,24},{24,32},{32,40},{40,48},{48,56},{56,64},{64,7... | collective-permute-start | bytes 1130504 | tf_op jit(solution)/shard_map/ppermute | solution.py:566
  29.4 8.5 %collective-permute-start.4 = (f32[80,128]{1,0:T(8,128)S(1)}, f32[80,128]{1,0:T(8,128)S(1)}, u32[]{:S(2)}, u32[]{:S(2)}) collective-permute-start(f32[80,128]{1,0:T(8,128)S(1)} %get-tuple-element.16), channel_id=1, source_target_pairs={{0,8},{8,16},{16,24},{24,32},{32,40},{40,48},{48,56},{56,64},{64,7... | collective-permute-start | bytes 122888 | tf_op jit(solution)/shard_map/ppermute | solution.py:566
  31.8 6.7 %collective-permute-start.5 = (f32[80,128]{1,0:T(8,128)S(1)}, f32[80,128]{1,0:T(8,128)S(1)}, u32[]{:S(2)}, u32[]{:S(2)}) collective-permute-start(f32[80,128]{1,0:T(8,128)S(1)} %get-tuple-element.17), channel_id=1, source_target_pairs={{8,0},{16,8},{24,16},{32,24},{40,32},{48,40},{56,48},{64,56},{72,6... | collective-permute-start | bytes 122888 | tf_op jit(solution)/shard_map/ppermute | solution.py:566
  45.2 21.9 %copy-start.4 = (f32[128,384]{1,0:T(8,128)S(1)}, f32[128,384]{1,0:T(8,128)}, u32[]{:S(2)}) copy-start(f32[128,384]{1,0:T(8,128)} %get-tuple-element.21.match) | copy-start | bytes 589828

commit v3 on v2

--- a/solution.py
+++ b/solution.py
@@ -21,6 +21,10 @@
 EX, EY = 20, 40
 UP_ROWS = 23
 DOWN_ROWS = 17
+UP_X = 17
+DOWN_X = 11
+BESIDE = (EY - 1, NY, EY - 2)
+TALL = NY + len(BESIDE)
 ROWS = 15
 
 
@@ -62,12 +66,6 @@
         preferred_element_type=F32,
     )
     return found[:, :width] + found[:, width:]
-
-
-def plan(to_next):
-    if to_next:
-        return [(0, 0, -2, 2), (0, 1, -2, 2), (0, 2, -2, 2), (1, 0, -1, 1), (1, 1, -2, 2), (1, 2, -2, 2)]
-    return [(0, 0, 0, 1), (0, 1, 0, 2), (0, 2, 0, 2), (1, 0, 0, 1), (1, 1, 0, 1), (1, 2, 0, 1)]
 
 
 def plan_y(to_next):
@@ -158,8 +156,8 @@
 
 def prepare_all(
     ef, hf, ea, ha, perm, pattern_hbm, owner_hbm, count_hbm, start_hbm,
-    up_x, down_x, up_y, down_y, message, match,
-    first, last, first_perm, last_perm, first_x, last_x, first_x_perm, last_x_perm,
+    first_x, last_x, first_x_perm, last_x_perm, up_y, down_y, message, match,
+    first, last, first_perm, last_perm,
     pattern, owner, count, start, sems,
 ):
     small = [(owner_hbm, owner), (count_hbm, count), (start_hbm, start), (pattern_hbm, pattern)]
@@ -194,17 +192,6 @@
                     out[pl.ds(at * NX, NX), :] = flat[pl.ds(row, NX, stride=8), :]
                     at += 1
         out[pl.ds(at * NX, NX), :] = flat_perm[pl.ds(7 if to_next else 0, NX, stride=8), :]
-    for to_next, src, src_perm, out in (
-        (True, last_x, last_x_perm, up_x),
-        (False, first_x, first_x_perm, down_x),
-    ):
-        at = 0
-        for evolution in range(2):
-            for field, comp, begin, planes in plan(to_next):
-                for k in range(planes):
-                    out[at] = src[field * 6 + evolution * 3 + comp, (begin + k) % 2]
-                    at += 1
-        out[at] = src_perm[1 if to_next else 0]
 
 
 def prepare(ef, hf, ea, ha, perm, pattern, owners, tile_count, tile_start):
@@ -212,24 +199,22 @@
     return pl.pallas_call(
         prepare_all,
         out_shape=(
-            shape(UP_ROWS, NY, LANES),
-            shape(DOWN_ROWS, NY, LANES),
+            shape(12, 2, NY, LANES),
+            shape(12, 2, NY, LANES),
+            shape(2, NY, LANES),
+            shape(2, NY, LANES),
             shape(UP_ROWS * NX, LANES),
             shape(DOWN_ROWS * NX, LANES),
             shape(tiles * ROWS, LANES),
             shape(tiles, 3 * tiles),
         ),
         in_specs=[hbm()] * 9,
-        out_specs=(vmem(),) * 6,
+        out_specs=(vmem(),) * 8,
         scratch_shapes=[
             pltpu.VMEM((12, NX, 8, LANES), F32),
             pltpu.VMEM((12, NX, 8, LANES), F32),
             pltpu.VMEM((NX, 8, LANES), F32),
             pltpu.VMEM((NX, 8, LANES), F32),
-            pltpu.VMEM((12, 2, NY, LANES), F32),
-            pltpu.VMEM((12, 2, NY, LANES), F32),
-            pltpu.VMEM((2, NY, LANES), F32),
-            pltpu.VMEM((2, NY, LANES), F32),
             pltpu.VMEM((tiles, 2 * LANES), F32),
             pltpu.VMEM((1, tiles), jnp.int32),
             pltpu.VMEM((1, tiles), jnp.int32),
@@ -282,28 +267,19 @@
 
 
 def evolve(
-    ef, hf, ea, ha, perm, below_any, above_any, before_any, after_any, low_any, high_any, message_any,
+    ef, hf, ea, ha, perm, below, above, before, after, message,
     final, reply,
-    final_v, forward, adjoint, perm_wide, rate, grow, turned, overlap, below, above, before, after, low, high, message, sems,
+    final_v, forward, adjoint, perm_wide, rate, grow, turned, overlap, sems,
 ):
     wide = (forward, adjoint)
-    pairs = [
-        (message_any, message),
-        (below_any, below),
-        (above_any, above),
-        (before_any, before),
-        (after_any, after),
-        (low_any, low),
-        (high_any, high),
-    ]
+    pairs = []
     pairs.append((perm, perm_wide.at[pl.ds(2, NX), pl.ds(0, NY)]))
     for i, src in ((0, ef), (1, hf), (2, ea), (3, ha)):
         pairs.append((src, wide[i // 2].at[pl.ds(3 * (i % 2), 3), pl.ds(2, NX), pl.ds(0, NY)]))
     copies = [pltpu.make_async_copy(a, b, sems.at[i]) for i, (a, b) in enumerate(pairs)]
     for copy in copies:
         copy.start()
-    final_copy = pltpu.make_async_copy(final_v, final, sems.at[12])
-    copies[0].wait()
+    final_copy = pltpu.make_async_copy(final_v, final, sems.at[5])
     tiles = message.shape[0] // ROWS
     square = (tiles, LANES)
     across = iota(square, 1)
@@ -392,53 +368,54 @@
     within = (y < NY) | ((y == NY) & high_y) | ((y == EY - 1) & low_y)
 
 
-    for copy in copies[1:8]:
-        copy.wait()
+    copies[0].wait()
     flat_perm = perm_wide.reshape(EX * EY, LANES)
-    for from_prev, beside, along, corner in ((True, before, below, low), (False, after, above, high)):
+    for from_prev, beside, along in ((True, before, below), (False, after, above)):
         row = EY - 1 if from_prev else NY
         flat_perm[pl.ds(2 * EY + row, NX, stride=EY), :] = beside[pl.ds(beside.shape[0] - NX, NX), :]
-        perm_wide[1 if from_prev else NX + 2, :NY, :] = along[along.shape[0] - 1]
-        for x in range(2):
-            for other_row, at in ((EY - 1, (x + 1) * UP_ROWS - 1), (NY, 2 * UP_ROWS + (x + 1) * DOWN_ROWS - 1)):
-                place = (0 if from_prev else NX + 2) + x
-                perm_wide[place, other_row : other_row + 1, :] = corner[pl.ds(at, 1), :]
+
+    def take_plane(src, planes, at, dest):
+        dest[:NY, :] = src[at * NY : (at + 1) * NY]
+        for k, row in enumerate(BESIDE):
+            dest[row : row + 1, :] = src[planes * NY + 3 * at + k : planes * NY + 3 * at + k + 1]
+
+    take_plane(below, UP_X, UP_X - 1, perm_wide.at[1])
+    take_plane(above, DOWN_X, DOWN_X - 1, perm_wide.at[NX + 2])
 
     def fill_halo(evolution):
-        fields = wide[evolution]
+        fields, h = wide[evolution], 6 + 3 * evolution
         flat = fields.reshape(6 * EX * EY, LANES)
-        for from_prev, beside, along in ((True, before, below), (False, after, above)):
+        for from_prev, beside in ((True, before), (False, after)):
             at = evolution * (beside.shape[0] // NX // 2)
             for field, comp, begin, count in plan_y(from_prev):
                 for k in range(count):
                     row = EY + begin + k if from_prev else NY + begin + k
                     c = field * 3 + comp
                     flat[pl.ds((c * EX + 2) * EY + row, NX, stride=EY), :] = beside[pl.ds(at * NX, NX), :]
-                    for corner, place in ((low, 0), (high, NX + 2)):
-                        planes, start = (UP_ROWS, 0) if from_prev else (DOWN_ROWS, 2 * UP_ROWS)
-                        for x in range(2):
-                            fields[c, place + x, row : row + 1, :] = corner[pl.ds(start + at + x * planes, 1), :]
                     at += 1
-            at = evolution * (along.shape[0] // 2)
-            for field, comp, begin, count in plan(from_prev):
-                for k in range(count):
-                    place = begin + k + 2 if from_prev else NX + 2 + begin + k
-                    fields[field * 3 + comp, place, :NY, :] = along[at]
-                    at += 1
+        places = [(fields, c, 1) for c in range(3)] + [(turned, h + c, 1) for c in range(3)]
+        places += [(turned, h + c, 0) for c in (1, 2)]
+        for i, (ref, c, x) in enumerate(places):
+            take_plane(below, UP_X, 8 * evolution + i, ref.at[c, x])
+        places = [(fields, c, NX + 2) for c in (1, 2)] + [(turned, h + c, NX + 2) for c in range(3)]
+        for i, (ref, c, x) in enumerate(places):
+            take_plane(above, DOWN_X, 5 * evolution + i, ref.at[c, x])
 
     cut = jnp.where((y < EY - 2) | low_y, COURANT, 0.0)
 
     for evolution in range(2):
         e, fields = 3 * evolution, wide[evolution]
-        for copy in copies[8 + 2 * evolution : 10 + 2 * evolution]:
+        for copy in copies[1 + 2 * evolution : 3 + 2 * evolution]:
             copy.wait()
         fill_halo(evolution)
-        for x in range(NX + 3):
-            factor = cut if x >= 2 else jnp.where(low_x, cut, 0.0)
+        edge_cut = jnp.where(low_x, cut, 0.0)
+        turned[7 + e, 1] = turned[7 + e, 1] + edge_cut * fields[2, 2]
+        turned[8 + e, 1] = turned[8 + e, 1] - edge_cut * fields[1, 2]
+        for x in range(2, NX + 2):
             here = [fields[c, x] for c in range(3)]
             curl = curl_e(here, [fields[c, x + 1] for c in (1, 2)])
             for c in range(3):
-                turned[6 + e + c, x] = fields[3 + c, x] - factor * curl[c]
+                turned[6 + e + c, x] = fields[3 + c, x] - cut * curl[c]
         for x in range(1, NX + 3):
             if e:
                 scale = rate[x]
@@ -453,7 +430,7 @@
                 rate[x] = scale
             here = [turned[6 + e + c, x] for c in range(3)]
             curl = curl_h(here, [turned[6 + e + c, x - 1] for c in (1, 2)])
-            for c in range(3):
+            for c in range(1 if x == NX + 2 else 0, 3):
                 turned[e + c, x] = fields[c, x] + scale * curl[c]
     for x in range(1, NX + 2):
         factor = cut if x >= 2 else jnp.where(low_x, cut, 0.0)
@@ -500,12 +477,12 @@
     final_copy.wait()
 
 
-def run_fields(ef, hf, ea, ha, perm, below, above, before, after, low, high, message):
+def run_fields(ef, hf, ea, ha, perm, below, above, before, after, message):
     tiles = message.shape[0] // ROWS
     return pl.pallas_call(
         evolve,
         out_shape=(shape(3, NX, NY, LANES), shape(tiles * 4, LANES)),
-        in_specs=[hbm()] * 5 + [anywhere()] * 7,
+        in_specs=[hbm()] * 5 + [vmem()] * 5,
         out_specs=(hbm(), vmem()),
         scratch_shapes=[
             pltpu.VMEM((3, NX, NY, LANES), F32),
@@ -516,19 +493,12 @@
             pltpu.VMEM((EX * EY, LANES), F32),
             pltpu.VMEM((12, EX, EY, LANES), F32),
             pltpu.VMEM((NX * NY, LANES), F32),
-            pltpu.VMEM(below.shape, F32),
-            pltpu.VMEM(above.shape, F32),
-            pltpu.VMEM(before.shape, F32),
-            pltpu.VMEM(after.shape, F32),
-            pltpu.VMEM(low.shape, F32),
-            pltpu.VMEM(high.shape, F32),
-            pltpu.VMEM(message.shape, F32),
-            pltpu.SemaphoreType.DMA((13,)),
+            pltpu.SemaphoreType.DMA((6,)),
         ],
-        compiler_params=params(50),
+        compiler_params=params(51),
         cost_estimate=cost(8),
         name="evolve",
-    )(ef, hf, ea, ha, perm, below, above, before, after, low, high, message)
+    )(ef, hf, ea, ha, perm, below, above, before, after, message)
 
 
 def unpack_tiles(reply, match, out):
@@ -575,39 +545,76 @@
     return out.reshape(block.shape)
 
 
-def corner_rows(before, after, low, high):
-    for out, first in ((low, NX - 2), (high, 0)):
+def faces_x(first_x, last_x, first_perm, last_perm, before, after, up, down, tiles):
+    places = (NX - 2, NX - 1, 0, 1)
+    for from_prev, src in ((True, before), (False, after)):
         at = 0
-        for src, planes in ((before, UP_ROWS), (after, DOWN_ROWS)):
-            for x in range(2):
-                out[pl.ds(at, planes), :] = src[pl.ds(first + x, planes, stride=NX), :]
-                at += planes
-
-
-def corners(before, after):
-    rows = 2 * (UP_ROWS + DOWN_ROWS)
+        for evolution in range(2):
+            for field, comp, begin, count in plan_y(from_prev):
+                for k in range(count):
+                    row = 8 + begin + k if from_prev else begin + k
+                    for i, x in enumerate(places):
+                        tiles[field * 6 + evolution * 3 + comp, i, row : row + 1, :] = src[
+                            pl.ds(at * NX + x, 1), :
+                        ]
+                    at += 1
+
+    def plane(c, i):
+        block = last_x[c, i] if i < 2 else first_x[c, i - 2]
+        return jnp.concatenate([block, tiles[c, i]], axis=0)
+
+    def send(out, planes, at, values):
+        out[at * NY : (at + 1) * NY] = values[:NY]
+        for k, row in enumerate(BESIDE):
+            out[planes * NY + 3 * at + k : planes * NY + 3 * at + k + 1] = values[row : row + 1]
+
+    inside_y = lax.axis_index("gy") > 0
+    rate = jnp.where((iota((EY, LANES), 0) < EY - 2) | inside_y, COURANT, 0.0)
+    nothing = jnp.zeros((EY, LANES), F32)
+    for evolution in range(2):
+        e, h = 3 * evolution, 6 + 3 * evolution
+        before_last, last, first, second = [[plane(e + c, i) for c in range(3)] for i in range(4)]
+        curl = curl_e(before_last, last[1:])
+        inner = [plane(h + c, 0) - rate * curl[c] for c in (1, 2)]
+        curl = curl_e(last, [nothing, nothing])
+        outer = [plane(h + c, 1) - rate * curl[c] for c in range(3)]
+        for i, values in enumerate(last + outer + inner):
+            send(up, UP_X, 8 * evolution + i, values)
+        curl = curl_e(first, second[1:])
+        outer = [plane(h + c, 2) - rate * curl[c] for c in range(3)]
+        for i, values in enumerate(first[1:] + outer):
+            send(down, DOWN_X, 5 * evolution + i, values)
+    for out, planes, block, x in ((up, UP_X, last_perm[1], NX - 1), (down, DOWN_X, first_perm[0], 0)):
+        at = planes - 1
+        out[at * NY : (at + 1) * NY] = block
+        for k, (src, rows) in enumerate(((before, UP_ROWS), (after, DOWN_ROWS))):
+            out[planes * NY + 3 * at + k : planes * NY + 3 * at + k + 1] = src[pl.ds((rows - 1) * NX + x, 1), :]
+        out[planes * TALL - 1 :] = jnp.zeros((1, LANES), F32)
+
+
+def send_x(first_x, last_x, first_perm, last_perm, before, after):
     return pl.pallas_call(
-        corner_rows,
-        out_shape=(shape(rows, LANES), shape(rows, LANES)),
-        in_specs=[vmem()] * 2,
+        faces_x,
+        out_shape=(shape(UP_X * TALL, LANES), shape(DOWN_X * TALL, LANES)),
+        in_specs=[vmem()] * 6,
         out_specs=(vmem(), vmem()),
-        compiler_params=params(16),
+        scratch_shapes=[pltpu.VMEM((12, 4, 8, LANES), F32)],
+        compiler_params=params(50),
         cost_estimate=cost(20),
-        name="corners",
-    )(before, after)
+        name="faces_x",
+    )(first_x, last_x, first_perm, last_perm, before, after)
 
 
 def shards(ef, hf, ea, ha, perm, pattern, owners, tile_count, tile_start):
-    up_x, down_x, up_y, down_y, message, match = prepare(
+    *edges, up_y, down_y, message, match = prepare(
         ef, hf, ea, ha, perm, pattern, owners, tile_count, tile_start
     )
     arrived = exchange(message, 1)
     before, after = passed(up_y, "gy", 1), passed(down_y, "gy", -1)
+    up_x, down_x = send_x(*edges, before, after)
     below, above = passed(up_x, "gx", 1), passed(down_x, "gx", -1)
-    low, high = corners(before, after)
-    low, high = passed(low, "gx", 1), passed(high, "gx", -1)
     final, reply = run_fields(
-        ef, hf, ea, ha, perm, below, above, before, after, low, high, arrived
+        ef, hf, ea, ha, perm, below, above, before, after, arrived
     )
     return final, unpack(exchange(reply, 4), match)
 

time: 68.8 us -> 64.5 us (0.938)
  waiting for transfers between devices: 6.24 us -> 11.4 us
  blocking collectives: 21.8 us -> 17.4 us
  starting transfers between devices: 28.5 us -> 24.1 us
    all_to_all x1, blocking collectives: 21.8 us -> 17.4 us  [exchange(): lax.all_to_all(block.reshape(-1, depth, LANES), ('gx', 'gy'), split_axis=...]
    ppermute x6 -> x4, starting transfers between devices: 15.7 us -> 11.3 us  [passed(): lax.ppermute(block, axis, [(i, i + distance) for i in devices if i + dist...]
    ppermute x6 -> x4, waiting for transfers between devices: 4.73 us -> 8.91 us  [passed(): lax.ppermute(block, axis, [(i, i + distance) for i in devices if i + dist...]
    all_to_all x1, waiting for transfers between devices: 1.51 us -> 2.52 us  [exchange(): lax.all_to_all(block.reshape(-1, depth, LANES), ('gx', 'gy'), split_axis=...]
    pallas_call x2, Pallas kernels: 4.52 us -> 3.8 us  [the longest x1 3.65 us: prepare(): pl.pallas_call(prepare_all, out_shape=(shape(12, 2, NY, LANES), shape(12,...]
  transfers between devices with their start and end apart: 7 -> 5, of which waited for: 3 -> 2; matrix products, arithmetic and copies ran while one was open for 0% -> 0% of each run, Pallas kernels for 1% -> 0%
where the time goes in v3:
time: 64.5 us; the launch traced here: 64.2 us
  starting transfers between devices  24.1 us (37%)
  blocking collectives  17.4 us (27%)
  waiting for transfers between devices  11.4 us (18%)
  Pallas kernels  10.5 us (16%)
  between operations  0.8 us (1%)
    all_to_all x1, blocking collectives, exchange(): lax.all_to_all(block.reshape(-1, depth, LANES), ('gx', 'gy'), split_axis=...  17.4 us
    all_to_all x1, starting transfers between devices, exchange(): lax.all_to_all(block.reshape(-1, depth, LANES), ('gx', 'gy'), split_axis=...  12.8 us
    ppermute x4, starting transfers between devices, passed(): lax.ppermute(block, axis, [(i, i + distance) for i in devices if i + dist...  11.3 us
    ppermute x4, waiting for transfers between devices, passed(): lax.ppermute(block, axis, [(i, i + distance) for i in devices if i + dist...  8.91 us
    pallas_call x1, Pallas kernels, run_fields(): pl.pallas_call(evolve, out_shape=(shape(3, NX, NY, LANES), shape(tiles *...  5.31 us
    pallas_call x1, Pallas kernels, prepare(): pl.pallas_call(prepare_all, out_shape=(shape(12, 2, NY, LANES), shape(12,...  3.65 us
    all_to_all x1, waiting for transfers between devices, exchange(): lax.all_to_all(block.reshape(-1, depth, LANES), ('gx', 'gy'), split_axis=...  2.52 us
    pallas_call x1, Pallas kernels, unpack(): pl.pallas_call(unpack_tiles, out_shape=shape(tiles, 2 * LANES), in_specs=...  1.36 us
  transfers between devices with their start and end apart: 5, of which 2 were waited for; matrix products, arithmetic and copies ran while one was open for 0% of the time, Pallas kernels for 0%

profile of v3, /device:TPU:1, one launch (start us, length us, event | category | flops | bytes accessed | tf_op | source)
XLA Modules:
  0.0 64.2 jit_solution(5069069602599898051)
XLA Ops:
  0.6 3.6 %prepare.1 = (f32[12,2,32,128]{3,2,1,0:T(8,128)}, f32[12,2,32,128]{3,2,1,0:T(8,128)}, f32[2,32,128]{2,1,0:T(8,128)}, f32[2,32,128]{2,1,0:T(8,128)}, f32[368,128]...) custom-call(f32[3,16,32,128]{3,2,1,0:T(8,128)} %ef.3, f32[3,16,32,128]{3,2,1,0:T(8,128)} %hf.3, ...), custom_call_target="tpu_custom_call" | custom-call | flops 3000000000 | tf_op jit(solution)/shard_map/prepare/pallas_call | solution.py:199
  4.3 4.4 %collective-permute-start = (f32[368,128]{1,0:T(8,128)}, f32[368,128]{1,0:T(8,128)S(1)}, u32[]{:S(2)}, u32[]{:S(2)}) collective-permute-start(f32[368,128]{1,0:T(8,128)} %get-tuple-element.18), channel_id=1, source_target_pairs={{0,1},{1,2},{2,3},{3,4},{4,5},{5,6},{6,7},{8,9},{9,10},{10,11},{11... | collective-permute-start | bytes 565256 | tf_op jit(solution)/shard_map/ppermute | solution.py:536
  8.7 1.3 %collective-permute-start.1 = (f32[272,128]{1,0:T(8,128)}, f32[272,128]{1,0:T(8,128)S(1)}, u32[]{:S(2)}, u32[]{:S(2)}) collective-permute-start(f32[272,128]{1,0:T(8,128)} %get-tuple-element.19), channel_id=1, source_target_pairs={{1,0},{2,1},{3,2},{4,3},{5,4},{6,5},{7,6},{9,8},{10,9},{11,10},{12... | collective-permute-start | bytes 417800 | tf_op jit(solution)/shard_map/ppermute | solution.py:536
  10.0 0.0 copy-start.3
  10.0 0.0 copy-start.4
  10.0 0.0 copy-start.6
  10.0 0.0 copy-start.7
  10.0 12.8 %all-to-all-start = ((f32[1920,1,128]{2,1,0:T(1,128)}), f32[1920,1,128]{2,1,0:T(1,128)}, u32[]{:S(2)}, u32[]{:S(2)}) async-start(f32[1920,1,128]{2,1,0:T(1,128)} %bitcast.11), calls=%async_computation | async-start | bytes 1966080 | tf_op jit(solution)/shard_map/all_to_all | solution.py:542
  22.8 0.0 collective-permute-done.1.after
  22.8 0.0 collective-permute-done.before
  22.9 0.0 copy-done.3
  22.9 0.0 copy-done.4
  22.9 0.0 copy-done.6
  22.9 0.0 copy-done.7
  22.9 0.0 copy-start
  22.9 0.0 copy-start.1
  22.9 0.0 copy-start.2
  22.9 0.2 faces_x.1
  23.1 3.7 %collective-permute-start.2 = (f32[595,128]{1,0:T(8,128)S(1)}, f32[595,128]{1,0:T(8,128)S(1)}, u32[]{:S(2)}, u32[]{:S(2)}) collective-permute-start(f32[595,128]{1,0:T(8,128)S(1)} %get-tuple-element.20), channel_id=1, source_target_pairs={{0,8},{8,16},{16,24},{24,32},{32,40},{40,48},{48,56},{56,64},{64,7... | collective-permute-start | bytes 913928 | tf_op jit(solution)/shard_map/ppermute | solution.py:536
  26.8 1.9 %collective-permute-start.3 = (f32[385,128]{1,0:T(8,128)S(1)}, f32[385,128]{1,0:T(8,128)S(1)}, u32[]{:S(2)}, u32[]{:S(2)}) collective-permute-start(f32[385,128]{1,0:T(8,128)S(1)} %get-tuple-element.21), channel_id=1, source_target_pairs={{8,0},{16,8},{24,16},{32,24},{40,32},{48,40},{56,48},{64,56},{72,6... | collective-permute-start | bytes 591368 | tf_op jit(solution)/shard_map/ppermute | solution.py:536
  28.7 8.9 %collective-permute-done.3.above = f32[385,128]{1,0:T(8,128)S(1)} collective-permute-done((f32[385,128]{1,0:T(8,128)S(1)}, f32[385,128]{1,0:T(8,128)S(1)}, u32[]{:S(2)}, u32[]{:S(2)}) %collective-permute-start.3) | collective-permute-done | bytes 197152 | tf_op jit(solution)/shard_map/ppermute | solution.py:536
  37.6 0.0 collective-permute-done.2.below
  37.6 2.5 %all-to-all-done = f32[1920,1,128]{2,1,0:T(1,128)} async-done(((f32[1920,1,128]{2,1,0:T(1,128)}), f32[1920,1,128]{2,1,0:T(1,128)}, u32[]{:S(2)}, u32[]{:S(2)}) %all-to-all-start) | async-done | bytes 983072 | tf_op jit(solution)/shard_map/all_to_all | solution.py:542
  40.1 0.0 copy-done
  40.1 0.0 copy-done.1
  40.1 0.0 copy-done.2
  40.1 5.3 %evolve.1 = (f32[3,16,32,128]{3,2,1,0:T(8,128)}, f32[512,128]{1,0:T(8,128)S(1)}) custom-call(f32[3,16,32,128]{3,2,1,0:T(8,128)S(1)} %copy-done, f32[3,16,32,128]{3,2,1,0:T(8,128)S(1)} %copy-done.1, f32[3,16,32,128]{3,2,1,0:T(8,128)} %ea.3, f32[3,16,32,128]{3,2,1,0:T(8,128)} %ha.3, f32[16,32,128]{2,1,0:T(8,128)S(1)} %copy-done.2, ...), custom_call_target="tpu_custom_call" | custom-call | flops 8000000000 | tf_op jit(solution)/shard_map/evolve/pallas_call | solution.py:482
  45.5 0.0 copy-start.5
  45.5 17.4 %all_to_all.10 = f32[128,4,128]{2,1,0:T(4,128)S(1)} all-to-all(f32[128,4,128]{2,1,0:T(4,128)S(1)} %bitcast.9), channel_id=1, replica_groups=mesh['gx'=16,'gy'=8] {'gx','gy'}, dimensions={0} | all-to-all | bytes 524288 | tf_op jit(solution)/shard_map/all_to_all | solution.py:542
  62.8 0.0 copy-done.5
  62.8 1.4 %unpack_tiles.1 = f32[128,256]{1,0:T(8,128)} custom-call(f32[512,128]{1,0:T(8,128)S(1)} %bitcast.10, f32[128,384]{1,0:T(8,128)S(1)} %copy-done.5), custom_call_target="tpu_custom_call" | custom-call | flops 2000000000 | tf_op jit(solution)/shard_map/unpack_tiles/pallas_call | solution.py:523
Async XLA Ops:
  4.3 18.6 %collective-permute-start = (f32[368,128]{1,0:T(8,128)}, f32[368,128]{1,0:T(8,128)S(1)}, u32[]{:S(2)}, u32[]{:S(2)}) collective-permute-start(f32[368,128]{1,0:T(8,128)} %get-tuple-element.18), channel_id=1, source_target_pairs={{0,1},{1,2},{2,3},{3,4},{4,5},{5,6},{6,7},{8,9},{9,10},{10,11},{11... | collective-permute-start | bytes 565256 | tf_op jit(solution)/shard_map/ppermute | solution.py:536
  8.7 14.2 %collective-permute-start.1 = (f32[272,128]{1,0:T(8,128)}, f32[272,128]{1,0:T(8,128)S(1)}, u32[]{:S(2)}, u32[]{:S(2)}) collective-permute-start(f32[272,128]{1,0:T(8,128)} %get-tuple-element.19), channel_id=1, source_target_pairs={{1,0},{2,1},{3,2},{4,3},{5,4},{6,5},{7,6},{9,8},{10,9},{11,10},{12... | collective-permute-start | bytes 417800 | tf_op jit(solution)/shard_map/ppermute | solution.py:536
  10.0 12.9 %copy-start.3 = (f32[12,2,32,128]{3,2,1,0:T(8,128)S(1)}, f32[12,2,32,128]{3,2,1,0:T(8,128)}, u32[]{:S(2)}) copy-start(f32[12,2,32,128]{3,2,1,0:T(8,128)} %get-tuple-element.14.first_x) | copy-start | bytes 1179652
  10.0 12.9 %copy-start.4 = (f32[12,2,32,128]{3,2,1,0:T(8,128)S(1)}, f32[12,2,32,128]{3,2,1,0:T(8,128)}, u32[]{:S(2)}) copy-start(f32[12,2,32,128]{3,2,1,0:T(8,128)} %get-tuple-element.15.last_x) | copy-start | bytes 1179652
  10.0 12.9 %copy-start.6 = (f32[2,32,128]{2,1,0:T(8,128)S(1)}, f32[2,32,128]{2,1,0:T(8,128)}, u32[]{:S(2)}) copy-start(f32[2,32,128]{2,1,0:T(8,128)} %get-tuple-element.16.first_perm) | copy-start | bytes 98308
  10.0 12.9 %copy-start.7 = (f32[2,32,128]{2,1,0:T(8,128)S(1)}, f32[2,32,128]{2,1,0:T(8,128)}, u32[]{:S(2)}) copy-start(f32[2,32,128]{2,1,0:T(8,128)} %get-tuple-element.17.last_perm) | copy-start | bytes 98308
  10.0 30.1 %all-to-all-start = ((f32[1920,1,128]{2,1,0:T(1,128)}), f32[1920,1,128]{2,1,0:T(1,128)}, u32[]{:S(2)}, u32[]{:S(2)}) async-start(f32[1920,1,128]{2,1,0:T(1,128)} %bitcast.11), calls=%async_computation | async-start | bytes 1966080 | tf_op jit(solution)/shard_map/all_to_all | solution.py:542
  22.9 17.2 %copy-start = (f32[3,16,32,128]{3,2,1,0:T(8,128)S(1)}, f32[3,16,32,128]{3,2,1,0:T(8,128)}, u32[]{:S(2)}) copy-start(f32[3,16,32,128]{3,2,1,0:T(8,128)} %ef.3) | copy-start | bytes 2359300
  22.9 17.2 %copy-start.1 = (f32[3,16,32,128]{3,2,1,0:T(8,128)S(1)}, f32[3,16,32,128]{3,2,1,0:T(8,128)}, u32[]{:S(2)}) copy-start(f32[3,16,32,128]{3,2,1,0:T(8,128)} %hf.3) | copy-start | bytes 2359300
  22.9 17.2 %copy-start.2 = (f32[16,32,128]{2,1,0:T(8,128)S(1)}, f32[16,32,128]{2,1,0:T(8,128)}, u32[]{:S(2)}) copy-start(f32[16,32,128]{2,1,0:T(8,128)} %perm.3) | copy-start | bytes 786436
  23.1 14.5 %collective-permute-start.2 = (f32[595,128]{1,0:T(8,128)S(1)}, f32[595,128]{1,0:T(8,128)S(1)}, u32[]{:S(2)}, u32[]{:S(2)}) collective-permute-start(f32[595,128]{1,0:T(8,128)S(1)} %get-tuple-element.20), channel_id=1, source_target_pairs={{0,8},{8,16},{16,24},{24,32},{32,40},{40,48},{48,56},{56,64},{64,7... | collective-permute-start | bytes 913928 | tf_op jit(solution)/shard_map/ppermute | solution.py:536
  26.8 10.8 %collective-permute-start.3 = (f32[385,128]{1,0:T(8,128)S(1)}, f32[385,128]{1,0:T(8,128)S(1)}, u32[]{:S(2)}, u32[]{:S(2)}) collective-permute-start(f32[385,128]{1,0:T(8,128)S(1)} %get-tuple-element.21), channel_id=1, source_target_pairs={{8,0},{16,8},{24,16},{32,24},{40,32},{48,40},{56,48},{64,56},{72,6... | collective-permute-start | bytes 591368 | tf_op jit(solution)/shard_map/ppermute | solution.py:536
  45.5 17.4 %copy-start.5 = (f32[128,384]{1,0:T(8,128)S(1)}, f32[128,384]{1,0:T(8,128)}, u32[]{:S(2)}) copy-start(f32[128,384]{1,0:T(8,128)} %get-tuple-element.25.match) | copy-start | bytes 589828

commit v4 on v3

v4 whole, which is shorter than its diff:
```python
import functools
import math

import jax
import jax.numpy as jnp
from jax import lax
from jax.experimental import pallas as pl
from jax.experimental.pallas import tpu as pltpu
from jax.sharding import PartitionSpec as P

F32 = jnp.float32
LANES = 128
LAYERS = 32
LOWER = 48
COURANT = 0.5
ANGULAR = 0.9
CONTRAST = 8.0
EXACT = lax.Precision.HIGHEST

NX, NY = 16, 32
EY = 40
UP_ROWS = 23
DOWN_ROWS = 17
PLANES = 4
UP_X = 17
DOWN_X = 11
BESIDE = (EY - 1, NY, EY - 2)
TALL = NY + len(BESIDE)
ROWS = 11


def iota(shape, dim):
    return lax.broadcasted_iota(jnp.int32, shape, dim)


def params(limit):
    return pltpu.CompilerParams(vmem_limit_bytes=limit * 2**20)


def cost(micros):
    return pl.CostEstimate(flops=micros * 10**9, bytes_accessed=0, transcendentals=0)


def vmem():
    return pl.BlockSpec(memory_space=pltpu.VMEM)


def anywhere():
    return pl.BlockSpec(memory_space=pl.ANY)


def hbm():
    return pl.BlockSpec(memory_space=pltpu.HBM)


def shape(*dims):
    return jax.ShapeDtypeStruct(dims, F32)


def select_rows(marks, values):
    width = values.shape[1]
    high = values.astype(jnp.bfloat16)
    low = (values - high.astype(F32)).astype(jnp.bfloat16)
    found = jnp.dot(
        marks.astype(jnp.bfloat16),
        jnp.concatenate([high, low], axis=1),
        preferred_element_type=F32,
    )
    return found[:, :width] + found[:, width:]


def plan_y(to_next):
    if to_next:
        return [(0, 0, -2, 2), (0, 1, -2, 2), (0, 2, -2, 2), (1, 0, -2, 2), (1, 1, -1, 1), (1, 2, -2, 2)]
    return [(0, 0, 0, 2), (0, 1, 0, 1), (0, 2, 0, 2), (1, 0, 0, 1), (1, 1, 0, 1), (1, 2, 0, 1)]


def pack_tiles(pattern, owner, count, start, message, match):
    tiles = pattern.shape[0]
    square = (tiles, tiles)
    down, across = iota(square, 0), iota(square, 1)
    eye = down == across

    def column(row):
        return jnp.sum(jnp.where(eye, row.astype(F32), 0.0), axis=1, keepdims=True)

    owner_row = owner[...].astype(F32)
    owner_col = column(owner[...])
    same = owner_col == owner_row
    rank_row = jnp.sum(jnp.where(same & (down < across), 1.0, 0.0), axis=0, keepdims=True)
    rank_col = jnp.sum(jnp.where(same & (across < down), 1.0, 0.0), axis=1, keepdims=True)
    down_f, across_f = down.astype(F32), across.astype(F32)
    for k in range(2):
        match[:, k * tiles : (k + 1) * tiles] = jnp.where(
            (owner_col == across_f) & (rank_col == k), 1.0, 0.0
        )
    starts = column(start[...]).astype(jnp.int32)
    counts = column(count[...]).astype(jnp.int32)
    shift = starts & (LANES - 1)
    first = starts >> 7
    phase = first & 7
    match[:, 2 * tiles :] = jnp.where(
        across == 0, shift.astype(F32), jnp.where(across == 1, counts.astype(F32), 0.0)
    )
    wide = iota(pattern.shape, 1)
    cells = jnp.where(wide < counts, pattern[...], 0.0)
    for bit in range(7):
        cells = jnp.where((shift >> bit) & 1 == 1, pltpu.roll(cells, 1 << bit, 1), cells)
    front, back = cells[:, :LANES], cells[:, LANES:]
    head = jnp.where(across >= shift, front, 0.0)
    tail = jnp.where(across >= shift, 0.0, front)

    def pick(a, b, c):
        return jnp.where(
            phase == a, head, jnp.where(phase == b, back, jnp.where(phase == c, tail, 0.0))
        )

    low_y = pick(0, 7, 6)
    high_y = pick(7, 6, 5)
    low_corner = pltpu.roll(jnp.where((first + 7) >> 3 == NX - 1, low_y, 0.0), 32, 1)
    high_corner = pltpu.roll(jnp.where(first >> 3 == 0, high_y, 0.0), 96, 1)
    edges = jnp.where(
        across < 32,
        low_y,
        jnp.where(across < 64, low_corner, jnp.where(across < 96, high_corner, high_y)),
    )
    origin = jnp.broadcast_to(starts.astype(F32), square)
    everything = jnp.concatenate([front, back, edges, origin], axis=1)
    meta = jnp.zeros(square, F32)
    choose = [jnp.where((owner_row == down_f) & (rank_row == k), 1.0, 0.0) for k in range(2)]
    every_slot = select_rows(jnp.concatenate(choose, axis=0), everything)
    for k in range(2):
        slots = every_slot[k * tiles : (k + 1) * tiles]
        pair = slots[:, : 2 * LANES]
        edge = slots[:, 2 * LANES : 3 * LANES]
        origins = slots[:, 3 * LANES :]

        def other(values, distance):
            return pltpu.roll(values, -distance % tiles, 0)

        beyond = jnp.where(iota(pair.shape, 0) & 8 == 0, other(pair, -8), other(pair, 8))
        for place, rows in ((0, pair), (6, beyond)):
            for half in range(2):
                message[pl.ds(place + 2 * k + half, tiles, stride=ROWS), :] = rows[
                    :, half * LANES : (half + 1) * LANES
                ]
        message[pl.ds(4 + k, tiles, stride=ROWS), :] = jnp.where(
            across < 32,
            other(edge, 1),
            jnp.where(across < 64, other(edge, -7), jnp.where(across < 96, other(edge, 7), other(edge, -1))),
        )
        outer_origins = jnp.where(down & 8 == 0, other(origins, -8), other(origins, 8))
        for place, moved in enumerate((origins, other(origins, 1), other(origins, -1), outer_origins)):
            meta = jnp.where(across == 2 * place + k, moved, meta)
    message[pl.ds(10, tiles, stride=ROWS), :] = meta


def prepare_all(
    ef, hf, ea, ha, perm, pattern_hbm, owner_hbm, count_hbm, start_hbm,
    inner_y, outer_y, message, match,
    first, last, first_perm, last_perm,
    pattern, owner, count, start, sems,
):
    small = [(owner_hbm, owner), (count_hbm, count), (start_hbm, start), (pattern_hbm, pattern)]
    loads_y = []
    for dest, dest_perm, low in ((first, first_perm, 0), (last, last_perm, NY - 8)):
        rows = pl.ds(low, 8)
        for i, src in enumerate((ef, ea, hf, ha)):
            loads_y.append((src.at[:, :, rows], dest.at[pl.ds(3 * i, 3)]))
        loads_y.append((perm.at[:, rows], dest_perm))
    copies = [
        pltpu.make_async_copy(a, b, sems.at[i]) for i, (a, b) in enumerate(small + loads_y)
    ]
    for copy in copies:
        copy.start()
    for copy in copies[:4]:
        copy.wait()
    pack_tiles(pattern, owner, count, start, message, match)
    for copy in copies[4:]:
        copy.wait()

    def fill(up, down):
        for to_next, src, src_perm, out in ((True, last, last_perm, up), (False, first, first_perm, down)):
            flat = src.reshape(12 * NX * 8, LANES)
            flat_perm = src_perm.reshape(NX * 8, LANES)
            at = 0
            for evolution in range(2):
                for field, comp, begin, planes in plan_y(to_next):
                    for k in range(planes):
                        row = (field * 6 + evolution * 3 + comp) * NX * 8 + (begin + k) % 8
                        out[pl.ds(at * NX, NX), :] = flat[pl.ds(row, NX, stride=8), :]
                        at += 1
            out[pl.ds(at * NX, NX), :] = flat_perm[pl.ds(7 if to_next else 0, NX, stride=8), :]
        down[DOWN_ROWS * NX :] = jnp.zeros(((UP_ROWS - DOWN_ROWS) * NX, LANES), F32)

    to_pairs("gy", fill, inner_y, outer_y)


def prepare(ef, hf, ea, ha, perm, pattern, owners, tile_count, tile_start):
    tiles = pattern.shape[0]
    return pl.pallas_call(
        prepare_all,
        out_shape=(
            shape(UP_ROWS * NX, LANES),
            shape(UP_ROWS * NX, LANES),
            shape(tiles * ROWS, LANES),
            shape(tiles, 3 * tiles),
        ),
        in_specs=[hbm()] * 9,
        out_specs=(vmem(),) * 4,
        scratch_shapes=[
            pltpu.VMEM((12, NX, 8, LANES), F32),
            pltpu.VMEM((12, NX, 8, LANES), F32),
            pltpu.VMEM((NX, 8, LANES), F32),
            pltpu.VMEM((NX, 8, LANES), F32),
            pltpu.VMEM((tiles, 2 * LANES), F32),
            pltpu.VMEM((1, tiles), jnp.int32),
            pltpu.VMEM((1, tiles), jnp.int32),
            pltpu.VMEM((1, tiles), jnp.int32),
            pltpu.SemaphoreType.DMA((14,)),
        ],
        compiler_params=params(56),
        cost_estimate=cost(3),
        name="prepare",
    )(
        ef, hf, ea, ha, perm, pattern,
        owners.reshape(1, tiles), tile_count.reshape(1, tiles), tile_start.reshape(1, tiles),
    )


def to_pairs(axis, fill, inner, outer):
    even = lax.axis_index(axis) % 2 == 0
    pl.when(even)(lambda: fill(inner, outer))
    pl.when(jnp.logical_not(even))(lambda: fill(outer, inner))


def from_pairs(axis, inner, outer):
    even = lax.axis_index(axis) % 2 == 0

    def rows(from_prev, begin, count):
        near, far = (outer, inner) if from_prev else (inner, outer)
        return jnp.where(even, near[pl.ds(begin, count), :], far[pl.ds(begin, count), :])

    return rows


def after_y(values):
    return pltpu.roll(values, values.shape[0] - 1, 0)


def before_y(values):
    return pltpu.roll(values, 1, 0)


def after_z(values):
    return jnp.where(iota(values.shape, 1) == LANES - 1, 0.0, pltpu.roll(values, LANES - 1, 1))


def before_z(values):
    return jnp.where(iota(values.shape, 1) == 0, 0.0, pltpu.roll(values, 1, 1))


def curl_e(here, ahead):
    ex, ey, ez = here
    next_y, next_z = ahead
    return (
        (after_y(ez) - ez) - (after_z(ey) - ey),
        (after_z(ex) - ex) - (next_z - ez),
        (next_y - ey) - (after_y(ex) - ex),
    )


def curl_h(here, behind):
    hx, hy, hz = here
    last_y, last_z = behind
    return (
        (hz - before_y(hz)) - (hy - before_z(hy)),
        (hx - before_z(hx)) - (hz - last_z),
        (hy - last_y) - (hx - before_y(hx)),
    )


def start_row(meta_rows, index):
    return meta_rows[index : index + 1, :].astype(jnp.int32)


def start_col(meta, index):
    return meta[:, index : index + 1].astype(jnp.int32)


def step_one(
    ef, hf, ea, ha, perm, inner_any, outer_any, inner_y_any, outer_y_any, message_any,
    final, overlap, sigma_out, state, inner_out,
    forward, adjoint, perm_wide, grow, e_out, h_out, turned, rate, final_v, outer_local,
    inner, outer, inner_y, outer_y, message, sems,
):
    wide = (forward, adjoint)
    loads = [(src, wide[i // 2].at[pl.ds(3 * (i % 2), 3), :, pl.ds(0, NY)]) for i, src in enumerate((ef, hf, ea, ha))]
    pairs = [(message_any, message), (inner_y_any, inner_y), (outer_y_any, outer_y)]
    pairs += [(perm, perm_wide.at[:, pl.ds(0, NY)]), (inner_any, inner), (outer_any, outer)]
    pairs += loads
    copies = [pltpu.make_async_copy(a, b, sems.at[i]) for i, (a, b) in enumerate(pairs)]
    for copy in copies:
        copy.start()
    copies[0].wait()
    tiles = message.shape[0] // ROWS
    square = (tiles, LANES)
    across = iota(square, 1)
    block = NX * 8

    def rows_of(place):
        return message[pl.ds(place, tiles, stride=ROWS), :]

    meta = rows_of(10)
    meta_rows = meta.T
    even = lax.axis_index("gx") % 2 == 0

    def place_cells(place, index, row):
        targets, values = [], []
        for k in range(2):
            first = start_row(meta_rows, index + k) >> 7
            shift = start_col(meta, index + k) & (LANES - 1)
            front, back = rows_of(place + 2 * k), rows_of(place + 2 * k + 1)
            head, tail = jnp.where(across >= shift, front, 0.0), jnp.where(across >= shift, 0.0, front)
            for step, part in enumerate((head, back, tail)):
                targets.append(jnp.where(first + step == row, 1.0, 0.0))
                values.append(part)
        return select_rows(jnp.concatenate(targets, axis=1), jnp.concatenate(values, axis=0))

    density = place_cells(0, 0, iota((block, tiles), 0))
    beyond = place_cells(6, 6, iota((16, tiles), 0) + jnp.where(even, block - 8, 0))[:8]
    sigma = jax.nn.sigmoid(density)
    sigma_out[...] = sigma
    own = CONTRAST * sigma
    targets = []
    row = iota((3 * NX, tiles), 0)
    for k in range(2):
        first = start_row(meta_rows, 2 + k) >> 7
        last = start_row(meta_rows, 4 + k) >> 7
        targets.append(
            jnp.where(
                (((first + 7) >> 3 == row) & (row < NX))
                | ((last >> 3) + NX == row)
                | (row >= 2 * NX),
                1.0,
                0.0,
            )
        )
    sides = CONTRAST * jax.nn.sigmoid(
        select_rows(jnp.concatenate(targets, axis=1), jnp.concatenate([rows_of(4), rows_of(5)], axis=0))
    )

    def lanes_to(values, source):
        lane = iota(values.shape, 1)
        moved = pltpu.roll(values, (LOWER - source) % LANES, 1)
        return jnp.where((lane >= LOWER) & (lane < LOWER + LAYERS), moved, 0.0)

    for quarter in range(4):
        moved = lanes_to(own, quarter * LAYERS)
        for x in range(NX):
            grow[pl.ds(x * EY + quarter, 8, stride=4), :] = moved[8 * x : 8 * x + 8]
    grow[pl.ds(NY, NX, stride=EY), :] = lanes_to(sides[:NX], 0)
    grow[pl.ds(EY - 1, NX, stride=EY), :] = lanes_to(sides[NX : 2 * NX], 96)
    beyond = CONTRAST * jax.nn.sigmoid(beyond)
    for quarter in range(4):
        grow[pl.ds(NX * EY + quarter, 8, stride=4), :] = lanes_to(beyond, quarter * LAYERS)
    corner = sides[2 * NX : 2 * NX + 8]
    grow[pl.ds(NX * EY + NY, 1), :] = lanes_to(corner, 32)[:1]
    grow[pl.ds(NX * EY + EY - 1, 1), :] = lanes_to(corner, 64)[:1]

    low_x = lax.axis_index("gx") > 0
    gy = lax.axis_index("gy")
    low_y, high_y = gy > 0, gy < lax.axis_size("gy") - 1
    y = iota((EY, LANES), 0)
    within = (y < NY) | ((y == NY) & high_y) | ((y == EY - 1) & low_y)
    cut = jnp.where((y < EY - 2) | low_y, COURANT, 0.0)
    edge_cut = jnp.where(low_x, cut, 0.0)
    nothing = jnp.zeros((EY, LANES), F32)
    for copy in copies[1:6]:
        copy.wait()
    flat_perm = perm_wide.reshape(NX * EY, LANES)
    beside_y = from_pairs("gy", inner_y, outer_y)
    flat_perm[pl.ds(EY - 1, NX, stride=EY), :] = beside_y(True, (UP_ROWS - 1) * NX, NX)
    flat_perm[pl.ds(NY, NX, stride=EY), :] = beside_y(False, (DOWN_ROWS - 1) * NX, NX)

    def halo_plane(src, planes, at):
        begin, row = planes * NY + 3 * at, iota((8, LANES), 0)
        tile = nothing[:8]
        for k in range(3):
            tile = jnp.where(row == BESIDE[k] - NY, src[begin + k : begin + k + 1], tile)
        return jnp.concatenate([src[at * NY : (at + 1) * NY], tile], axis=0)

    def e_ahead(evolution, c):
        return jnp.where(
            even,
            halo_plane(inner, PLANES, 2 * evolution + c - 1),
            halo_plane(outer, DOWN_X, 5 * evolution + c - 1),
        )

    def h_behind(evolution, c):
        return jnp.where(
            even,
            halo_plane(outer, UP_X, 8 * evolution + 3 + c),
            halo_plane(inner, PLANES, 2 * evolution + c - 1),
        )

    for evolution in range(2):
        e, fields = 3 * evolution, wide[evolution]
        for copy in copies[6 + 2 * evolution : 8 + 2 * evolution]:
            copy.wait()
        flat = fields.reshape(6 * NX * EY, LANES)
        for from_prev, planes in ((True, UP_ROWS), (False, DOWN_ROWS)):
            at = evolution * (planes // 2)
            for field, comp, begin, count in plan_y(from_prev):
                for k in range(count):
                    row = EY + begin + k if from_prev else NY + begin + k
                    place = (field * 3 + comp) * NX * EY + row
                    flat[pl.ds(place, NX, stride=EY), :] = beside_y(from_prev, at * NX, NX)
                    at += 1
        for x in range(NX):
            here = [fields[c, x] for c in range(3)]
            if x < NX - 1:
                ahead = [fields[c, x + 1] for c in (1, 2)]
            else:
                ahead = [e_ahead(evolution, c) for c in (1, 2)]
            curl = curl_e(here, ahead)
            for c in range(3):
                h_out[e + c, x] = fields[3 + c, x] - cut * curl[c]
        for x in range(NX):
            if evolution:
                scale = grow[pl.ds(x * EY, EY), :]
            else:
                eps = perm_wide[x] + grow[pl.ds(x * EY, EY), :]
                scale = jnp.where(within, COURANT / eps, 0.0)
                grow[pl.ds(x * EY, EY), :] = scale
                rate[x] = scale[:NY]
            here = [h_out[e + c, x] for c in range(3)]
            if x > 0:
                behind = [h_out[e + c, x - 1] for c in (1, 2)]
            else:
                behind = [
                    h_behind(evolution, 1) + edge_cut * fields[2, 0],
                    h_behind(evolution, 2) - edge_cut * fields[1, 0],
                ]
            curl = curl_h(here, behind)
            for c in range(3):
                e_out[e + c, x] = fields[c, x] + scale * curl[c]

    def outer_rate(planes, inside, rows):
        eps = halo_plane(outer, planes, planes - 1) + grow[pl.ds(NX * EY, EY), :]
        return jnp.where(rows & inside, COURANT / eps, 0.0)

    def put_up(out, evolution, h, e, factor):
        curl = curl_e(e, [nothing, nothing])
        for c in (1, 2):
            at = (2 * evolution + c - 1) * NY
            out[at : at + NY] = (h[c] - factor * curl[c])[:NY]

    def put_down(out, evolution, e_y, e_z):
        at = 2 * evolution * NY
        out[at : at + NY] = e_y[:NY]
        out[at + NY : at + 2 * NY] = e_z[:NY]
        at = PLANES * NY + evolution
        out[at : at + 1] = e_y[EY - 1 :]

    for out in (inner_out, outer_local):
        out[PLANES * NY :] = jnp.zeros((8, LANES), F32)

    def even_device():
        scale = outer_rate(UP_X, low_x, within & (y < EY - 1))
        for evolution in range(2):
            e = 3 * evolution
            last = [e_out[e + c, NX - 1] for c in range(3)]
            put_up(inner_out, evolution, [h_out[e + c, NX - 1] for c in range(3)], last, cut)
            electric, magnetic = [
                [halo_plane(outer, UP_X, 8 * evolution + i + c) for c in range(3)] for i in (0, 3)
            ]
            start = wide[evolution]
            magnetic[1] = magnetic[1] + edge_cut * start[2, 0]
            magnetic[2] = magnetic[2] - edge_cut * start[1, 0]
            curl = curl_h(magnetic, [halo_plane(outer, UP_X, 8 * evolution + 6 + c) for c in range(2)])
            electric = [electric[c] + scale * curl[c] for c in range(3)]
            put_up(outer_local, evolution, magnetic, electric, edge_cut)

    def odd_device():
        scale = outer_rate(DOWN_X, lax.axis_index("gx") < lax.axis_size("gx") - 1, within & (y != NY))
        for evolution in range(2):
            e = 3 * evolution
            put_down(inner_out, evolution, e_out[e + 1, 0], e_out[e + 2, 0])
            planes = [halo_plane(outer, DOWN_X, 5 * evolution + i) for i in range(5)]
            curl = curl_h(planes[2:], [h_out[e + c, NX - 1] for c in (1, 2)])
            put_down(outer_local, evolution, planes[0] + scale * curl[1], planes[1] + scale * curl[2])

    pl.when(even)(even_device)
    pl.when(jnp.logical_not(even))(odd_device)

    def ahead_plane(at, evolution):
        tile = jnp.where(iota((8, LANES), 0) == 7, outer_local[pl.ds(PLANES * NY + evolution, 1), :], 0.0)
        plane = jnp.concatenate([outer_local[pl.ds(at * NY, NY), :], tile], axis=0)
        return jnp.where(even, 0.0, plane)

    for x in range(NX):
        for evolution in range(2):
            e = 3 * evolution
            here = [e_out[e + c, x] for c in range(3)]
            if x < NX - 1:
                ahead = [e_out[e + c, x + 1] for c in (1, 2)]
            else:
                ahead = [ahead_plane(2 * evolution + c, evolution) for c in range(2)]
            curl = curl_e(here, ahead)
            for c in range(3):
                turned[e + c, x] = h_out[e + c, x] - cut * curl[c]
    leaving = []
    for x in range(NX):
        old, new = [], []
        for evolution in range(2):
            e = 3 * evolution
            if x > 0:
                behind = [turned[e + c, x - 1][:NY] for c in (1, 2)]
            else:
                at = 2 * evolution * NY
                factor = edge_cut[:NY]
                behind = [
                    outer_local[pl.ds(at, NY), :] + factor * e_out[e + 2, 0][:NY],
                    outer_local[pl.ds(at + NY, NY), :] - factor * e_out[e + 1, 0][:NY],
                ]
            old.append([e_out[e + c, x][:NY] for c in range(3)])
            new.append(last_e(old[-1], rate[x], [turned[e + c, x] for c in range(3)], behind))
        for c in range(3):
            final_v[c, x] = new[0][c]
        overlap[pl.ds(x * NY, NY), :] = product(old, new)
        if x % 4 == 3:
            part = pl.ds(x - 3, 4)
            leaving.append(pltpu.make_async_copy(final_v.at[:, part], final.at[:, part], sems.at[10 + x // 4]))
            leaving[-1].start()

    def keep(x):
        for c in range(6):
            state[c] = e_out[c, x]
            state[6 + c] = turned[c, x]
        for evolution in range(2):
            for c in (1, 2):
                state[11 + 2 * evolution + c] = turned[3 * evolution + c, NX - 2]
        state[16, :NY] = rate[x]
        state[16, NY:] = nothing[NY:]

    pl.when(even)(lambda: keep(NX - 1))
    pl.when(jnp.logical_not(even))(lambda: keep(0))
    for copy in leaving:
        copy.wait()


def last_e(electric, scale, magnetic, behind):
    last_x, last_z = before_y(magnetic[0])[:NY], before_y(magnetic[2])[:NY]
    hx, hy, hz = [v[:NY] for v in magnetic]
    curl = (
        (hz - last_z) - (hy - before_z(hy)),
        (hx - before_z(hx)) - (hz - behind[1]),
        (hy - behind[0]) - (hx - last_x),
    )
    return [electric[c] + scale * curl[c] for c in range(3)]


def product(old, new):
    blend = math.cos(ANGULAR)
    total = 0.0
    for c in range(3):
        total += old[0][c] * (old[1][c] + blend * new[1][c])
        total += new[0][c] * (new[1][c] + blend * old[1][c])
    return total


def first_step(ef, hf, ea, ha, perm, inner, outer, inner_y, outer_y, message):
    return pl.pallas_call(
        step_one,
        out_shape=(
            shape(3, NX, NY, LANES),
            shape(NX * NY, LANES),
            shape(NX * 8, LANES),
            shape(17, EY, LANES),
            shape(PLANES * NY + 8, LANES),
        ),
        in_specs=[hbm()] * 5 + [anywhere()] * 5,
        out_specs=(hbm(),) + (vmem(),) * 4,
        scratch_shapes=[
            pltpu.VMEM((6, NX, EY, LANES), F32),
            pltpu.VMEM((6, NX, EY, LANES), F32),
            pltpu.VMEM((NX, EY, LANES), F32),
            pltpu.VMEM(((NX + 1) * EY, LANES), F32),
            pltpu.VMEM((6, NX, EY, LANES), F32),
            pltpu.VMEM((6, NX, EY, LANES), F32),
            pltpu.VMEM((6, NX, EY, LANES), F32),
            pltpu.VMEM((NX, NY, LANES), F32),
            pltpu.VMEM((3, NX, NY, LANES), F32),
            pltpu.VMEM((PLANES * NY + 8, LANES), F32),
            pltpu.VMEM(inner.shape, F32),
            pltpu.VMEM(outer.shape, F32),
            pltpu.VMEM(inner_y.shape, F32),
            pltpu.VMEM(outer_y.shape, F32),
            pltpu.VMEM(message.shape, F32),
            pltpu.SemaphoreType.DMA((14,)),
        ],
        compiler_params=params(51),
        cost_estimate=cost(5),
        name="step_one",
    )(ef, hf, ea, ha, perm, inner, outer, inner_y, outer_y, message)


def step_two(final_in, overlap_in, sigma_in, state, inner, message, final, reply, plane, overlap, sem):
    even = lax.axis_index("gx") % 2 == 0
    low_y = lax.axis_index("gy") > 0
    y = iota((EY, LANES), 0)
    cut = jnp.where(((y < EY - 2) | low_y) & even, COURANT, 0.0)
    x = jnp.where(even, NX - 1, 0)
    overlap[...] = overlap_in[...]
    old, new = [], []
    for evolution in range(2):
        e, at = 3 * evolution, 2 * evolution * NY
        rows = [inner[at + c * NY : at + (c + 1) * NY] for c in range(2)]
        beside = inner[PLANES * NY + evolution : PLANES * NY + evolution + 1]
        tile = jnp.where(iota((8, LANES), 0) == 7, beside, 0.0)
        ahead = [jnp.concatenate([r, tile], axis=0) for r in rows]
        old.append([state[e + c][:NY] for c in range(3)])
        magnetic = [state[6 + e], state[7 + e] + cut * ahead[1], state[8 + e] - cut * ahead[0]]
        behind = [
            jnp.where(even, state[12 + 2 * evolution][:NY], rows[0] + COURANT * old[-1][2]),
            jnp.where(even, state[13 + 2 * evolution][:NY], rows[1] - COURANT * old[-1][1]),
        ]
        new.append(last_e(old[-1], state[16][:NY], magnetic, behind))
    for c in range(3):
        plane[c] = new[0][c]
    final_copy = pltpu.make_async_copy(plane, final.at[:, x], sem)
    final_copy.start()
    overlap[pl.ds(pl.multiple_of(x * NY, NY), NY), :] = product(old, new)
    tiles = message.shape[0] // ROWS
    across = iota((tiles, LANES), 1)
    meta = message[pl.ds(10, tiles, stride=ROWS), :]
    block = NX * 8
    compact = jnp.zeros((block, LANES), F32)
    lane = iota((block, LANES), 1)
    for quarter in range(4):
        part = pltpu.roll(
            overlap[pl.ds(quarter, block, stride=4), :], (quarter * LAYERS - LOWER) % LANES, 1
        )
        compact = jnp.where(lane // LAYERS == quarter, part, compact)
    sigma = sigma_in[...]
    gradient = CONTRAST * sigma * (1.0 - sigma) * compact
    picks, shifts = [], []
    for k in range(2):
        starts = start_col(meta, k)
        shifts.append(starts & (LANES - 1))
        for step in range(3):
            picks.append(jnp.where(iota((tiles, block), 1) == (starts >> 7) + step, 1.0, 0.0))
    found = select_rows(jnp.concatenate(picks, axis=0), gradient)
    for k in range(2):
        head, back, tail = [found[(3 * k + i) * tiles : (3 * k + i + 1) * tiles] for i in range(3)]
        reply[pl.ds(2 * k, tiles, stride=4), :] = jnp.where(across >= shifts[k], head, tail)
        reply[pl.ds(2 * k + 1, tiles, stride=4), :] = back
    final_copy.wait()


def second_step(final, overlap, sigma, state, inner, message):
    tiles = message.shape[0] // ROWS
    return pl.pallas_call(
        step_two,
        out_shape=(shape(3, NX, NY, LANES), shape(tiles * 4, LANES)),
        in_specs=[hbm()] + [vmem()] * 5,
        out_specs=(hbm(), vmem()),
        input_output_aliases={0: 0},
        scratch_shapes=[
            pltpu.VMEM((3, NY, LANES), F32),
            pltpu.VMEM((NX * NY, LANES), F32),
            pltpu.SemaphoreType.DMA,
        ],
        compiler_params=params(30),
        cost_estimate=cost(1),
        name="step_two",
    )(final, overlap, sigma, state, inner, message)


def unpack_tiles(reply, match, out):
    tiles = out.shape[0]
    shift = match[:, 2 * tiles : 2 * tiles + 1].astype(jnp.int32)
    count = match[:, 2 * tiles + 1 : 2 * tiles + 2].astype(jnp.int32)
    rows = [
        jnp.concatenate(
            [reply[pl.ds(2 * k + half, tiles, stride=4), :] for half in range(2)], axis=1
        )
        for k in range(2)
    ]
    cells = select_rows(match[:, : 2 * tiles], jnp.concatenate(rows, axis=0))
    width = out.shape[1]
    for bit in range(7):
        cells = jnp.where((shift >> bit) & 1 == 1, pltpu.roll(cells, width - (1 << bit), 1), cells)
    out[...] = jnp.where(iota(out.shape, 1) < count, cells, 0.0)


def unpack(reply, match):
    tiles = match.shape[0]
    return pl.pallas_call(
        unpack_tiles,
        out_shape=shape(tiles, 2 * LANES),
        in_specs=[vmem()] * 2,
        out_specs=vmem(),
        compiler_params=params(16),
        cost_estimate=cost(2),
        name="unpack_tiles",
    )(reply, match)


def swapped(block, axis, first):
    pairs = [(i, i + 1) for i in range(first, lax.axis_size(axis) - 1, 2)]
    return lax.ppermute(block, axis, pairs + [(j, i) for i, j in pairs])


def exchange(block, depth):
    out = lax.all_to_all(
        block.reshape(-1, depth, LANES), ("gx", "gy"), split_axis=0, concat_axis=0, tiled=True
    )
    return out.reshape(block.shape)


def faces_x(ef, hf, ea, ha, perm, inner_y, outer_y, inner_out, outer_out, first_x, last_x, edge_perm, tiles, sems):
    pairs = []
    for i, src in enumerate((ef, ea, hf, ha)):
        pairs.append((src.at[:, pl.ds(NX - 2, 2)], last_x.at[pl.ds(3 * i, 3)]))
        pairs.append((src.at[:, pl.ds(0, 2)], first_x.at[pl.ds(3 * i, 3)]))
    pairs.append((perm.at[NX - 1], edge_perm.at[0]))
    pairs.append((perm.at[0], edge_perm.at[1]))
    copies = [pltpu.make_async_copy(a, b, sems.at[i]) for i, (a, b) in enumerate(pairs)]
    for copy in copies:
        copy.start()
    beside = from_pairs("gy", inner_y, outer_y)
    for from_prev in (True, False):
        at = 0
        for evolution in range(2):
            for field, comp, begin, count in plan_y(from_prev):
                for k in range(count):
                    row = 8 + begin + k if from_prev else begin + k
                    for i, x in enumerate((NX - 2, NX - 1, 0, 1)):
                        tiles[field * 6 + evolution * 3 + comp, i, row : row + 1, :] = beside(
                            from_prev, at * NX + x, 1
                        )
                    at += 1
    for copy in copies:
        copy.wait()

    def plane(c, i):
        block = last_x[c, i] if i < 2 else first_x[c, i - 2]
        return jnp.concatenate([block, tiles[c, i]], axis=0)

    def send(out, planes, at, values):
        out[at * NY : (at + 1) * NY] = values[:NY]
        for k, row in enumerate(BESIDE):
            out[planes * NY + 3 * at + k : planes * NY + 3 * at + k + 1] = values[row : row + 1]

    def send_perm(out, planes, i, x):
        at = planes - 1
        out[at * NY : (at + 1) * NY] = edge_perm[i]
        for k, (from_prev, count) in enumerate(((True, UP_ROWS), (False, DOWN_ROWS))):
            begin = planes * NY + 3 * at + k
            out[begin : begin + 1] = beside(from_prev, (count - 1) * NX + x, 1)
        out[planes * TALL - 1 :] = jnp.zeros((outer_out.shape[0] - planes * TALL + 1, LANES), F32)

    inside_y = lax.axis_index("gy") > 0
    rate = jnp.where((iota((EY, LANES), 0) < EY - 2) | inside_y, COURANT, 0.0)
    nothing = jnp.zeros((EY, LANES), F32)

    def even_device():
        for evolution in range(2):
            e, h = 3 * evolution, 6 + 3 * evolution
            curl = curl_e([plane(e + c, 1) for c in range(3)], [nothing, nothing])
            for c in (1, 2):
                send(inner_out, PLANES, 2 * evolution + c - 1, plane(h + c, 1) - rate * curl[c])
            first, second = [[plane(e + c, i) for c in range(3)] for i in (2, 3)]
            curl = curl_e(first, second[1:])
            planes = first[1:] + [plane(h + c, 2) - rate * curl[c] for c in range(3)]
            for i, values in enumerate(planes):
                send(outer_out, DOWN_X, 5 * evolution + i, values)
        send_perm(outer_out, DOWN_X, 1, 0)

    def odd_device():
        for evolution in range(2):
            e, h = 3 * evolution, 6 + 3 * evolution
            for c in (1, 2):
                send(inner_out, PLANES, 2 * evolution + c - 1, plane(e + c, 2))
            before_last, last = [[plane(e + c, i) for c in range(3)] for i in (0, 1)]
            curl = curl_e(before_last, last[1:])
            planes = [plane(h + c, 0) - rate * curl[c] for c in (1, 2)]
            curl = curl_e(last, [nothing, nothing])
            planes = last + [plane(h + c, 1) - rate * curl[c] for c in range(3)] + planes
            for i, values in enumerate(planes):
                send(outer_out, UP_X, 8 * evolution + i, values)
        send_perm(outer_out, UP_X, 0, NX - 1)

    even = lax.axis_index("gx") % 2 == 0
    pl.when(even)(even_device)
    pl.when(jnp.logical_not(even))(odd_device)


def send_x(ef, hf, ea, ha, perm, inner_y, outer_y):
    return pl.pallas_call(
        faces_x,
        out_shape=(shape(PLANES * TALL, LANES), shape(UP_X * TALL, LANES)),
        in_specs=[hbm()] * 5 + [vmem()] * 2,
        out_specs=(vmem(), vmem()),
        scratch_shapes=[
            pltpu.VMEM((12, 2, NY, LANES), F32),
            pltpu.VMEM((12, 2, NY, LANES), F32),
            pltpu.VMEM((2, NY, LANES), F32),
            pltpu.VMEM((12, 4, 8, LANES), F32),
            pltpu.SemaphoreType.DMA((10,)),
        ],
        compiler_params=params(50),
        cost_estimate=cost(20),
        name="faces_x",
    )(ef, hf, ea, ha, perm, inner_y, outer_y)


def shards(ef, hf, ea, ha, perm, pattern, owners, tile_count, tile_start):
    inner_y, outer_y, message, match = prepare(
        ef, hf, ea, ha, perm, pattern, owners, tile_count, tile_start
    )
    outer_y, inner_y = swapped(outer_y, "gy", 1), swapped(inner_y, "gy", 0)
    arrived = exchange(message, 1)
    inner, outer = send_x(ef, hf, ea, ha, perm, inner_y, outer_y)
    outer, inner = swapped(outer, "gx", 1), swapped(inner, "gx", 0)
    *state, inner = first_step(
        ef, hf, ea, ha, perm, inner, outer, inner_y, outer_y, arrived
    )
    final, reply = second_step(*state, swapped(inner, "gx", 0), arrived)
    return final, unpack(exchange(reply, 4), match)


def solution(mesh):
    grid = P(None, "gx", "gy", None)
    tiles = ("gx", "gy")
    return jax.shard_map(
        shards,
        mesh=mesh,
        in_specs=(grid,) * 4 + (P("gx", "gy", None), P(tiles, None), P(tiles, None), P(tiles), P(tiles)),
        out_specs=(grid, P(tiles, None)),
        check_vma=False,
    )
```

time: 64.5 us -> 61.4 us (0.952)
  starting transfers between devices: 24.1 us -> 21.5 us
  Pallas kernels: 10.5 us -> 12.9 us
  waiting for transfers between devices: 11.4 us -> 9.87 us
  blocking collectives: 17.4 us -> 16.1 us
    pallas_call x3 -> x4, Pallas kernels: 9.11 us -> 11.5 us  [the longest x1 5.05 us: first_step(): pl.pallas_call(step_one, out_shape=(shape(3, NX, NY, LANES), shape(NX * N...]
    ppermute x4 -> x5, starting transfers between devices: 11.3 us -> 9.24 us  [swapped(): return lax.ppermute(block, axis, pairs + [(j, i) for i, j in pairs])]
    all_to_all x1, blocking collectives: 17.4 us -> 16.1 us  [exchange(): lax.all_to_all(block.reshape(-1, depth, LANES), ('gx', 'gy'), split_axis=...]
    all_to_all x1, waiting for transfers between devices: 2.52 us -> 1.49 us  [exchange(): lax.all_to_all(block.reshape(-1, depth, LANES), ('gx', 'gy'), split_axis=...]
    ppermute x4 -> x5, waiting for transfers between devices: 8.91 us -> 8.38 us  [swapped(): return lax.ppermute(block, axis, pairs + [(j, i) for i, j in pairs])]
  transfers between devices with their start and end apart: 5 -> 6, of which waited for: 2 -> 4; matrix products, arithmetic and copies ran while one was open for 0% -> 0% of each run, Pallas kernels for 0% -> 4%
where the time goes in v4:
time: 61.4 us; the launch traced here: 61.1 us
  starting transfers between devices  21.5 us (35%)
  blocking collectives  16.1 us (26%)
  Pallas kernels  12.9 us (21%)
  waiting for transfers between devices  9.87 us (16%)
  between operations  0.77 us (1%)
    all_to_all x1, blocking collectives, exchange(): lax.all_to_all(block.reshape(-1, depth, LANES), ('gx', 'gy'), split_axis=...  16.1 us
    all_to_all x1, starting transfers between devices, exchange(): lax.all_to_all(block.reshape(-1, depth, LANES), ('gx', 'gy'), split_axis=...  12.3 us
    ppermute x5, starting transfers between devices, swapped(): return lax.ppermute(block, axis, pairs + [(j, i) for i, j in pairs])  9.24 us
    ppermute x5, waiting for transfers between devices, swapped(): return lax.ppermute(block, axis, pairs + [(j, i) for i, j in pairs])  8.38 us
    pallas_call x1, Pallas kernels, first_step(): pl.pallas_call(step_one, out_shape=(shape(3, NX, NY, LANES), shape(NX * N...  5.05 us
    pallas_call x1, Pallas kernels, prepare(): pl.pallas_call(prepare_all, out_shape=(shape(UP_ROWS * NX, LANES), shape(...  3.36 us
    pallas_call x1, Pallas kernels, send_x(): pl.pallas_call(faces_x, out_shape=(shape(PLANES * TALL, LANES), shape(UP_...  2.3 us
    all_to_all x1, waiting for transfers between devices, exchange(): lax.all_to_all(block.reshape(-1, depth, LANES), ('gx', 'gy'), split_axis=...  1.49 us
  transfers between devices with their start and end apart: 6, of which 4 were waited for; matrix products, arithmetic and copies ran while one was open for 0% of the time, Pallas kernels for 4%

profile of v4, /device:TPU:1, one launch (start us, length us, event | category | flops | bytes accessed | tf_op | source)
XLA Modules:
  0.0 61.1 jit_solution(453504976894460180)
XLA Ops:
  0.6 0.0 copy-start.1
  0.6 0.0 copy-start.2
  0.7 3.4 %prepare.1 = (f32[368,128]{1,0:T(8,128)}, f32[368,128]{1,0:T(8,128)}, f32[1408,128]{1,0:T(8,128)}, f32[128,384]{1,0:T(8,128)}) custom-call(f32[3,16,32,128]{3,2,1,0:T(8,128)} %ef.5, f32[3,16,32,128]{3,2,1,0:T(8,128)} %hf.5, f32[3,16,32,128]{3,2,1,0:T(8,128)} %ea.5, f32[3,16,32,128]{3,2,1,0:T(8,128)} %ha.5, f32[16,32,128]{2,1,0:T(8,128)} %perm.5, ...), custom_call_target="tpu_custom_call" | custom-call | flops 3000000000 | tf_op jit(solution)/shard_map/prepare/pallas_call | solution.py:201
  4.0 0.0 copy-start
  4.0 2.5 %collective-permute-start = (f32[368,128]{1,0:T(8,128)}, f32[368,128]{1,0:T(8,128)S(1)}, u32[]{:S(2)}, u32[]{:S(2)}) collective-permute-start(f32[368,128]{1,0:T(8,128)} %get-tuple-element.15), channel_id=1, source_target_pairs={{0,1},{2,3},{4,5},{6,7},{1,0},{3,2},{5,4},{7,6},{8,9},{10,11},{12,... | collective-permute-start | bytes 565256 | tf_op jit(solution)/shard_map/ppermute | solution.py:713
  6.6 1.3 %collective-permute-start.1 = (f32[368,128]{1,0:T(8,128)}, f32[368,128]{1,0:T(8,128)}, u32[]{:S(2)}, u32[]{:S(2)}) collective-permute-start(f32[368,128]{1,0:T(8,128)} %get-tuple-element.16), channel_id=1, source_target_pairs={{1,2},{3,4},{5,6},{2,1},{4,3},{6,5},{9,10},{11,12},{13,14},{10,9},... | collective-permute-start | bytes 565256 | tf_op jit(solution)/shard_map/ppermute | solution.py:713
  7.9 0.0 copy-start.3
  7.9 12.3 %all-to-all-start = ((f32[1408,1,128]{2,1,0:T(1,128)}), f32[1408,1,128]{2,1,0:T(1,128)S(1)}, u32[]{:S(2)}, u32[]{:S(2)}) async-start(f32[1408,1,128]{2,1,0:T(1,128)} %bitcast.13), calls=%async_computation | async-start | bytes 1441792 | tf_op jit(solution)/shard_map/all_to_all | solution.py:717
  20.2 0.0 collective-permute-done.inner_y.inner_y_any
  20.2 0.0 collective-permute-done.1.outer_y.outer_y_any
  20.2 0.0 copy-done.1
  20.2 0.0 copy-done.2
  20.2 0.0 copy-done
  20.3 0.0 copy-done.3
  20.3 2.3 %faces_x.1 = (f32[140,128]{1,0:T(8,128)S(1)}, f32[595,128]{1,0:T(8,128)S(1)}) custom-call(f32[3,16,32,128]{3,2,1,0:T(8,128)S(1)} %copy-done, f32[3,16,32,128]{3,2,1,0:T(8,128)S(1)} %copy-done.1, f32[3,16,32,128]{3,2,1,0:T(8,128)S(1)} %copy-done.2, f32[3,16,32,128]{3,2,1,0:T(8,128)} %ha.5, f32[16,32,128]{2,1,0:T(8,128)S(1)} %copy-done.3, ...), custom_call_target="tpu_custom_call" | custom-call | flops 20000000000 | tf_op jit(solution)/shard_map/faces_x/pallas_call | solution.py:802
  22.6 3.5 %collective-permute-start.3 = (f32[595,128]{1,0:T(8,128)S(1)}, f32[595,128]{1,0:T(8,128)S(1)}, u32[]{:S(2)}, u32[]{:S(2)}) collective-permute-start(f32[595,128]{1,0:T(8,128)S(1)} %get-tuple-element.18), channel_id=1, source_target_pairs={{8,16},{24,32},{40,48},{56,64},{72,80},{88,96},{104,112},{16,8},{3... | collective-permute-start | bytes 913928 | tf_op jit(solution)/shard_map/ppermute | solution.py:713
  26.1 0.1 collective-permute-start.2
  26.2 1.3 %collective-permute-done.2.inner_any = f32[140,128]{1,0:T(8,128)S(1)} collective-permute-done((f32[140,128]{1,0:T(8,128)S(1)}, f32[140,128]{1,0:T(8,128)S(1)}, u32[]{:S(2)}, u32[]{:S(2)}) %collective-permute-start.2) | collective-permute-done | bytes 71712 | tf_op jit(solution)/shard_map/ppermute | solution.py:713
  27.5 6.2 %collective-permute-done.3.outer_any = f32[595,128]{1,0:T(8,128)S(1)} collective-permute-done((f32[595,128]{1,0:T(8,128)S(1)}, f32[595,128]{1,0:T(8,128)S(1)}, u32[]{:S(2)}, u32[]{:S(2)}) %collective-permute-start.3) | collective-permute-done | bytes 304672 | tf_op jit(solution)/shard_map/ppermute | solution.py:713
  33.7 1.5 %all-to-all-done = f32[1408,1,128]{2,1,0:T(1,128)S(1)} async-done(((f32[1408,1,128]{2,1,0:T(1,128)}), f32[1408,1,128]{2,1,0:T(1,128)S(1)}, u32[]{:S(2)}, u32[]{:S(2)}) %all-to-all-start) | async-done | bytes 720928 | tf_op jit(solution)/shard_map/all_to_all | solution.py:717
  35.2 5.0 %step_one.1 = (f32[3,16,32,128]{3,2,1,0:T(8,128)}, f32[512,128]{1,0:T(8,128)S(1)}, f32[128,128]{1,0:T(8,128)S(1)}, f32[17,40,128]{2,1,0:T(8,128)S(1)}, f32[136,128]{1,0:T(8,128)S(1)}) custom-call(f32[3,16,32,128]{3,2,1,0:T(8,128)} %ef.5, f32[3,16,32,128]{3,2,1,0:T(8,128)} %hf.5, f32[3,16,32,128]{3,2,1,0:T(8,128)} %ea.5, f32[3,16,32,128]{3,2,1,0:T(8,128)} %ha.5, ...), custom_call_target="tpu_custom_call" | custom-call | flops 5000000000 | tf_op jit(solution)/shard_map/step_one/pallas_call | solution.py:574
  40.2 1.7 %collective-permute-start.4 = (f32[136,128]{1,0:T(8,128)S(1)}, f32[136,128]{1,0:T(8,128)S(1)}, u32[]{:S(2)}, u32[]{:S(2)}) collective-permute-start(f32[136,128]{1,0:T(8,128)S(1)} %get-tuple-element.24), channel_id=1, source_target_pairs={{0,8},{16,24},{32,40},{48,56},{64,72},{80,88},{96,104},{112,120},{... | collective-permute-start | bytes 208904 | tf_op jit(solution)/shard_map/ppermute | solution.py:713
  42.0 0.9 %collective-permute-done.4.inner = f32[136,128]{1,0:T(8,128)S(1)} collective-permute-done((f32[136,128]{1,0:T(8,128)S(1)}, f32[136,128]{1,0:T(8,128)S(1)}, u32[]{:S(2)}, u32[]{:S(2)}) %collective-permute-start.4) | collective-permute-done | bytes 69664 | tf_op jit(solution)/shard_map/ppermute | solution.py:713
  42.9 0.8 %step_two.1 = (f32[3,16,32,128]{3,2,1,0:T(8,128)}, f32[512,128]{1,0:T(8,128)S(1)}) custom-call(f32[3,16,32,128]{3,2,1,0:T(8,128)} %get-tuple-element.20.final_in, f32[512,128]{1,0:T(8,128)S(1)} %get-tuple-element.21.overlap_in, f32[128,128]{1,0:T(8,128)S(1)} %get-tuple-element.22.sigma_in, ...), custom_call_target="tpu_custom_call", output_to_operand_aliasing={{0}: (0, {})} | custom-call | flops 1000000000 | tf_op jit(solution)/shard_map/step_two/pallas_call | solution.py:664
  43.7 0.0 copy-start.4
  43.7 16.1 %all_to_all.10 = f32[128,4,128]{2,1,0:T(4,128)S(1)} all-to-all(f32[128,4,128]{2,1,0:T(4,128)S(1)} %bitcast.11), channel_id=1, replica_groups=mesh['gx'=16,'gy'=8] {'gx','gy'}, dimensions={0} | all-to-all | bytes 524288 | tf_op jit(solution)/shard_map/all_to_all | solution.py:717
  59.7 0.0 copy-done.4
  59.7 1.4 %unpack_tiles.1 = f32[128,256]{1,0:T(8,128)} custom-call(f32[512,128]{1,0:T(8,128)S(1)} %bitcast.12, f32[128,384]{1,0:T(8,128)S(1)} %copy-done.4), custom_call_target="tpu_custom_call" | custom-call | flops 2000000000 | tf_op jit(solution)/shard_map/unpack_tiles/pallas_call | solution.py:700
Async XLA Ops:
  0.6 19.6 %copy-start.1 = (f32[3,16,32,128]{3,2,1,0:T(8,128)S(1)}, f32[3,16,32,128]{3,2,1,0:T(8,128)}, u32[]{:S(2)}) copy-start(f32[3,16,32,128]{3,2,1,0:T(8,128)} %hf.5) | copy-start | bytes 2359300
  0.6 19.6 %copy-start.2 = (f32[3,16,32,128]{3,2,1,0:T(8,128)S(1)}, f32[3,16,32,128]{3,2,1,0:T(8,128)}, u32[]{:S(2)}) copy-start(f32[3,16,32,128]{3,2,1,0:T(8,128)} %ea.5) | copy-start | bytes 2359300
  4.0 16.2 %copy-start = (f32[3,16,32,128]{3,2,1,0:T(8,128)S(1)}, f32[3,16,32,128]{3,2,1,0:T(8,128)}, u32[]{:S(2)}) copy-start(f32[3,16,32,128]{3,2,1,0:T(8,128)} %ef.5) | copy-start | bytes 2359300
  4.0 16.2 %collective-permute-start = (f32[368,128]{1,0:T(8,128)}, f32[368,128]{1,0:T(8,128)S(1)}, u32[]{:S(2)}, u32[]{:S(2)}) collective-permute-start(f32[368,128]{1,0:T(8,128)} %get-tuple-element.15), channel_id=1, source_target_pairs={{0,1},{2,3},{4,5},{6,7},{1,0},{3,2},{5,4},{7,6},{8,9},{10,11},{12,... | collective-permute-start | bytes 565256 | tf_op jit(solution)/shard_map/ppermute | solution.py:713
  6.6 13.6 %collective-permute-start.1 = (f32[368,128]{1,0:T(8,128)}, f32[368,128]{1,0:T(8,128)}, u32[]{:S(2)}, u32[]{:S(2)}) collective-permute-start(f32[368,128]{1,0:T(8,128)} %get-tuple-element.16), channel_id=1, source_target_pairs={{1,2},{3,4},{5,6},{2,1},{4,3},{6,5},{9,10},{11,12},{13,14},{10,9},... | collective-permute-start | bytes 565256 | tf_op jit(solution)/shard_map/ppermute | solution.py:713
  7.9 12.3 %copy-start.3 = (f32[16,32,128]{2,1,0:T(8,128)S(1)}, f32[16,32,128]{2,1,0:T(8,128)}, u32[]{:S(2)}) copy-start(f32[16,32,128]{2,1,0:T(8,128)} %perm.5) | copy-start | bytes 786436
  7.9 27.3 %all-to-all-start = ((f32[1408,1,128]{2,1,0:T(1,128)}), f32[1408,1,128]{2,1,0:T(1,128)S(1)}, u32[]{:S(2)}, u32[]{:S(2)}) async-start(f32[1408,1,128]{2,1,0:T(1,128)} %bitcast.13), calls=%async_computation | async-start | bytes 1441792 | tf_op jit(solution)/shard_map/all_to_all | solution.py:717
  22.6 11.1 %collective-permute-start.3 = (f32[595,128]{1,0:T(8,128)S(1)}, f32[595,128]{1,0:T(8,128)S(1)}, u32[]{:S(2)}, u32[]{:S(2)}) collective-permute-start(f32[595,128]{1,0:T(8,128)S(1)} %get-tuple-element.18), channel_id=1, source_target_pairs={{8,16},{24,32},{40,48},{56,64},{72,80},{88,96},{104,112},{16,8},{3... | collective-permute-start | bytes 913928 | tf_op jit(solution)/shard_map/ppermute | solution.py:713
  26.1 1.3 %collective-permute-start.2 = (f32[140,128]{1,0:T(8,128)S(1)}, f32[140,128]{1,0:T(8,128)S(1)}, u32[]{:S(2)}, u32[]{:S(2)}) collective-permute-start(f32[140,128]{1,0:T(8,128)S(1)} %get-tuple-element.17), channel_id=1, source_target_pairs={{0,8},{16,24},{32,40},{48,56},{64,72},{80,88},{96,104},{112,120},{... | collective-permute-start | bytes 215048 | tf_op jit(solution)/shard_map/ppermute | solution.py:713
  40.2 2.6 %collective-permute-start.4 = (f32[136,128]{1,0:T(8,128)S(1)}, f32[136,128]{1,0:T(8,128)S(1)}, u32[]{:S(2)}, u32[]{:S(2)}) collective-permute-start(f32[136,128]{1,0:T(8,128)S(1)} %get-tuple-element.24), channel_id=1, source_target_pairs={{0,8},{16,24},{32,40},{48,56},{64,72},{80,88},{96,104},{112,120},{... | collective-permute-start | bytes 208904 | tf_op jit(solution)/shard_map/ppermute | solution.py:713
  43.7 16.1 %copy-start.4 = (f32[128,384]{1,0:T(8,128)S(1)}, f32[128,384]{1,0:T(8,128)}, u32[]{:S(2)}) copy-start(f32[128,384]{1,0:T(8,128)} %get-tuple-element.27.match) | copy-start | bytes 589828

commit v5 on v4

--- a/solution.py
+++ b/solution.py
@@ -26,7 +26,8 @@
 DOWN_X = 11
 BESIDE = (EY - 1, NY, EY - 2)
 TALL = NY + len(BESIDE)
-ROWS = 11
+ROWS = 10
+META = 64
 
 
 def iota(shape, dim):
@@ -126,7 +127,6 @@
     )
     origin = jnp.broadcast_to(starts.astype(F32), square)
     everything = jnp.concatenate([front, back, edges, origin], axis=1)
-    meta = jnp.zeros(square, F32)
     choose = [jnp.where((owner_row == down_f) & (rank_row == k), 1.0, 0.0) for k in range(2)]
     every_slot = select_rows(jnp.concatenate(choose, axis=0), everything)
     for k in range(2):
@@ -144,15 +144,12 @@
                 message[pl.ds(place + 2 * k + half, tiles, stride=ROWS), :] = rows[
                     :, half * LANES : (half + 1) * LANES
                 ]
-        message[pl.ds(4 + k, tiles, stride=ROWS), :] = jnp.where(
-            across < 32,
-            other(edge, 1),
-            jnp.where(across < 64, other(edge, -7), jnp.where(across < 96, other(edge, 7), other(edge, -1))),
-        )
+        corner = jnp.where(down & 8 == 0, other(edge, -7), pltpu.roll(other(edge, 7), 96, 1))
+        row = jnp.where(across < 32, other(edge, 1), jnp.where(across < 64, corner, other(edge, -1)))
         outer_origins = jnp.where(down & 8 == 0, other(origins, -8), other(origins, 8))
         for place, moved in enumerate((origins, other(origins, 1), other(origins, -1), outer_origins)):
-            meta = jnp.where(across == 2 * place + k, moved, meta)
-    message[pl.ds(10, tiles, stride=ROWS), :] = meta
+            row = jnp.where(across == META + place, moved, row)
+        message[pl.ds(4 + k, tiles, stride=ROWS), :] = row
 
 
 def prepare_all(
@@ -280,12 +277,12 @@
     )
 
 
-def start_row(meta_rows, index):
-    return meta_rows[index : index + 1, :].astype(jnp.int32)
-
-
-def start_col(meta, index):
-    return meta[:, index : index + 1].astype(jnp.int32)
+def start_row(meta_rows, k, index):
+    return meta_rows[k][META + index : META + index + 1, :].astype(jnp.int32)
+
+
+def start_col(meta, k, index):
+    return meta[k][:, META + index : META + index + 1].astype(jnp.int32)
 
 
 def step_one(
@@ -311,15 +308,15 @@
     def rows_of(place):
         return message[pl.ds(place, tiles, stride=ROWS), :]
 
-    meta = rows_of(10)
-    meta_rows = meta.T
+    meta = [rows_of(4), rows_of(5)]
+    meta_rows = [rows.T for rows in meta]
     even = lax.axis_index("gx") % 2 == 0
 
     def place_cells(place, index, row):
         targets, values = [], []
         for k in range(2):
-            first = start_row(meta_rows, index + k) >> 7
-            shift = start_col(meta, index + k) & (LANES - 1)
+            first = start_row(meta_rows, k, index) >> 7
+            shift = start_col(meta, k, index) & (LANES - 1)
             front, back = rows_of(place + 2 * k), rows_of(place + 2 * k + 1)
             head, tail = jnp.where(across >= shift, front, 0.0), jnp.where(across >= shift, 0.0, front)
             for step, part in enumerate((head, back, tail)):
@@ -328,15 +325,15 @@
         return select_rows(jnp.concatenate(targets, axis=1), jnp.concatenate(values, axis=0))
 
     density = place_cells(0, 0, iota((block, tiles), 0))
-    beyond = place_cells(6, 6, iota((16, tiles), 0) + jnp.where(even, block - 8, 0))[:8]
+    beyond = place_cells(6, 3, iota((16, tiles), 0) + jnp.where(even, block - 8, 0))[:8]
     sigma = jax.nn.sigmoid(density)
     sigma_out[...] = sigma
     own = CONTRAST * sigma
     targets = []
     row = iota((3 * NX, tiles), 0)
     for k in range(2):
-        first = start_row(meta_rows, 2 + k) >> 7
-        last = start_row(meta_rows, 4 + k) >> 7
+        first = start_row(meta_rows, k, 1) >> 7
+        last = start_row(meta_rows, k, 2) >> 7
         targets.append(
             jnp.where(
                 (((first + 7) >> 3 == row) & (row < NX))
@@ -347,7 +344,7 @@
             )
         )
     sides = CONTRAST * jax.nn.sigmoid(
-        select_rows(jnp.concatenate(targets, axis=1), jnp.concatenate([rows_of(4), rows_of(5)], axis=0))
+        select_rows(jnp.concatenate(targets, axis=1), jnp.concatenate(meta, axis=0))
     )
 
     def lanes_to(values, source):
@@ -366,7 +363,7 @@
         grow[pl.ds(NX * EY + quarter, 8, stride=4), :] = lanes_to(beyond, quarter * LAYERS)
     corner = sides[2 * NX : 2 * NX + 8]
     grow[pl.ds(NX * EY + NY, 1), :] = lanes_to(corner, 32)[:1]
-    grow[pl.ds(NX * EY + EY - 1, 1), :] = lanes_to(corner, 64)[:1]
+    grow[pl.ds(NX * EY + EY - 1, 1), :] = lanes_to(corner, 32)[:1]
 
     low_x = lax.axis_index("gx") > 0
     gy = lax.axis_index("gy")
@@ -511,28 +508,32 @@
             for c in range(3):
                 turned[e + c, x] = h_out[e + c, x] - cut * curl[c]
     leaving = []
-    for x in range(NX):
-        old, new = [], []
-        for evolution in range(2):
-            e = 3 * evolution
+    for evolution in range(2):
+        e, at = 3 * evolution, 2 * evolution * NY
+        for x in range(NX):
             if x > 0:
                 behind = [turned[e + c, x - 1][:NY] for c in (1, 2)]
             else:
-                at = 2 * evolution * NY
                 factor = edge_cut[:NY]
                 behind = [
                     outer_local[pl.ds(at, NY), :] + factor * e_out[e + 2, 0][:NY],
                     outer_local[pl.ds(at + NY, NY), :] - factor * e_out[e + 1, 0][:NY],
                 ]
-            old.append([e_out[e + c, x][:NY] for c in range(3)])
-            new.append(last_e(old[-1], rate[x], [turned[e + c, x] for c in range(3)], behind))
-        for c in range(3):
-            final_v[c, x] = new[0][c]
-        overlap[pl.ds(x * NY, NY), :] = product(old, new)
-        if x % 4 == 3:
-            part = pl.ds(x - 3, 4)
-            leaving.append(pltpu.make_async_copy(final_v.at[:, part], final.at[:, part], sems.at[10 + x // 4]))
-            leaving[-1].start()
+            old = [e_out[e + c, x][:NY] for c in range(3)]
+            new = last_e(old, rate[x], [turned[e + c, x] for c in range(3)], behind)
+            if evolution:
+                forward_old = [e_out[c, x][:NY] for c in range(3)]
+                forward_new = [final_v[c, x] for c in range(3)]
+                overlap[pl.ds(x * NY, NY), :] = product([forward_old, old], [forward_new, new])
+            else:
+                for c in range(3):
+                    final_v[c, x] = new[c]
+                if x % 4 == 3:
+                    part = pl.ds(x - 3, 4)
+                    leaving.append(
+                        pltpu.make_async_copy(final_v.at[:, part], final.at[:, part], sems.at[10 + x // 4])
+                    )
+                    leaving[-1].start()
 
     def keep(x):
         for c in range(6):
@@ -634,7 +635,7 @@
     overlap[pl.ds(pl.multiple_of(x * NY, NY), NY), :] = product(old, new)
     tiles = message.shape[0] // ROWS
     across = iota((tiles, LANES), 1)
-    meta = message[pl.ds(10, tiles, stride=ROWS), :]
+    meta = [message[pl.ds(4 + k, tiles, stride=ROWS), :] for k in range(2)]
     block = NX * 8
     compact = jnp.zeros((block, LANES), F32)
     lane = iota((block, LANES), 1)
@@ -647,7 +648,7 @@
     gradient = CONTRAST * sigma * (1.0 - sigma) * compact
     picks, shifts = [], []
     for k in range(2):
-        starts = start_col(meta, k)
+        starts = start_col(meta, k, 0)
         shifts.append(starts & (LANES - 1))
         for step in range(3):
             picks.append(jnp.where(iota((tiles, block), 1) == (starts >> 7) + step, 1.0, 0.0))

time: 61.4 us -> 60.9 us (level)
  waiting for transfers between devices: 9.87 us -> 9.22 us
where the time goes in v5:
time: 60.9 us; the launch traced here: 60.6 us
  starting transfers between devices  21.5 us (35%)
  blocking collectives  16.6 us (27%)
  Pallas kernels  12.6 us (21%)
  waiting for transfers between devices  9.22 us (15%)
  between operations  0.77 us (1%)
    all_to_all x1, blocking collectives, exchange(): lax.all_to_all(block.reshape(-1, depth, LANES), ('gx', 'gy'), split_axis=...  16.6 us
    all_to_all x1, starting transfers between devices, exchange(): lax.all_to_all(block.reshape(-1, depth, LANES), ('gx', 'gy'), split_axis=...  12.3 us
    ppermute x5, starting transfers between devices, swapped(): return lax.ppermute(block, axis, pairs + [(j, i) for i, j in pairs])  9.22 us
    ppermute x5, waiting for transfers between devices, swapped(): return lax.ppermute(block, axis, pairs + [(j, i) for i, j in pairs])  7.93 us
    pallas_call x1, Pallas kernels, first_step(): pl.pallas_call(step_one, out_shape=(shape(3, NX, NY, LANES), shape(NX * N...  4.66 us
    pallas_call x1, Pallas kernels, prepare(): pl.pallas_call(prepare_all, out_shape=(shape(UP_ROWS * NX, LANES), shape(...  3.41 us
    pallas_call x1, Pallas kernels, send_x(): pl.pallas_call(faces_x, out_shape=(shape(PLANES * TALL, LANES), shape(UP_...  2.3 us
    pallas_call x1, Pallas kernels, unpack(): pl.pallas_call(unpack_tiles, out_shape=shape(tiles, 2 * LANES), in_specs=...  1.37 us
  transfers between devices with their start and end apart: 6, of which 4 were waited for; matrix products, arithmetic and copies ran while one was open for 0% of the time, Pallas kernels for 4%

profile of v5, /device:TPU:1, one launch (start us, length us, event | category | flops | bytes accessed | tf_op | source)
XLA Modules:
  0.0 60.6 jit_solution(5618933253034537886)
XLA Ops:
  0.6 0.0 copy-start.1
  0.6 0.0 copy-start.2
  0.7 3.4 %prepare.1 = (f32[368,128]{1,0:T(8,128)}, f32[368,128]{1,0:T(8,128)}, f32[1280,128]{1,0:T(8,128)}, f32[128,384]{1,0:T(8,128)}) custom-call(f32[3,16,32,128]{3,2,1,0:T(8,128)} %ef.5, f32[3,16,32,128]{3,2,1,0:T(8,128)} %hf.5, f32[3,16,32,128]{3,2,1,0:T(8,128)} %ea.5, f32[3,16,32,128]{3,2,1,0:T(8,128)} %ha.5, f32[16,32,128]{2,1,0:T(8,128)} %perm.5, ...), custom_call_target="tpu_custom_call" | custom-call | flops 3000000000 | tf_op jit(solution)/shard_map/prepare/pallas_call | solution.py:198
  4.1 0.0 copy-start
  4.1 2.5 %collective-permute-start = (f32[368,128]{1,0:T(8,128)}, f32[368,128]{1,0:T(8,128)S(1)}, u32[]{:S(2)}, u32[]{:S(2)}) collective-permute-start(f32[368,128]{1,0:T(8,128)} %get-tuple-element.15), channel_id=1, source_target_pairs={{0,1},{2,3},{4,5},{6,7},{1,0},{3,2},{5,4},{7,6},{8,9},{10,11},{12,... | collective-permute-start | bytes 565256 | tf_op jit(solution)/shard_map/ppermute | solution.py:714
  6.6 1.3 %collective-permute-start.1 = (f32[368,128]{1,0:T(8,128)}, f32[368,128]{1,0:T(8,128)}, u32[]{:S(2)}, u32[]{:S(2)}) collective-permute-start(f32[368,128]{1,0:T(8,128)} %get-tuple-element.16), channel_id=1, source_target_pairs={{1,2},{3,4},{5,6},{2,1},{4,3},{6,5},{9,10},{11,12},{13,14},{10,9},... | collective-permute-start | bytes 565256 | tf_op jit(solution)/shard_map/ppermute | solution.py:714
  8.0 0.0 copy-start.3
  8.0 12.3 %all-to-all-start = ((f32[1280,1,128]{2,1,0:T(1,128)}), f32[1280,1,128]{2,1,0:T(1,128)S(1)}, u32[]{:S(2)}, u32[]{:S(2)}) async-start(f32[1280,1,128]{2,1,0:T(1,128)} %bitcast.13), calls=%async_computation | async-start | bytes 1310720 | tf_op jit(solution)/shard_map/all_to_all | solution.py:718
  20.3 0.0 collective-permute-done.inner_y.inner_y_any
  20.3 0.0 collective-permute-done.1.outer_y.outer_y_any
  20.3 0.0 copy-done.1
  20.3 0.0 copy-done.2
  20.3 0.0 copy-done
  20.3 0.0 copy-done.3
  20.3 2.3 %faces_x.1 = (f32[140,128]{1,0:T(8,128)S(1)}, f32[595,128]{1,0:T(8,128)S(1)}) custom-call(f32[3,16,32,128]{3,2,1,0:T(8,128)S(1)} %copy-done, f32[3,16,32,128]{3,2,1,0:T(8,128)S(1)} %copy-done.1, f32[3,16,32,128]{3,2,1,0:T(8,128)S(1)} %copy-done.2, f32[3,16,32,128]{3,2,1,0:T(8,128)} %ha.5, f32[16,32,128]{2,1,0:T(8,128)S(1)} %copy-done.3, ...), custom_call_target="tpu_custom_call" | custom-call | flops 20000000000 | tf_op jit(solution)/shard_map/faces_x/pallas_call | solution.py:803
  22.6 3.5 %collective-permute-start.3 = (f32[595,128]{1,0:T(8,128)S(1)}, f32[595,128]{1,0:T(8,128)S(1)}, u32[]{:S(2)}, u32[]{:S(2)}) collective-permute-start(f32[595,128]{1,0:T(8,128)S(1)} %get-tuple-element.18), channel_id=1, source_target_pairs={{8,16},{24,32},{40,48},{56,64},{72,80},{88,96},{104,112},{16,8},{3... | collective-permute-start | bytes 913928 | tf_op jit(solution)/shard_map/ppermute | solution.py:714
  26.2 0.1 collective-permute-start.2
  26.3 1.3 %collective-permute-done.2.inner_any = f32[140,128]{1,0:T(8,128)S(1)} collective-permute-done((f32[140,128]{1,0:T(8,128)S(1)}, f32[140,128]{1,0:T(8,128)S(1)}, u32[]{:S(2)}, u32[]{:S(2)}) %collective-permute-start.2) | collective-permute-done | bytes 71712 | tf_op jit(solution)/shard_map/ppermute | solution.py:714
  27.5 5.8 %collective-permute-done.3.outer_any = f32[595,128]{1,0:T(8,128)S(1)} collective-permute-done((f32[595,128]{1,0:T(8,128)S(1)}, f32[595,128]{1,0:T(8,128)S(1)}, u32[]{:S(2)}, u32[]{:S(2)}) %collective-permute-start.3) | collective-permute-done | bytes 304672 | tf_op jit(solution)/shard_map/ppermute | solution.py:714
  33.3 1.3 %all-to-all-done = f32[1280,1,128]{2,1,0:T(1,128)S(1)} async-done(((f32[1280,1,128]{2,1,0:T(1,128)}), f32[1280,1,128]{2,1,0:T(1,128)S(1)}, u32[]{:S(2)}, u32[]{:S(2)}) %all-to-all-start) | async-done | bytes 655392 | tf_op jit(solution)/shard_map/all_to_all | solution.py:718
  34.6 4.7 %step_one.1 = (f32[3,16,32,128]{3,2,1,0:T(8,128)}, f32[512,128]{1,0:T(8,128)S(1)}, f32[128,128]{1,0:T(8,128)S(1)}, f32[17,40,128]{2,1,0:T(8,128)S(1)}, f32[136,128]{1,0:T(8,128)S(1)}) custom-call(f32[3,16,32,128]{3,2,1,0:T(8,128)} %ef.5, f32[3,16,32,128]{3,2,1,0:T(8,128)} %hf.5, f32[3,16,32,128]{3,2,1,0:T(8,128)} %ea.5, f32[3,16,32,128]{3,2,1,0:T(8,128)} %ha.5, ...), custom_call_target="tpu_custom_call" | custom-call | flops 5000000000 | tf_op jit(solution)/shard_map/step_one/pallas_call | solution.py:575
  39.2 1.7 %collective-permute-start.4 = (f32[136,128]{1,0:T(8,128)S(1)}, f32[136,128]{1,0:T(8,128)S(1)}, u32[]{:S(2)}, u32[]{:S(2)}) collective-permute-start(f32[136,128]{1,0:T(8,128)S(1)} %get-tuple-element.24), channel_id=1, source_target_pairs={{0,8},{16,24},{32,40},{48,56},{64,72},{80,88},{96,104},{112,120},{... | collective-permute-start | bytes 208904 | tf_op jit(solution)/shard_map/ppermute | solution.py:714
  41.0 0.9 %collective-permute-done.4.inner = f32[136,128]{1,0:T(8,128)S(1)} collective-permute-done((f32[136,128]{1,0:T(8,128)S(1)}, f32[136,128]{1,0:T(8,128)S(1)}, u32[]{:S(2)}, u32[]{:S(2)}) %collective-permute-start.4) | collective-permute-done | bytes 69664 | tf_op jit(solution)/shard_map/ppermute | solution.py:714
  41.9 0.8 %step_two.1 = (f32[3,16,32,128]{3,2,1,0:T(8,128)}, f32[512,128]{1,0:T(8,128)S(1)}) custom-call(f32[3,16,32,128]{3,2,1,0:T(8,128)} %get-tuple-element.20.final_in, f32[512,128]{1,0:T(8,128)S(1)} %get-tuple-element.21.overlap_in, f32[128,128]{1,0:T(8,128)S(1)} %get-tuple-element.22.sigma_in, ...), custom_call_target="tpu_custom_call", output_to_operand_aliasing={{0}: (0, {})} | custom-call | flops 1000000000 | tf_op jit(solution)/shard_map/step_two/pallas_call | solution.py:665
  42.7 0.0 copy-start.4
  42.7 16.6 %all_to_all.10 = f32[128,4,128]{2,1,0:T(4,128)S(1)} all-to-all(f32[128,4,128]{2,1,0:T(4,128)S(1)} %bitcast.11), channel_id=1, replica_groups=mesh['gx'=16,'gy'=8] {'gx','gy'}, dimensions={0} | all-to-all | bytes 524288 | tf_op jit(solution)/shard_map/all_to_all | solution.py:718
  59.3 0.0 copy-done.4
  59.3 1.4 %unpack_tiles.1 = f32[128,256]{1,0:T(8,128)} custom-call(f32[512,128]{1,0:T(8,128)S(1)} %bitcast.12, f32[128,384]{1,0:T(8,128)S(1)} %copy-done.4), custom_call_target="tpu_custom_call" | custom-call | flops 2000000000 | tf_op jit(solution)/shard_map/unpack_tiles/pallas_call | solution.py:701
Async XLA Ops:
  0.6 19.6 %copy-start.1 = (f32[3,16,32,128]{3,2,1,0:T(8,128)S(1)}, f32[3,16,32,128]{3,2,1,0:T(8,128)}, u32[]{:S(2)}) copy-start(f32[3,16,32,128]{3,2,1,0:T(8,128)} %hf.5) | copy-start | bytes 2359300
  0.6 19.6 %copy-start.2 = (f32[3,16,32,128]{3,2,1,0:T(8,128)S(1)}, f32[3,16,32,128]{3,2,1,0:T(8,128)}, u32[]{:S(2)}) copy-start(f32[3,16,32,128]{3,2,1,0:T(8,128)} %ea.5) | copy-start | bytes 2359300
  4.1 16.2 %copy-start = (f32[3,16,32,128]{3,2,1,0:T(8,128)S(1)}, f32[3,16,32,128]{3,2,1,0:T(8,128)}, u32[]{:S(2)}) copy-start(f32[3,16,32,128]{3,2,1,0:T(8,128)} %ef.5) | copy-start | bytes 2359300
  4.1 16.2 %collective-permute-start = (f32[368,128]{1,0:T(8,128)}, f32[368,128]{1,0:T(8,128)S(1)}, u32[]{:S(2)}, u32[]{:S(2)}) collective-permute-start(f32[368,128]{1,0:T(8,128)} %get-tuple-element.15), channel_id=1, source_target_pairs={{0,1},{2,3},{4,5},{6,7},{1,0},{3,2},{5,4},{7,6},{8,9},{10,11},{12,... | collective-permute-start | bytes 565256 | tf_op jit(solution)/shard_map/ppermute | solution.py:714
  6.6 13.6 %collective-permute-start.1 = (f32[368,128]{1,0:T(8,128)}, f32[368,128]{1,0:T(8,128)}, u32[]{:S(2)}, u32[]{:S(2)}) collective-permute-start(f32[368,128]{1,0:T(8,128)} %get-tuple-element.16), channel_id=1, source_target_pairs={{1,2},{3,4},{5,6},{2,1},{4,3},{6,5},{9,10},{11,12},{13,14},{10,9},... | collective-permute-start | bytes 565256 | tf_op jit(solution)/shard_map/ppermute | solution.py:714
  8.0 12.3 %copy-start.3 = (f32[16,32,128]{2,1,0:T(8,128)S(1)}, f32[16,32,128]{2,1,0:T(8,128)}, u32[]{:S(2)}) copy-start(f32[16,32,128]{2,1,0:T(8,128)} %perm.5) | copy-start | bytes 786436
  8.0 26.6 %all-to-all-start = ((f32[1280,1,128]{2,1,0:T(1,128)}), f32[1280,1,128]{2,1,0:T(1,128)S(1)}, u32[]{:S(2)}, u32[]{:S(2)}) async-start(f32[1280,1,128]{2,1,0:T(1,128)} %bitcast.13), calls=%async_computation | async-start | bytes 1310720 | tf_op jit(solution)/shard_map/all_to_all | solution.py:718
  22.6 10.7 %collective-permute-start.3 = (f32[595,128]{1,0:T(8,128)S(1)}, f32[595,128]{1,0:T(8,128)S(1)}, u32[]{:S(2)}, u32[]{:S(2)}) collective-permute-start(f32[595,128]{1,0:T(8,128)S(1)} %get-tuple-element.18), channel_id=1, source_target_pairs={{8,16},{24,32},{40,48},{56,64},{72,80},{88,96},{104,112},{16,8},{3... | collective-permute-start | bytes 913928 | tf_op jit(solution)/shard_map/ppermute | solution.py:714
  26.2 1.3 %collective-permute-start.2 = (f32[140,128]{1,0:T(8,128)S(1)}, f32[140,128]{1,0:T(8,128)S(1)}, u32[]{:S(2)}, u32[]{:S(2)}) collective-permute-start(f32[140,128]{1,0:T(8,128)S(1)} %get-tuple-element.17), channel_id=1, source_target_pairs={{0,8},{16,24},{32,40},{48,56},{64,72},{80,88},{96,104},{112,120},{... | collective-permute-start | bytes 215048 | tf_op jit(solution)/shard_map/ppermute | solution.py:714
  39.2 2.6 %collective-permute-start.4 = (f32[136,128]{1,0:T(8,128)S(1)}, f32[136,128]{1,0:T(8,128)S(1)}, u32[]{:S(2)}, u32[]{:S(2)}) collective-permute-start(f32[136,128]{1,0:T(8,128)S(1)} %get-tuple-element.24), channel_id=1, source_target_pairs={{0,8},{16,24},{32,40},{48,56},{64,72},{80,88},{96,104},{112,120},{... | collective-permute-start | bytes 208904 | tf_op jit(solution)/shard_map/ppermute | solution.py:714
  42.7 16.6 %copy-start.4 = (f32[128,384]{1,0:T(8,128)S(1)}, f32[128,384]{1,0:T(8,128)}, u32[]{:S(2)}) copy-start(f32[128,384]{1,0:T(8,128)} %get-tuple-element.27.match) | copy-start | bytes 589828

commit v6 on v5

--- a/solution.py
+++ b/solution.py
@@ -812,7 +812,7 @@
             pltpu.VMEM((12, 4, 8, LANES), F32),
             pltpu.SemaphoreType.DMA((10,)),
         ],
-        compiler_params=params(50),
+        compiler_params=params(52),
         cost_estimate=cost(20),
         name="faces_x",
     )(ef, hf, ea, ha, perm, inner_y, outer_y)

time: 60.9 us -> 60.4 us (level)
  waiting for transfers between devices: 9.22 us -> 10.1 us
  Pallas kernels: 12.6 us -> 11.8 us
    pallas_call x1, Pallas kernels: 2.3 us -> 1.42 us  [send_x(): pl.pallas_call(faces_x, out_shape=(shape(PLANES * TALL, LANES), shape(UP_...]
    ppermute x5, starting transfers between devices: 9.22 us -> 8.55 us  [swapped(): return lax.ppermute(block, axis, pairs + [(j, i) for i, j in pairs])]
    all_to_all x1, starting transfers between devices: 12.3 us -> 12.9 us  [exchange(): lax.all_to_all(block.reshape(-1, depth, LANES), ('gx', 'gy'), split_axis=...]
  transfers between devices with their start and end apart: 6 -> 6, of which waited for: 4 -> 4; matrix products, arithmetic and copies ran while one was open for 0% -> 0% of each run, Pallas kernels for 4% -> 2%
where the time goes in v6:
time: 60.4 us; the launch traced here: 60.2 us
  starting transfers between devices  21.5 us (36%)
  blocking collectives  16 us (26%)
  Pallas kernels  11.8 us (20%)
  waiting for transfers between devices  10.1 us (17%)
  between operations  0.75 us (1%)
    all_to_all x1, blocking collectives, exchange(): lax.all_to_all(block.reshape(-1, depth, LANES), ('gx', 'gy'), split_axis=...  16 us
    all_to_all x1, starting transfers between devices, exchange(): lax.all_to_all(block.reshape(-1, depth, LANES), ('gx', 'gy'), split_axis=...  12.9 us
    ppermute x5, starting transfers between devices, swapped(): return lax.ppermute(block, axis, pairs + [(j, i) for i, j in pairs])  8.55 us
    ppermute x5, waiting for transfers between devices, swapped(): return lax.ppermute(block, axis, pairs + [(j, i) for i, j in pairs])  8.29 us
    pallas_call x1, Pallas kernels, first_step(): pl.pallas_call(step_one, out_shape=(shape(3, NX, NY, LANES), shape(NX * N...  4.88 us
    pallas_call x1, Pallas kernels, prepare(): pl.pallas_call(prepare_all, out_shape=(shape(UP_ROWS * NX, LANES), shape(...  3.29 us
    all_to_all x1, waiting for transfers between devices, exchange(): lax.all_to_all(block.reshape(-1, depth, LANES), ('gx', 'gy'), split_axis=...  1.83 us
    pallas_call x1, Pallas kernels, send_x(): pl.pallas_call(faces_x, out_shape=(shape(PLANES * TALL, LANES), shape(UP_...  1.42 us
  transfers between devices with their start and end apart: 6, of which 4 were waited for; matrix products, arithmetic and copies ran while one was open for 0% of the time, Pallas kernels for 2%

profile of v6, /device:TPU:1, one launch (start us, length us, event | category | flops | bytes accessed | tf_op | source)
XLA Modules:
  0.0 60.2 jit_solution(10707299029422373790)
XLA Ops:
  0.6 3.3 %prepare.1 = (f32[368,128]{1,0:T(8,128)}, f32[368,128]{1,0:T(8,128)}, f32[1280,128]{1,0:T(8,128)}, f32[128,384]{1,0:T(8,128)}) custom-call(f32[3,16,32,128]{3,2,1,0:T(8,128)} %ef.5, f32[3,16,32,128]{3,2,1,0:T(8,128)} %hf.5, f32[3,16,32,128]{3,2,1,0:T(8,128)} %ea.5, f32[3,16,32,128]{3,2,1,0:T(8,128)} %ha.5, f32[16,32,128]{2,1,0:T(8,128)} %perm.5, ...), custom_call_target="tpu_custom_call" | custom-call | flops 3000000000 | tf_op jit(solution)/shard_map/prepare/pallas_call | solution.py:198
  3.9 0.0 copy-start
  3.9 2.5 %collective-permute-start = (f32[368,128]{1,0:T(8,128)}, f32[368,128]{1,0:T(8,128)S(1)}, u32[]{:S(2)}, u32[]{:S(2)}) collective-permute-start(f32[368,128]{1,0:T(8,128)} %get-tuple-element.15), channel_id=1, source_target_pairs={{0,1},{2,3},{4,5},{6,7},{1,0},{3,2},{5,4},{7,6},{8,9},{10,11},{12,... | collective-permute-start | bytes 565256 | tf_op jit(solution)/shard_map/ppermute | solution.py:714
  6.5 0.7 %collective-permute-start.1 = (f32[368,128]{1,0:T(8,128)}, f32[368,128]{1,0:T(8,128)S(1)}, u32[]{:S(2)}, u32[]{:S(2)}) collective-permute-start(f32[368,128]{1,0:T(8,128)} %get-tuple-element.16), channel_id=1, source_target_pairs={{1,2},{3,4},{5,6},{2,1},{4,3},{6,5},{9,10},{11,12},{13,14},{10,9},... | collective-permute-start | bytes 565256 | tf_op jit(solution)/shard_map/ppermute | solution.py:714
  7.2 0.0 copy-start.1
  7.2 12.9 %all-to-all-start = ((f32[1280,1,128]{2,1,0:T(1,128)}), f32[1280,1,128]{2,1,0:T(1,128)S(1)}, u32[]{:S(2)}, u32[]{:S(2)}) async-start(f32[1280,1,128]{2,1,0:T(1,128)} %bitcast.13), calls=%async_computation | async-start | bytes 1310720 | tf_op jit(solution)/shard_map/all_to_all | solution.py:718
  20.1 0.0 collective-permute-done.inner_y.inner_y_any
  20.1 0.0 collective-permute-done.1.outer_y.outer_y_any
  20.1 0.0 copy-done
  20.1 0.0 copy-done.1
  20.1 1.4 %faces_x.1 = (f32[140,128]{1,0:T(8,128)S(1)}, f32[595,128]{1,0:T(8,128)S(1)}) custom-call(f32[3,16,32,128]{3,2,1,0:T(8,128)S(1)} %copy-done, f32[3,16,32,128]{3,2,1,0:T(8,128)} %hf.5, f32[3,16,32,128]{3,2,1,0:T(8,128)} %ea.5, f32[3,16,32,128]{3,2,1,0:T(8,128)} %ha.5, f32[16,32,128]{2,1,0:T(8,128)S(1)} %copy-done.1, ...), custom_call_target="tpu_custom_call" | custom-call | flops 20000000000 | tf_op jit(solution)/shard_map/faces_x/pallas_call | solution.py:803
  21.6 3.5 %collective-permute-start.3 = (f32[595,128]{1,0:T(8,128)S(1)}, f32[595,128]{1,0:T(8,128)S(1)}, u32[]{:S(2)}, u32[]{:S(2)}) collective-permute-start(f32[595,128]{1,0:T(8,128)S(1)} %get-tuple-element.18), channel_id=1, source_target_pairs={{8,16},{24,32},{40,48},{56,64},{72,80},{88,96},{104,112},{16,8},{3... | collective-permute-start | bytes 913928 | tf_op jit(solution)/shard_map/ppermute | solution.py:714
  25.1 0.1 collective-permute-start.2
  25.2 1.3 %collective-permute-done.2.inner_any = f32[140,128]{1,0:T(8,128)S(1)} collective-permute-done((f32[140,128]{1,0:T(8,128)S(1)}, f32[140,128]{1,0:T(8,128)S(1)}, u32[]{:S(2)}, u32[]{:S(2)}) %collective-permute-start.2) | collective-permute-done | bytes 71712 | tf_op jit(solution)/shard_map/ppermute | solution.py:714
  26.5 6.1 %collective-permute-done.3.outer_any = f32[595,128]{1,0:T(8,128)S(1)} collective-permute-done((f32[595,128]{1,0:T(8,128)S(1)}, f32[595,128]{1,0:T(8,128)S(1)}, u32[]{:S(2)}, u32[]{:S(2)}) %collective-permute-start.3) | collective-permute-done | bytes 304672 | tf_op jit(solution)/shard_map/ppermute | solution.py:714
  32.6 1.8 %all-to-all-done = f32[1280,1,128]{2,1,0:T(1,128)S(1)} async-done(((f32[1280,1,128]{2,1,0:T(1,128)}), f32[1280,1,128]{2,1,0:T(1,128)S(1)}, u32[]{:S(2)}, u32[]{:S(2)}) %all-to-all-start) | async-done | bytes 655392 | tf_op jit(solution)/shard_map/all_to_all | solution.py:718
  34.4 4.9 %step_one.1 = (f32[3,16,32,128]{3,2,1,0:T(8,128)}, f32[512,128]{1,0:T(8,128)S(1)}, f32[128,128]{1,0:T(8,128)S(1)}, f32[17,40,128]{2,1,0:T(8,128)S(1)}, f32[136,128]{1,0:T(8,128)S(1)}) custom-call(f32[3,16,32,128]{3,2,1,0:T(8,128)} %ef.5, f32[3,16,32,128]{3,2,1,0:T(8,128)} %hf.5, f32[3,16,32,128]{3,2,1,0:T(8,128)} %ea.5, f32[3,16,32,128]{3,2,1,0:T(8,128)} %ha.5, ...), custom_call_target="tpu_custom_call" | custom-call | flops 5000000000 | tf_op jit(solution)/shard_map/step_one/pallas_call | solution.py:575
  39.3 1.7 %collective-permute-start.4 = (f32[136,128]{1,0:T(8,128)S(1)}, f32[136,128]{1,0:T(8,128)S(1)}, u32[]{:S(2)}, u32[]{:S(2)}) collective-permute-start(f32[136,128]{1,0:T(8,128)S(1)} %get-tuple-element.24), channel_id=1, source_target_pairs={{0,8},{16,24},{32,40},{48,56},{64,72},{80,88},{96,104},{112,120},{... | collective-permute-start | bytes 208904 | tf_op jit(solution)/shard_map/ppermute | solution.py:714
  41.0 0.9 %collective-permute-done.4.inner = f32[136,128]{1,0:T(8,128)S(1)} collective-permute-done((f32[136,128]{1,0:T(8,128)S(1)}, f32[136,128]{1,0:T(8,128)S(1)}, u32[]{:S(2)}, u32[]{:S(2)}) %collective-permute-start.4) | collective-permute-done | bytes 69664 | tf_op jit(solution)/shard_map/ppermute | solution.py:714
  41.9 0.8 %step_two.1 = (f32[3,16,32,128]{3,2,1,0:T(8,128)}, f32[512,128]{1,0:T(8,128)S(1)}) custom-call(f32[3,16,32,128]{3,2,1,0:T(8,128)} %get-tuple-element.20.final_in, f32[512,128]{1,0:T(8,128)S(1)} %get-tuple-element.21.overlap_in, f32[128,128]{1,0:T(8,128)S(1)} %get-tuple-element.22.sigma_in, ...), custom_call_target="tpu_custom_call", output_to_operand_aliasing={{0}: (0, {})} | custom-call | flops 1000000000 | tf_op jit(solution)/shard_map/step_two/pallas_call | solution.py:665
  42.8 0.0 copy-start.2
  42.8 16.0 %all_to_all.10 = f32[128,4,128]{2,1,0:T(4,128)S(1)} all-to-all(f32[128,4,128]{2,1,0:T(4,128)S(1)} %bitcast.11), channel_id=1, replica_groups=mesh['gx'=16,'gy'=8] {'gx','gy'}, dimensions={0} | all-to-all | bytes 524288 | tf_op jit(solution)/shard_map/all_to_all | solution.py:718
  58.8 0.0 copy-done.2
  58.8 1.4 %unpack_tiles.1 = f32[128,256]{1,0:T(8,128)} custom-call(f32[512,128]{1,0:T(8,128)S(1)} %bitcast.12, f32[128,384]{1,0:T(8,128)S(1)} %copy-done.2), custom_call_target="tpu_custom_call" | custom-call | flops 2000000000 | tf_op jit(solution)/shard_map/unpack_tiles/pallas_call | solution.py:701
Async XLA Ops:
  3.9 16.2 %copy-start = (f32[3,16,32,128]{3,2,1,0:T(8,128)S(1)}, f32[3,16,32,128]{3,2,1,0:T(8,128)}, u32[]{:S(2)}) copy-start(f32[3,16,32,128]{3,2,1,0:T(8,128)} %ef.5) | copy-start | bytes 2359300
  3.9 16.2 %collective-permute-start = (f32[368,128]{1,0:T(8,128)}, f32[368,128]{1,0:T(8,128)S(1)}, u32[]{:S(2)}, u32[]{:S(2)}) collective-permute-start(f32[368,128]{1,0:T(8,128)} %get-tuple-element.15), channel_id=1, source_target_pairs={{0,1},{2,3},{4,5},{6,7},{1,0},{3,2},{5,4},{7,6},{8,9},{10,11},{12,... | collective-permute-start | bytes 565256 | tf_op jit(solution)/shard_map/ppermute | solution.py:714
  6.5 13.6 %collective-permute-start.1 = (f32[368,128]{1,0:T(8,128)}, f32[368,128]{1,0:T(8,128)S(1)}, u32[]{:S(2)}, u32[]{:S(2)}) collective-permute-start(f32[368,128]{1,0:T(8,128)} %get-tuple-element.16), channel_id=1, source_target_pairs={{1,2},{3,4},{5,6},{2,1},{4,3},{6,5},{9,10},{11,12},{13,14},{10,9},... | collective-permute-start | bytes 565256 | tf_op jit(solution)/shard_map/ppermute | solution.py:714
  7.2 13.0 %copy-start.1 = (f32[16,32,128]{2,1,0:T(8,128)S(1)}, f32[16,32,128]{2,1,0:T(8,128)}, u32[]{:S(2)}) copy-start(f32[16,32,128]{2,1,0:T(8,128)} %perm.5) | copy-start | bytes 786436
  7.2 27.3 %all-to-all-start = ((f32[1280,1,128]{2,1,0:T(1,128)}), f32[1280,1,128]{2,1,0:T(1,128)S(1)}, u32[]{:S(2)}, u32[]{:S(2)}) async-start(f32[1280,1,128]{2,1,0:T(1,128)} %bitcast.13), calls=%async_computation | async-start | bytes 1310720 | tf_op jit(solution)/shard_map/all_to_all | solution.py:718
  21.6 11.0 %collective-permute-start.3 = (f32[595,128]{1,0:T(8,128)S(1)}, f32[595,128]{1,0:T(8,128)S(1)}, u32[]{:S(2)}, u32[]{:S(2)}) collective-permute-start(f32[595,128]{1,0:T(8,128)S(1)} %get-tuple-element.18), channel_id=1, source_target_pairs={{8,16},{24,32},{40,48},{56,64},{72,80},{88,96},{104,112},{16,8},{3... | collective-permute-start | bytes 913928 | tf_op jit(solution)/shard_map/ppermute | solution.py:714
  25.1 1.3 %collective-permute-start.2 = (f32[140,128]{1,0:T(8,128)S(1)}, f32[140,128]{1,0:T(8,128)S(1)}, u32[]{:S(2)}, u32[]{:S(2)}) collective-permute-start(f32[140,128]{1,0:T(8,128)S(1)} %get-tuple-element.17), channel_id=1, source_target_pairs={{0,8},{16,24},{32,40},{48,56},{64,72},{80,88},{96,104},{112,120},{... | collective-permute-start | bytes 215048 | tf_op jit(solution)/shard_map/ppermute | solution.py:714
  39.3 2.6 %collective-permute-start.4 = (f32[136,128]{1,0:T(8,128)S(1)}, f32[136,128]{1,0:T(8,128)S(1)}, u32[]{:S(2)}, u32[]{:S(2)}) collective-permute-start(f32[136,128]{1,0:T(8,128)S(1)} %get-tuple-element.24), channel_id=1, source_target_pairs={{0,8},{16,24},{32,40},{48,56},{64,72},{80,88},{96,104},{112,120},{... | collective-permute-start | bytes 208904 | tf_op jit(solution)/shard_map/ppermute | solution.py:714
  42.8 16.0 %copy-start.2 = (f32[128,384]{1,0:T(8,128)S(1)}, f32[128,384]{1,0:T(8,128)}, u32[]{:S(2)}) copy-start(f32[128,384]{1,0:T(8,128)} %get-tuple-element.27.match) | copy-start | bytes 589828
